TPU v7x, 32 devices: a whole 2x2x4 slice. The times are simulated.
32 devices in a mesh: groups: 2 (over y), tensor: 4 (over z), expert: 2 (over x), sub: 2 (over core).
Axes of the slice: x: 2, y: 2, z: 4, core: 2. Of those that a mesh axis runs over, the one named last changes fastest.
Arguments:
- tokens: bfloat16 [1024, 3072], P(('groups', 'expert', 'sub'), 'tensor'), parts along dimension 0, may hold values from -6 to 6
- cotangent: bfloat16 [1024, 3072], P(('groups', 'expert', 'sub'), 'tensor'), parts along dimension 0, may hold values from -6 to 6
- expert_ids: int32 [1024, 2], P(('groups', 'expert', 'sub')), parts along dimension 0, may hold values from 0 to 3, all different within a row; in each aligned block of 128 rows (0 to 127, 128 to 255, ...) at most 80 rows name the same one
- gate_values: float32 [1024, 2], P(('groups', 'expert', 'sub')), parts along dimension 0, may hold values from 0.2 to 1
- w_gate: bfloat16 [4, 3072, 16384], P('expert', 'sub', 'tensor'), may hold values from -0.15625 to 0.15625
- w_up: bfloat16 [4, 3072, 16384], P('expert', 'sub', 'tensor'), may hold values from -0.15625 to 0.15625
- w_down: bfloat16 [4, 16384, 3072], P('expert', 'tensor', 'sub'), may hold values from -0.0625 to 0.0625
Outputs:
- mixed: bfloat16 [1024, 3072], P(('groups', 'expert', 'sub'), 'tensor'), parts along dimension 0
- token_grad: bfloat16 [1024, 3072], P(('groups', 'expert', 'sub'), 'tensor'), parts along dimension 0
There are 2 independent parts, one for each index of `groups`. A program takes and returns all parts, laid end to end along the dimension named above; an argument that names none is the same for every part. Nothing has to cross between parts.
Inputs may be any that keep to these rules, and one draw needn't show every extreme that they name: `expert_ids`: each row names 2 different experts. Within each aligned block of 128 rows no expert is named by more than 80 rows, and in some block one expert is named by exactly 80 rows.
All inputs are finite; a program needn't handle non-finite values.
Results may differ from a plain program's by a relative error of at most 0.012.
Values may be sent and summed in bfloat16 or wider, within the bound.
No kernel may reach another device: no remote copies, remote signals or barrier semaphores. Data moves between devices by JAX's collectives and lax.ppermute only.
A program may use at most 448 MiB of HBM per device.

v0:
```python
import jax
import jax.numpy as jnp
from jax import lax
from jax.sharding import PartitionSpec as P

EXPERTS = 4
CAP = 80


def slot_targets(expert_ids, capacity, experts):
    flat_ids = expert_ids.reshape(-1)
    onehot = (flat_ids[:, None] == jnp.arange(experts, dtype=jnp.int32)[None, :]).astype(jnp.int32)
    earlier = jnp.cumsum(onehot, axis=0) - onehot
    return flat_ids * capacity + jnp.sum(earlier * onehot, axis=1)


def per_device(tokens, cotangent, expert_ids, gate_values, w_gate, w_up, w_down):
    local_count = w_gate.shape[0]
    sources = lax.axis_size("expert")
    choose_count = expert_ids.shape[1]
    full_gate, full_up, full_down = (
        lax.all_gather(w_gate, "sub", axis=1, tiled=True),
        lax.all_gather(w_up, "sub", axis=1, tiled=True),
        lax.all_gather(w_down, "sub", axis=2, tiled=True),
    )
    targets = slot_targets(expert_ids, CAP, EXPERTS)
    placing = (jnp.arange(EXPERTS * CAP, dtype=jnp.int32)[:, None] == targets[None, :]).astype(
        jnp.bfloat16
    )

    def dispatch(row_block):
        doubled = jnp.repeat(row_block, choose_count, axis=0)
        return jnp.dot(placing, doubled, preferred_element_type=jnp.float32).astype(jnp.bfloat16)

    def grouped(flat_rows):
        return flat_rows.reshape(sources, local_count, CAP, flat_rows.shape[1])

    whole_tokens, whole_grads = (
        lax.all_gather(tokens, "tensor", axis=1, tiled=True),
        lax.all_gather(cotangent, "tensor", axis=1, tiled=True),
    )
    arrived = (
        lax.all_to_all(dispatch(whole_tokens), "expert", split_axis=0, concat_axis=0, tiled=True),
        lax.all_to_all(dispatch(whole_grads), "expert", split_axis=0, concat_axis=0, tiled=True),
    )
    inputs = grouped(arrived[0])
    grad_rows = grouped(arrived[1])
    gate_pre = jnp.einsum("secd,edf->secf", inputs, full_gate, preferred_element_type=jnp.float32)
    up_pre = jnp.einsum("secd,edf->secf", inputs, full_up, preferred_element_type=jnp.float32)
    hidden_grad = jnp.einsum(
        "secd,efd->secf", grad_rows, full_down, preferred_element_type=jnp.float32
    )
    rows_total = sources * local_count * CAP
    sigmoid = jax.nn.sigmoid(gate_pre)
    hidden = (gate_pre * sigmoid * up_pre).astype(jnp.bfloat16)
    out_terms = jnp.einsum(
        "secf,efd->secd", hidden, full_down, preferred_element_type=jnp.float32
    ).reshape(rows_total, full_down.shape[2])
    out_share = lax.psum_scatter(
        out_terms.astype(jnp.bfloat16), "tensor", scatter_dimension=1, tiled=True
    )
    out_returned = lax.all_to_all(out_share, "expert", split_axis=0, concat_axis=0, tiled=True)
    up_grad = (hidden_grad * gate_pre * sigmoid).astype(jnp.bfloat16)
    gate_grad = (hidden_grad * up_pre * sigmoid * (1.0 + gate_pre * (1.0 - sigmoid))).astype(
        jnp.bfloat16
    )
    summed = jnp.einsum(
        "secf,edf->secd", gate_grad, full_gate, preferred_element_type=jnp.float32
    ) + jnp.einsum("secf,edf->secd", up_grad, full_up, preferred_element_type=jnp.float32)
    grad_terms = summed.reshape(rows_total, full_gate.shape[1])
    grad_share = lax.psum_scatter(
        grad_terms.astype(jnp.bfloat16), "tensor", scatter_dimension=1, tiled=True
    )
    grad_returned = lax.all_to_all(grad_share, "expert", split_axis=0, concat_axis=0, tiled=True)

    def combine(returned):
        picked = jnp.take(returned, targets, axis=0).reshape(
            tokens.shape[0], choose_count, returned.shape[1]
        )
        return jnp.sum(gate_values[:, :, None] * picked.astype(jnp.float32), axis=1).astype(
            jnp.bfloat16
        )

    return (combine(out_returned), combine(grad_returned))


def solution(mesh):
    return jax.shard_map(
        per_device,
        mesh=mesh,
        in_specs=(
            P(("groups", "expert", "sub"), "tensor"),
            P(("groups", "expert", "sub"), "tensor"),
            P(("groups", "expert", "sub"), None),
            P(("groups", "expert", "sub"), None),
            P("expert", "sub", "tensor"),
            P("expert", "sub", "tensor"),
            P("expert", "tensor", "sub"),
        ),
        out_specs=(
            P(("groups", "expert", "sub"), "tensor"),
            P(("groups", "expert", "sub"), "tensor"),
        ),
        check_vma=False,
    )
```

profile of v0, /device:TPU:0, one launch (start us, length us, event | category | flops | bytes accessed | tf_op | source)
XLA Modules:
  0.0 427.4 jit_solution(4336637303483103475)
XLA Ops:
  7.2 0.7 all-gather.4.cloned.1.call-update
  7.9 0.7 all-gather.6.cloned.1.call-update
  8.7 0.7 all-gather.8.cloned.1.call-update
  9.8 1.2 reduce-window.6
  11.4 21.3 %all_gather.15 = bf16[128,3072]{1,0:T(8,128)(2,1)S(1)} all-gather(bf16[128,768]{1,0:T(8,128)(2,1)S(1)} %copy-done), channel_id=1, replica_groups=mesh['groups'=2,'tensor'=4,'expert'=2,'sub'=2] {'tensor'}, dimensions={1}, use_global_device_ids=true | all-gather | bytes 983040 | tf_op jit(solution)/shard_map/all_gather | solution.py:39
  32.7 0.8 broadcast_in_dim.20
  34.7 2.1 convolution_convert_fusion.1
  36.9 4.1 all-to-all-start
  41.0 17.7 %all_gather.19 = bf16[128,3072]{1,0:T(8,128)(2,1)S(1)} all-gather(bf16[128,768]{1,0:T(8,128)(2,1)S(1)} %copy-done.1), channel_id=1, replica_groups=mesh['groups'=2,'tensor'=4,'expert'=2,'sub'=2] {'tensor'}, dimensions={1}, use_global_device_ids=true | all-gather | bytes 983040 | tf_op jit(solution)/shard_map/all_gather | solution.py:40
  58.7 0.8 broadcast_in_dim.21
  59.6 1.5 reshape.74
  61.1 3.4 convolution_convert_fusion
  64.4 4.8 %all-to-all-start.2 = ((bf16[2,160,3072]{2,1,0:T(8,128)(2,1)}), bf16[2,160,3072]{2,1,0:T(8,128)(2,1)}, u32[]{:S(2)}, u32[]{:S(2)}) async-start(bf16[2,160,3072]{2,1,0:T(8,128)(2,1)} %bitcast.80), calls=%async_computation.3 | async-start | bytes 3932160 | tf_op jit(solution)/shard_map/all_to_all | solution.py:44
  69.4 16.0 %all-gather.4.cloned.1.call-done = bf16[2,3072,4096]{2,1,0:T(8,128)(2,1)} async-done(((bf16[2,1536,4096]{2,1,0:T(8,128)(2,1)}), bf16[2,3072,4096]{2,1,0:T(8,128)(2,1)}) %all-gather.4.cloned.1.call-update) | async-done | bytes 50331664 | tf_op jit(solution)/shard_map/all_gather | solution.py:22
  85.4 30.2 %fusion.12 = f32[2,2,80,4096]{3,2,0,1:T(8,128)} fusion(bf16[2,3072,4096]{2,1,0:T(8,128)(2,1)} %all-gather.4.cloned.1.call-done, bf16[2,2,80,3072]{3,2,1,0:T(8,128)(2,1)S(1)} %bitcast.76), kind=kOutput, calls=%fused_computation.14 | convolution fusion | flops 8053063680 | bytes 57540608 | tf_op jit(solution)/shard_map/secd,edf->secf/dot_general | solution.py:48
  115.7 45.7 %all-gather.6.cloned.1.call-done = bf16[2,3072,4096]{2,1,0:T(8,128)(2,1)} async-done(((bf16[2,1536,4096]{2,1,0:T(8,128)(2,1)}), bf16[2,3072,4096]{2,1,0:T(8,128)(2,1)}) %all-gather.6.cloned.1.call-update) | async-done | bytes 50331664 | tf_op jit(solution)/shard_map/all_gather | solution.py:23
  161.4 30.3 %fusion.15 = f32[2,2,80,4096]{3,2,0,1:T(8,128)} fusion(bf16[2,3072,4096]{2,1,0:T(8,128)(2,1)} %all-gather.6.cloned.1.call-done, bf16[2,2,80,3072]{3,2,1,0:T(8,128)(2,1)S(1)} %bitcast.77), kind=kOutput, calls=%fused_computation.15 | convolution fusion | flops 8053063680 | bytes 57540608 | tf_op jit(solution)/shard_map/secd,edf->secf/dot_general | solution.py:49
  191.6 47.9 %all-gather.8.cloned.1.call-done = bf16[2,4096,3072]{2,1,0:T(8,128)(2,1)} async-done(((bf16[2,4096,1536]{2,1,0:T(8,128)(2,1)}), bf16[2,4096,3072]{2,1,0:T(8,128)(2,1)}) %all-gather.8.cloned.1.call-update) | async-done | bytes 50331664 | tf_op jit(solution)/shard_map/all_gather | solution.py:24
  239.5 24.4 %fusion.18 = f32[2,2,80,4096]{3,2,0,1:T(8,128)} fusion(bf16[2,4096,3072]{2,1,0:T(8,128)(2,1)} %all-gather.8.cloned.1.call-done, bf16[2,2,80,3072]{3,2,1,0:T(8,128)(2,1)} %bitcast.17), kind=kOutput, calls=%fused_computation.16 | convolution fusion | flops 8053063680 | bytes 57540608 | tf_op jit(solution)/shard_map/secd,efd->secf/dot_general | solution.py:50
  263.9 25.8 %fusion = f32[2,2,80,3072]{3,2,1,0:T(8,128)} fusion(bf16[2,3072,4096]{2,1,0:T(8,128)(2,1)} %all-gather.6.cloned.1.call-done, f32[2,2,80,4096]{3,2,0,1:T(8,128)} %fusion.18, f32[2,2,80,4096]{3,2,0,1:T(8,128)} %fusion.12), kind=kOutput, calls=%fused_computation.2 | convolution fusion | flops 8060928000 | bytes 64749568 | tf_op jit(solution)/shard_map/secf,edf->secd/dot_general | solution.py:69
  289.8 27.6 %fusion.29 = bf16[2,2,80,3072]{3,2,0,1:T(8,128)(2,1)S(1)} fusion(f32[2,2,80,3072]{3,2,1,0:T(8,128)} %fusion, bf16[2,3072,4096]{2,1,0:T(8,128)(2,1)} %all-gather.4.cloned.1.call-done, f32[2,2,80,4096]{3,2,0,1:T(8,128)} %fusion.12, f32[2,2,80,4096]{3,2,0,1:T(8,128)} %fusion.18, f32[2,2,80,4096]{3,2,0,1:T(8,128)} %fusion.15), kind=kOutput, calls=%fused_computation.26 | convolution fusion | flops 8068136960 | bytes 71958528 | tf_op jit(solution)/shard_map/secf,edf->secd/dot_general | solution.py:67
  317.4 1.4 copy.21
  318.9 21.8 %fusion.24 = bf16[2,2,80,3072]{3,2,0,1:T(8,128)(2,1)S(1)} fusion(bf16[2,4096,3072]{2,1,0:T(8,128)(2,1)} %all-gather.8.cloned.1.call-done, f32[2,2,80,4096]{3,2,0,1:T(8,128)} %fusion.15, f32[2,2,80,4096]{3,2,0,1:T(8,128)} %fusion.12), kind=kOutput, calls=%fused_computation.25 | convolution fusion | flops 8061911040 | bytes 62783488 | tf_op jit(solution)/shard_map/secf,efd->secd/dot_general | solution.py:56
  340.7 1.4 copy.19
  342.1 19.5 %reduce-scatter.5.cloned.1.call-done = bf16[320,768]{1,0:T(8,128)(2,1)} async-done(((bf16[320,3072]{1,0:T(8,128)(2,1)}), bf16[320,768]{1,0:T(8,128)(2,1)}) %reduce-scatter.5.cloned.1.call-update) | async-done | bytes 491536 | tf_op jit(solution)/shard_map/reduce_scatter | solution.py:71
  361.6 3.5 all-to-all-start.3
  365.2 39.3 %reduce-scatter.3.cloned.1.call-done = bf16[320,768]{1,0:T(8,128)(2,1)} async-done(((bf16[320,3072]{1,0:T(8,128)(2,1)}), bf16[320,768]{1,0:T(8,128)(2,1)}) %reduce-scatter.3.cloned.1.call-update) | async-done | bytes 491536 | tf_op jit(solution)/shard_map/reduce_scatter | solution.py:59
  404.5 3.5 all-to-all-start.1
  408.0 1.2 gather_fusion.1
  409.2 6.5 %all-to-all-done.1 = bf16[2,160,768]{2,1,0:T(8,128)(2,1)S(1)} async-done(((bf16[2,160,768]{2,1,0:T(8,128)(2,1)}), bf16[2,160,768]{2,1,0:T(8,128)(2,1)S(1)}, u32[]{:S(2)}, u32[]{:S(2)}) %all-to-all-start.1) | async-done | bytes 491552 | tf_op jit(solution)/shard_map/all_to_all | solution.py:62
  415.7 1.2 gather_fusion
  418.0 2.8 multiply_reduce_fusion
  (43 shorter events, 3.6 us)
Async XLA Ops:
  7.2 78.3 %all-gather.4.cloned.1.call-start = ((), (), s32[]{:S(2)}) async-start(), calls=%async_computation.6 | async-start | bytes 75497472 | tf_op jit(solution)/shard_map/all_gather | solution.py:22
  7.9 153.5 %all-gather.6.cloned.1.call-start = ((), (), s32[]{:S(2)}) async-start(), calls=%async_computation.7 | async-start | bytes 75497472 | tf_op jit(solution)/shard_map/all_gather | solution.py:23
  8.6 0.8 copy-start.5
  8.7 2.7 copy-start
  8.7 230.9 %all-gather.8.cloned.1.call-start = ((), (), s32[]{:S(2)}) async-start(), calls=%async_computation.8 | async-start | bytes 75497472 | tf_op jit(solution)/shard_map/all_gather | solution.py:24
  33.5 7.5 %copy-start.1 = (bf16[128,768]{1,0:T(8,128)(2,1)S(1)}, bf16[128,768]{1,0:T(8,128)(2,1)}, u32[]{:S(2)}) copy-start(bf16[128,768]{1,0:T(8,128)(2,1)} %param.10) | copy-start | bytes 589828
  34.7 26.3 %copy-start.2 = (s32[256]{0:T(256)}, s32[256]{0:T(256)S(1)}, u32[]{:S(2)}) copy-start(s32[256]{0:T(256)S(1)} %get-tuple-element.6) | copy-start | bytes 3076
  36.9 27.6 %all-to-all-start = ((bf16[2,160,3072]{2,1,0:T(8,128)(2,1)}), bf16[2,160,3072]{2,1,0:T(8,128)(2,1)S(1)}, u32[]{:S(2)}, u32[]{:S(2)}) async-start(bf16[2,160,3072]{2,1,0:T(8,128)(2,1)} %bitcast.81), calls=%async_computation | async-start | bytes 3932160 | tf_op jit(solution)/shard_map/all_to_all | solution.py:43
  64.4 127.2 %all-to-all-start.2 = ((bf16[2,160,3072]{2,1,0:T(8,128)(2,1)}), bf16[2,160,3072]{2,1,0:T(8,128)(2,1)}, u32[]{:S(2)}, u32[]{:S(2)}) async-start(bf16[2,160,3072]{2,1,0:T(8,128)(2,1)} %bitcast.80), calls=%async_computation.3 | async-start | bytes 3932160 | tf_op jit(solution)/shard_map/all_to_all | solution.py:44
  69.2 292.4 %reduce-scatter.5.cloned.1.call-start = ((), (), s32[]{:S(2)}) async-start(), calls=%async_computation.10 | async-start | bytes 2457600 | tf_op jit(solution)/shard_map/reduce_scatter | solution.py:71
  318.8 85.6 %reduce-scatter.3.cloned.1.call-start = ((), (), s32[]{:S(2)}) async-start(), calls=%async_computation.9 | async-start | bytes 2457600 | tf_op jit(solution)/shard_map/reduce_scatter | solution.py:59
  340.7 24.4 %copy-start.6 = (f32[128,2]{0,1:T(2,128)S(1)}, f32[128,2]{0,1:T(2,128)}, u32[]{:S(2)}) copy-start(f32[128,2]{0,1:T(2,128)} %param.12) | copy-start | bytes 3076
  340.7 67.3 %copy-start.3 = (s32[256]{0:T(256)S(1)}, s32[256]{0:T(256)}, u32[]{:S(2)}) copy-start(s32[256]{0:T(256)} %copy-done.2) | copy-start | bytes 3076
  342.1 74.8 %copy-start.4 = (pred[256]{0:T(512)(128)(4,1)S(1)}, pred[256]{0:T(512)(128)(4,1)}, u32[]{:S(2)}) copy-start(pred[256]{0:T(512)(128)(4,1)} %get-tuple-element.5) | copy-start | bytes 772
  361.6 42.9 %all-to-all-start.3 = ((bf16[2,160,768]{2,1,0:T(8,128)(2,1)}), bf16[2,160,768]{2,1,0:T(8,128)(2,1)S(1)}, u32[]{:S(2)}, u32[]{:S(2)}) async-start(bf16[2,160,768]{2,1,0:T(8,128)(2,1)} %bitcast.84), calls=%async_computation.5 | async-start | bytes 983040 | tf_op jit(solution)/shard_map/all_to_all | solution.py:74
  404.5 11.2 %all-to-all-start.1 = ((bf16[2,160,768]{2,1,0:T(8,128)(2,1)}), bf16[2,160,768]{2,1,0:T(8,128)(2,1)S(1)}, u32[]{:S(2)}, u32[]{:S(2)}) async-start(bf16[2,160,768]{2,1,0:T(8,128)(2,1)} %bitcast.85), calls=%async_computation.2 | async-start | bytes 983040 | tf_op jit(solution)/shard_map/all_to_all | solution.py:62
Sparse Core Ops, SparseCore 0:
  9.5 75.8 all-gather.3
  87.0 74.3 all-gather.5
  162.9 76.5 all-gather.7
  318.9 42.6 reduce-scatter.4
  363.8 40.6 reduce-scatter.2
where the time goes:
time: 428 us; the launch traced here: 427 us
  waiting for transfers between devices  177 us (41%)
  matrix products  166 us (39%)
  blocking collectives  39 us (9%)
  starting transfers between devices  16.2 us (4%)
  between operations  14 us (3%)
  local copies, waits for them, and re-layouts  10.7 us (2%)
  other arithmetic  4.92 us (1%)
    all_gather x1, waiting for transfers between devices, per_device(): lax.all_gather(w_down, 'sub', axis=2, tiled=True)  47.9 us
    all_gather x1, waiting for transfers between devices, per_device(): lax.all_gather(w_up, 'sub', axis=1, tiled=True)  45.7 us
    reduce_scatter x1, waiting for transfers between devices, per_device(): lax.psum_scatter(out_terms.astype(jnp.bfloat16), 'tensor', scatter_dimens...  39.3 us
    dot_general x1, matrix products, per_device(): jnp.einsum('secd,edf->secf', inputs, full_up, preferred_element_type=jnp....  30.3 us
    dot_general x1, matrix products, per_device(): jnp.einsum('secd,edf->secf', inputs, full_gate, preferred_element_type=jn...  30.2 us
    dot_general x1, matrix products, per_device(): jnp.einsum('secf,edf->secd', gate_grad, full_gate, preferred_element_type...  27.6 us
    dot_general x1, matrix products, per_device(): jnp.einsum('secf,edf->secd', up_grad, full_up, preferred_element_type=jnp...  25.8 us
    dot_general x1, matrix products, per_device(): jnp.einsum('secd,efd->secf', grad_rows, full_down, preferred_element_type...  24.4 us
  transfers between devices with their start and end apart: 9, of which 6 were waited for; matrix products, arithmetic and copies ran while one was open for 23% of the time, Pallas kernels for 0%

commit v1 on v0

v1 whole, which is shorter than its diff:
```python
import functools

import jax
import jax.numpy as jnp
from jax import lax
from jax.experimental import pallas as pl
from jax.experimental.pallas import tpu as pltpu
from jax.sharding import PartitionSpec as P

EXPERTS = 4
CAP = 80
BF16 = jnp.bfloat16
F32 = jnp.float32
VMEM_BYTES = 48 * 1024 * 1024


def slot_ranks(expert_ids, experts):
    flat_ids = expert_ids.reshape(-1)
    onehot = (flat_ids[:, None] == jnp.arange(experts, dtype=jnp.int32)[None, :]).astype(jnp.int32)
    earlier = jnp.cumsum(onehot, axis=0) - onehot
    return jnp.sum(earlier * onehot, axis=1).reshape(expert_ids.shape)


def swap(value, axis):
    return lax.ppermute(value, axis, [(0, 1), (1, 0)])


def across(value, distance):
    return lax.ppermute(value, "tensor", [(i, i ^ distance) for i in range(lax.axis_size("tensor"))])


def nt(a, b):
    return lax.dot_general(a, b, (((1,), (1,)), ((), ())), preferred_element_type=F32)


class Place:
    def __init__(self):
        self.sources = lax.axis_size("expert")
        self.tensors = lax.axis_size("tensor")
        self.small = self.sources == 2 and self.tensors == 4
        self.expert = lax.axis_index("expert")
        self.sub = lax.axis_index("sub")
        self.tensor = lax.axis_index("tensor")
        self.blocks = 2 * self.sources
        self.index = jnp.stack([self.expert, self.sub, self.tensor]).astype(jnp.int32)


def pieces_of(small, blocks, index_ref, width):
    if not small:
        return [(block, 0) for block in range(blocks)]
    expert, sub, tensor = index_ref[0], index_ref[1], index_ref[2]
    found = []
    for sub_far in range(2):
        for expert_far in range(2):
            for low_far in range(2):
                at_expert = expert + expert_far - 2 * expert * expert_far
                at_sub = sub + sub_far - 2 * sub * sub_far
                low = lax.rem(tensor, 2)
                low = low + low_far - 2 * low * low_far
                found.append((at_expert * 2 + at_sub, low * width))
    return found


def gather_rows(place, rows):
    if place.small:
        near = [rows] + [across(rows, k) for k in (1, 2, 3)]
        far = [swap(block, "expert") for block in near]
        high = (place.tensor // 2 + place.sub) % 2 == 1
        low_half = jnp.stack([near[0], near[1], far[0], far[1]])
        high_half = jnp.stack([near[2], near[3], far[2], far[3]])
        keep = jnp.where(high, high_half, low_half)
        send = jnp.where(high, low_half, high_half)
        return [keep, swap(send, "sub")]
    count = rows.shape[0]
    whole = lax.all_gather(rows, ("tensor", "expert"))
    whole = whole.reshape(place.tensors, place.sources, count, rows.shape[1])
    whole = whole.transpose(1, 2, 0, 3).reshape(place.sources, count, 2, -1)
    halves = (whole[:, :, 0], whole[:, :, 1])
    first = place.sub == 0
    keep = jnp.where(first, halves[0], halves[1])
    got = swap(jnp.where(first, halves[1], halves[0]), "sub")
    both = jnp.where(first, jnp.stack([keep, got], 1), jnp.stack([got, keep], 1))
    return [both.reshape((2 * place.sources, count, -1))]


def scatter_rows(place, parts):
    if place.small:
        kept, same_far, core_near, core_far = parts
        from_far = swap(same_far, "expert")
        from_core = swap(core_near, "sub")
        from_both = lax.ppermute(core_far, ("expert", "sub"), [(i, 3 - i) for i in range(4)])
        own_half = kept.astype(F32) + from_far.astype(F32)
        other_half = from_core.astype(F32) + from_both.astype(F32)
        high = (place.tensor // 2 + place.sub) % 2 == 1
        near_pair = jnp.where(high, other_half, own_half).astype(BF16)
        far_pair = jnp.where(high, own_half, other_half).astype(BF16)
        width = near_pair.shape[1] // 2
        total = near_pair[:, :width].astype(F32)
        total = total + across(near_pair[:, width:], 1).astype(F32)
        total = total + across(far_pair[:, :width], 2).astype(F32)
        total = total + across(far_pair[:, width:], 3).astype(F32)
        return total.astype(BF16)
    stacked = jnp.stack(parts)
    count, half = stacked.shape[1:]
    stacked = stacked.reshape(place.sources, 2, count, half)
    first = place.sub == 0
    keep = jnp.where(first, stacked[:, 0], stacked[:, 1])
    got = swap(jnp.where(first, stacked[:, 1], stacked[:, 0]), "sub")
    both = jnp.where(first, jnp.concatenate([keep, got], 2), jnp.concatenate([got, keep], 2))
    both = both.reshape(place.sources, count, place.tensors, -1).transpose(0, 2, 1, 3)
    share = lax.psum_scatter(both, "expert", scatter_dimension=0)
    return lax.psum_scatter(share, "tensor", scatter_dimension=0)


def chosen(meta, first_slot):
    rows = meta.shape[1]
    slots = (lax.broadcasted_iota(jnp.int32, (CAP, rows), 0) + first_slot).astype(F32)
    return slots == meta[0:1], slots == meta[1:2]


def place_rows(small, blocks, local, locals_, index_ref, meta_ref, groups, rows_ref):
    width = groups[0].shape[2]
    flat = [group.at[i] for group in groups for i in range(group.shape[0])]
    expert = index_ref[0] * locals_ + local
    for piece, (block, column) in zip(flat, pieces_of(small, blocks, index_ref, width), strict=True):
        one, two = chosen(meta_ref[block], expert * blocks * CAP + block * CAP)
        take = jnp.where(one | two, 1.0, 0.0).astype(BF16)
        start = block * CAP if isinstance(block, int) else pl.multiple_of(block * CAP, 16)
        column = column if isinstance(column, int) else pl.multiple_of(column, 128)
        rows_ref[pl.ds(start, CAP), pl.ds(column, width)] = jnp.dot(
            take, piece[...], preferred_element_type=F32
        ).astype(BF16)


def place_gates(blocks, local, locals_, index_ref, meta_ref, gate_ref):
    expert = index_ref[0] * locals_ + local
    for block in range(blocks):
        meta = meta_ref[block]
        one, two = chosen(meta, expert * blocks * CAP + block * CAP)
        weight = jnp.where(one, meta[2:3], 0.0) + jnp.where(two, meta[3:4], 0.0)
        gate_ref[block * CAP : (block + 1) * CAP, :] = jnp.sum(weight, axis=1, keepdims=True)


def combine_rows(small, blocks, locals_, index_ref, meta_ref, slots_of, outs):
    half = outs[0].shape[1]
    width = half // 2 if small else half
    for out_at, out in enumerate(outs):
        if small:
            expert, sub = index_ref[0], index_ref[1]
            expert_far, sub_far = out_at % 2, out_at // 2
            block = (expert + expert_far - 2 * expert * expert_far) * 2 + sub + sub_far - 2 * sub * sub_far
            start = pl.multiple_of(block * CAP, 16)
        else:
            block = out_at
            start = block * CAP
        total = None
        for local in range(locals_):
            first = (index_ref[0] * locals_ + local) * blocks * CAP + block * CAP
            one, two = chosen(meta_ref[block], first)
            take = jnp.where(one | two, 1.0, 0.0).astype(BF16)
            term = lax.dot_general(
                take, slots_of[local][pl.ds(start, CAP), :], (((0,), (0,)), ((), ())),
                preferred_element_type=F32,
            )
            total = term if total is None else total + term
        total = total.astype(BF16)
        if small:
            low = lax.rem(index_ref[2], 2)
            for chunk in range(2):
                column = (chunk + low - 2 * chunk * low) * width
                out[:, pl.ds(pl.multiple_of(column, 128), width)] = total[:, chunk * width : (chunk + 1) * width]
        else:
            out[...] = total


def first_body(small, blocks, local, locals_, n_groups, index_ref, meta_ref, *refs):
    groups, (gate_w, up_w, out, rows) = refs[:n_groups], refs[n_groups:]

    @pl.when(pl.program_id(0) == 0)
    def _():
        place_rows(small, blocks, local, locals_, index_ref, meta_ref, groups, rows)

    out[0] = jnp.dot(rows[...], gate_w[0], preferred_element_type=F32).astype(BF16)
    out[1] = jnp.dot(rows[...], up_w[0], preferred_element_type=F32).astype(BF16)


def middle_body(small, blocks, local, locals_, n_groups, index_ref, meta_ref, *refs):
    groups, refs = refs[:n_groups], refs[n_groups:]
    last = local == locals_ - 1
    before, refs = (refs[:local], refs[local:]) if last else ((), refs)
    own, other, down, slopes, back, *outs, rows, gates, total, slots = refs
    step = pl.program_id(0)

    @pl.when(step == 0)
    def _():
        place_rows(small, blocks, local, locals_, index_ref, meta_ref, groups, rows)
        place_gates(blocks, local, locals_, index_ref, meta_ref, gates)

    back[...] = nt(rows[...], down[0]).astype(BF16)
    gate_pre = own[0].astype(F32) + other[0].astype(F32)
    up_pre = own[1].astype(F32) + other[1].astype(F32)
    sigmoid = 0.5 * jnp.tanh(0.5 * gate_pre) + 0.5
    weight = gates[...]
    silu = gate_pre * sigmoid
    weighted = up_pre * weight
    hidden = (silu * weighted).astype(BF16)
    slopes[0] = (silu * weight).astype(BF16)
    slopes[1] = (weighted * (sigmoid + silu * (1.0 - sigmoid))).astype(BF16)
    term = jnp.dot(hidden, down[0], preferred_element_type=F32)

    @pl.when(step == 0)
    def _():
        total[...] = term

    @pl.when(step > 0)
    def _():
        total[...] += term

    @pl.when(step == pl.num_programs(0) - 1)
    def _():
        if last:
            slots[...] = total[...].astype(BF16)
            combine_rows(small, blocks, locals_, index_ref, meta_ref, [*before, slots], outs)
        else:
            outs[0][...] = total[...].astype(BF16)


def last_body(small, blocks, local, locals_, index_ref, meta_ref, *refs):
    last = local == locals_ - 1
    before, refs = (refs[:local], refs[local:]) if last else ((), refs)
    own, other, slopes, gate_w, up_w, *outs, total, slots = refs
    step = pl.program_id(0)
    back = own[...].astype(F32) + other[...].astype(F32)
    up_grad = (back * slopes[0].astype(F32)).astype(BF16)
    gate_grad = (back * slopes[1].astype(F32)).astype(BF16)
    term = nt(gate_grad, gate_w[0]) + nt(up_grad, up_w[0])

    @pl.when(step == 0)
    def _():
        total[...] = term

    @pl.when(step > 0)
    def _():
        total[...] += term

    @pl.when(step == pl.num_programs(0) - 1)
    def _():
        if last:
            slots[...] = total[...].astype(BF16)
            combine_rows(small, blocks, locals_, index_ref, meta_ref, [*before, slots], outs)
        else:
            outs[0][...] = total[...].astype(BF16)


def whole_spec(array):
    dims = len(array.shape)
    return pl.BlockSpec(array.shape, lambda f, index: (0,) * dims)


def call(body, grid, index, ins, in_specs, outs, out_specs, scratch, flops, moved):
    return pl.pallas_call(
        body,
        grid_spec=pltpu.PrefetchScalarGridSpec(
            num_scalar_prefetch=1, grid=(grid,), in_specs=in_specs, out_specs=out_specs, scratch_shapes=scratch
        ),
        out_shape=outs,
        compiler_params=pltpu.CompilerParams(vmem_limit_bytes=VMEM_BYTES),
        cost_estimate=pl.CostEstimate(flops=flops, bytes_accessed=moved, transcendentals=0),
    )(index, *ins)


def per_device(tokens, cotangent, expert_ids, gate_values, w_gate, w_up, w_down):
    place = Place()
    small, blocks, index = place.small, place.blocks, place.index
    locals_, half, hidden = w_gate.shape
    count = tokens.shape[0]
    slots = blocks * CAP
    tile = min(1024, hidden)
    steps = hidden // tile
    flops = 2 * slots * half * hidden
    weight_bytes = half * hidden * 2

    block = place.expert * 2 + place.sub
    slot = expert_ids * slots + block * CAP + slot_ranks(expert_ids, EXPERTS)
    meta = jnp.concatenate([slot.astype(F32).T, gate_values.T, jnp.zeros((4, count), F32)])
    meta = lax.all_gather(meta, ("expert", "sub"))

    token_groups = gather_rows(place, tokens)
    grad_groups = gather_rows(place, cotangent)
    n_groups = len(token_groups)

    by_column = [
        pl.BlockSpec((1, half, tile), functools.partial(lambda local, f, index: (local, 0, f), local))
        for local in range(locals_)
    ]
    by_row = [
        pl.BlockSpec((1, tile, half), functools.partial(lambda local, f, index: (local, f, 0), local))
        for local in range(locals_)
    ]
    pair_spec = pl.BlockSpec((2, slots, tile), lambda f, index: (0, 0, f))
    one_spec = pl.BlockSpec((slots, tile), lambda f, index: (0, f))
    pair = jax.ShapeDtypeStruct((2, slots, hidden), BF16)
    one = jax.ShapeDtypeStruct((slots, hidden), BF16)
    slot_rows = jax.ShapeDtypeStruct((slots, half), BF16)
    row_parts = [jax.ShapeDtypeStruct((count, half), BF16)] * blocks

    def ends(local):
        shapes = row_parts if local == locals_ - 1 else [slot_rows]
        return shapes, [whole_spec(shape) for shape in shapes]

    own_pre, other_pre = [], []
    for local in range(locals_):
        own = call(
            functools.partial(first_body, small, blocks, local, locals_, n_groups),
            steps, index,
            [meta, *token_groups, w_gate, w_up],
            [whole_spec(meta), *map(whole_spec, token_groups), by_column[local], by_column[local]],
            pair, pair_spec,
            [pltpu.VMEM((slots, half), BF16)],
            2 * flops, 2 * weight_bytes,
        )
        own_pre.append(own)
        other_pre.append(swap(own, "sub"))

    done, own_back, other_back, slopes = [], [], [], []
    for local in range(locals_):
        before = done if local == locals_ - 1 else []
        shapes, specs = ends(local)
        slope, back, *rest = call(
            functools.partial(middle_body, small, blocks, local, locals_, n_groups),
            steps, index,
            [meta, *grad_groups, *before, own_pre[local], other_pre[local], w_down],
            [whole_spec(meta), *map(whole_spec, grad_groups), *map(whole_spec, before), pair_spec, pair_spec,
             by_row[local]],
            [pair, one, *shapes], [pair_spec, one_spec, *specs],
            [pltpu.VMEM((slots, half), BF16), pltpu.VMEM((slots, 1), F32), pltpu.VMEM((slots, half), F32),
             pltpu.VMEM((slots, half), BF16)],
            2 * flops, weight_bytes,
        )
        slopes.append(slope)
        own_back.append(back)
        other_back.append(swap(back, "sub"))
        done.append(rest[0])
    mixed = scatter_rows(place, rest)

    done = []
    for local in range(locals_):
        before = done if local == locals_ - 1 else []
        shapes, specs = ends(local)
        rest = call(
            functools.partial(last_body, small, blocks, local, locals_),
            steps, index,
            [meta, *before, own_back[local], other_back[local], slopes[local], w_gate, w_up],
            [whole_spec(meta), *map(whole_spec, before), one_spec, one_spec, pair_spec, by_column[local],
             by_column[local]],
            shapes, specs,
            [pltpu.VMEM((slots, half), F32), pltpu.VMEM((slots, half), BF16)],
            2 * flops, 2 * weight_bytes,
        )
        done.append(rest[0])
    return mixed, scatter_rows(place, rest)


def solution(mesh):
    rows = P(("groups", "expert", "sub"), "tensor")
    ids = P(("groups", "expert", "sub"), None)
    return jax.shard_map(
        per_device,
        mesh=mesh,
        in_specs=(rows, rows, ids, ids, P("expert", "sub", "tensor"), P("expert", "sub", "tensor"),
                  P("expert", "tensor", "sub")),
        out_specs=(rows, rows),
        check_vma=False,
    )
```

time: 428 us -> 228 us (0.53)
  matrix products: 166 us -> 0 us
  waiting for transfers between devices: 177 us -> 72.8 us
  Pallas kernels: 0 us -> 96.4 us
  blocking collectives: 39 us -> 5.17 us
  starting transfers between devices: 16.2 us -> 35.4 us
  between operations: 14 us -> 0.81 us
    dot_general x8 -> x0, matrix products: 166 us -> none  [the longest x1 30.3 us: per_device(): jnp.einsum('secd,edf->secf', inputs, full_up, preferred_element_type=jnp....]
    all_gather x3 -> x0, waiting for transfers between devices: 110 us -> none  [the longest x1 47.9 us: per_device(): lax.all_gather(w_down, 'sub', axis=2, tiled=True)]
    pallas_call x0 -> x6, Pallas kernels: none -> 96.4 us  [call(): pl.pallas_call(body, grid_spec=pltpu.PrefetchScalarGridSpec(num_scalar_pr...]
    ppermute x0 -> x32, waiting for transfers between devices: none -> 72.8 us  [the longest x12 35.3 us: across(): lax.ppermute(value, 'tensor', [(i, i ^ distance) for i in range(lax.axis_...]
    reduce_scatter x2 -> x0, waiting for transfers between devices: 58.7 us -> none  [the longest x1 39.3 us: per_device(): lax.psum_scatter(out_terms.astype(jnp.bfloat16), 'tensor', scatter_dimens...]
    ppermute x0 -> x32, starting transfers between devices: none -> 35.4 us  [the longest x12 19.5 us: across(): lax.ppermute(value, 'tensor', [(i, i ^ distance) for i in range(lax.axis_...]
    all_gather x2 -> x1, blocking collectives: 39 us -> 5.17 us  [per_device(): meta = lax.all_gather(meta, ('expert', 'sub'))]
    all_to_all x4 -> x0, starting transfers between devices: 15.8 us -> none  [the longest x1 4.75 us: per_device(): lax.all_to_all(dispatch(whole_grads), 'expert', split_axis=0, concat_axis...]
  transfers between devices with their start and end apart: 9 -> 32, of which waited for: 6 -> 14; matrix products, arithmetic and copies ran while one was open for 23% -> 3% of each run, Pallas kernels for 0% -> 36%
where the time goes in v1:
time: 228 us; the launch traced here: 226 us
  Pallas kernels  96.4 us (42%)
  waiting for transfers between devices  72.8 us (32%)
  starting transfers between devices  35.4 us (16%)
  local copies, waits for them, and re-layouts  9.28 us (4%)
  other arithmetic  6.25 us (3%)
  blocking collectives  5.17 us (2%)
    pallas_call x6, Pallas kernels, call(): pl.pallas_call(body, grid_spec=pltpu.PrefetchScalarGridSpec(num_scalar_pr...  96.4 us
    ppermute x12, waiting for transfers between devices, across(): lax.ppermute(value, 'tensor', [(i, i ^ distance) for i in range(lax.axis_...  35.3 us
    ppermute x18, waiting for transfers between devices, swap(): return lax.ppermute(value, axis, [(0, 1), (1, 0)])  33.4 us
    ppermute x12, starting transfers between devices, across(): lax.ppermute(value, 'tensor', [(i, i ^ distance) for i in range(lax.axis_...  19.5 us
    ppermute x18, starting transfers between devices, swap(): return lax.ppermute(value, axis, [(0, 1), (1, 0)])  12.8 us
    unnamed x13, local copies, waits for them, and re-layouts  8.36 us
    all_gather x1, blocking collectives, per_device(): meta = lax.all_gather(meta, ('expert', 'sub'))  5.17 us
  transfers between devices with their start and end apart: 32, of which 14 were waited for; matrix products, arithmetic and copies ran while one was open for 3% of the time, Pallas kernels for 36%

profile of v1, /device:TPU:0, one launch (start us, length us, event | category | flops | bytes accessed | tf_op | source)
XLA Modules:
  0.0 226.0 jit_solution(14640526755351246644)
XLA Ops:
  0.6 4.1 %collective-permute-start.8 = (bf16[128,768]{1,0:T(8,128)(2,1)}, bf16[128,768]{1,0:T(8,128)(2,1)S(1)}, u32[]{:S(2)}, u32[]{:S(2)}) collective-permute-start(bf16[128,768]{1,0:T(8,128)(2,1)} %param.7), channel_id=1, source_target_pairs={{0,8},{4,12},{8,0},{12,4},{1,9},{5,13},{9,1},{13,5},{2,10},{6,14},... | collective-permute-start | bytes 589832 | tf_op jit(solution)/shard_map/ppermute | solution.py:29
  6.3 1.5 collective-permute-start.13
  8.7 10.4 %collective-permute-done.8 = bf16[128,768]{1,0:T(8,128)(2,1)S(1)} collective-permute-done((bf16[128,768]{1,0:T(8,128)(2,1)}, bf16[128,768]{1,0:T(8,128)(2,1)S(1)}, u32[]{:S(2)}, u32[]{:S(2)}) %collective-permute-start.8) | collective-permute-done | bytes 196640 | tf_op jit(solution)/shard_map/ppermute | solution.py:29
  19.1 1.8 collective-permute-start.10
  21.2 1.8 collective-permute-start.14
  24.5 2.4 %collective-permute-done.10 = bf16[128,768]{1,0:T(8,128)(2,1)S(1)} collective-permute-done((bf16[128,768]{1,0:T(8,128)(2,1)S(1)}, bf16[128,768]{1,0:T(8,128)(2,1)S(1)}, u32[]{:S(2)}, u32[]{:S(2)}) %collective-permute-start.10) | collective-permute-done | bytes 196640 | tf_op jit(solution)/shard_map/ppermute | solution.py:25
  27.0 3.7 %collective-permute-done.11 = bf16[128,768]{1,0:T(8,128)(2,1)S(1)} collective-permute-done((bf16[128,768]{1,0:T(8,128)(2,1)S(1)}, bf16[128,768]{1,0:T(8,128)(2,1)S(1)}, u32[]{:S(2)}, u32[]{:S(2)}) %collective-permute-start.11) | collective-permute-done | bytes 196640 | tf_op jit(solution)/shard_map/ppermute | solution.py:25
  30.7 2.1 collective-permute-done.14
  36.0 5.2 %all-gather = f32[32,128]{1,0:T(8,128)S(1)} all-gather(f32[8,128]{1,0:T(8,128)S(1)} %maximum_maximum_fusion), channel_id=2, replica_groups=mesh['groups'=2,'tensor'=4,'expert'=2,'sub'=2] {'expert','sub'}, dimensions={0}, use_global_device_ids=true | all-gather | bytes 20480 | tf_op jit(solution)/shard_map/all_gather | solution.py:286
  41.3 15.1 %shard_map.86.refs_2_ = bf16[2,320,4096]{2,1,0:T(8,128)(2,1)} custom-call(s32[3]{0:T(128)S(1)} %pad_add_fusion.index_ref, f32[4,8,128]{2,1,0:T(8,128)S(1)} %bitcast.42, bf16[4,128,768]{2,1,0:T(8,128)(2,1)S(1)} %get-tuple-element.33.refs_0_, bf16[4,128,768]{2,1,0:T(8,128)(2,1)S(1)} %collective-permute-done.15.refs_1_, bf16[2,1536,4096]{2,1,0:T(8,128)(2,1)} %refs_4_.5, ...), custom_call_target="tpu_custom_call" | custom-call | flops 8053063680 | bytes 25165824 | tf_op jit(solution)/shard_map/pallas_call | solution.py:261
  56.7 15.2 %shard_map.88.refs_3_ = bf16[2,320,4096]{2,1,0:T(8,128)(2,1)} custom-call(s32[3]{0:T(128)S(1)} %pad_add_fusion.index_ref, f32[4,8,128]{2,1,0:T(8,128)S(1)} %bitcast.43, bf16[4,128,768]{2,1,0:T(8,128)(2,1)S(1)} %get-tuple-element.33.refs_0_, bf16[4,128,768]{2,1,0:T(8,128)(2,1)S(1)} %collective-permute-done.15.refs_1_, bf16[2,1536,4096]{2,1,0:T(8,128)(2,1)} %refs_4_.5, ...), custom_call_target="tpu_custom_call" | custom-call | flops 8053063680 | bytes 25165824 | tf_op jit(solution)/shard_map/pallas_call | solution.py:261
  72.2 3.4 %collective-permute-start = (bf16[128,768]{1,0:T(8,128)(2,1)S(1)}, bf16[128,768]{1,0:T(8,128)(2,1)S(1)}, u32[]{:S(2)}, u32[]{:S(2)}) collective-permute-start(bf16[128,768]{1,0:T(8,128)(2,1)S(1)} %copy-done.5), channel_id=1, source_target_pairs={{0,8},{4,12},{8,0},{12,4},{1,9},{5,13},{9,1},{13,5},{2,10},{6,14},... | collective-permute-start | bytes 589832 | tf_op jit(solution)/shard_map/ppermute | solution.py:29
  77.0 12.7 %collective-permute-done = bf16[128,768]{1,0:T(8,128)(2,1)S(1)} collective-permute-done((bf16[128,768]{1,0:T(8,128)(2,1)S(1)}, bf16[128,768]{1,0:T(8,128)(2,1)S(1)}, u32[]{:S(2)}, u32[]{:S(2)}) %collective-permute-start) | collective-permute-done | bytes 196640 | tf_op jit(solution)/shard_map/ppermute | solution.py:29
  93.2 4.3 %collective-permute-done.5 = bf16[128,768]{1,0:T(8,128)(2,1)S(1)} collective-permute-done((bf16[128,768]{1,0:T(8,128)(2,1)S(1)}, bf16[128,768]{1,0:T(8,128)(2,1)S(1)}, u32[]{:S(2)}, u32[]{:S(2)}) %collective-permute-start.5) | collective-permute-done | bytes 196640 | tf_op jit(solution)/shard_map/ppermute | solution.py:25
  99.0 2.7 %collective-permute-done.2 = bf16[128,768]{1,0:T(8,128)(2,1)S(1)} collective-permute-done((bf16[128,768]{1,0:T(8,128)(2,1)S(1)}, bf16[128,768]{1,0:T(8,128)(2,1)S(1)}, u32[]{:S(2)}, u32[]{:S(2)}) %collective-permute-start.2) | collective-permute-done | bytes 196640 | tf_op jit(solution)/shard_map/ppermute | solution.py:25
  101.7 4.2 %collective-permute-done.3 = bf16[128,768]{1,0:T(8,128)(2,1)S(1)} collective-permute-done((bf16[128,768]{1,0:T(8,128)(2,1)S(1)}, bf16[128,768]{1,0:T(8,128)(2,1)S(1)}, u32[]{:S(2)}, u32[]{:S(2)}) %collective-permute-start.3) | collective-permute-done | bytes 196640 | tf_op jit(solution)/shard_map/ppermute | solution.py:25
  105.9 2.7 %collective-permute-done.6 = bf16[128,768]{1,0:T(8,128)(2,1)S(1)} collective-permute-done((bf16[128,768]{1,0:T(8,128)(2,1)S(1)}, bf16[128,768]{1,0:T(8,128)(2,1)S(1)}, u32[]{:S(2)}, u32[]{:S(2)}) %collective-permute-start.6) | collective-permute-done | bytes 196640 | tf_op jit(solution)/shard_map/ppermute | solution.py:25
  108.9 2.3 %collective-permute-done.7.refs_1_ = bf16[4,128,768]{2,1,0:T(8,128)(2,1)S(1)} collective-permute-done((bf16[4,128,768]{2,1,0:T(8,128)(2,1)S(1)}, bf16[4,128,768]{2,1,0:T(8,128)(2,1)S(1)}, u32[]{:S(2)}, u32[]{:S(2)}) %collective-permute-start.7) | collective-permute-done | bytes 786464 | tf_op jit(solution)/shard_map/ppermute | solution.py:25
  111.2 2.3 %copy-done.2 = bf16[2,320,4096]{2,1,0:T(8,128)(2,1)} copy-done((bf16[2,320,4096]{2,1,0:T(8,128)(2,1)}, bf16[2,320,4096]{2,1,0:T(8,128)(2,1)S(1)}, u32[]{:S(2)}) %copy-start.2) | copy-done | bytes 5242904
  113.5 16.6 %shard_map.87 = (bf16[2,320,4096]{2,1,0:T(8,128)(2,1)}, bf16[320,4096]{1,0:T(8,128)(2,1)S(1)}, bf16[320,1536]{1,0:T(8,128)(2,1)S(1)}) custom-call(s32[3]{0:T(128)S(1)} %pad_add_fusion.index_ref, f32[4,8,128]{2,1,0:T(8,128)S(1)} %bitcast.44, bf16[4,128,768]{2,1,0:T(8,128)(2,1)S(1)} %get-tuple-element.35.refs_0_, ...), custom_call_target="tpu_custom_call" | custom-call | flops 8053063680 | bytes 12582912 | tf_op jit(solution)/shard_map/pallas_call | solution.py:261
  130.2 2.3 %copy-done.1 = bf16[2,320,4096]{2,1,0:T(8,128)(2,1)} copy-done((bf16[2,320,4096]{2,1,0:T(8,128)(2,1)}, bf16[2,320,4096]{2,1,0:T(8,128)(2,1)S(1)}, u32[]{:S(2)}) %copy-start.1) | copy-done | bytes 5242904
  132.5 18.1 %shard_map.89 = (bf16[2,320,4096]{2,1,0:T(8,128)(2,1)}, bf16[320,4096]{1,0:T(8,128)(2,1)}, bf16[128,1536]{1,0:T(8,128)(2,1)S(1)}, bf16[128,1536]{1,0:T(8,128)(2,...) custom-call(s32[3]{0:T(128)S(1)} %pad_add_fusion.index_ref, f32[4,8,128]{2,1,0:T(8,128)S(1)} %bitcast.45, ...), custom_call_target="tpu_custom_call" | custom-call | flops 8053063680 | bytes 12582912 | tf_op jit(solution)/shard_map/pallas_call | solution.py:261
  153.1 1.5 copy-done.3
  154.6 15.3 %shard_map.90.refs_0_ = bf16[320,1536]{1,0:T(8,128)(2,1)S(1)} custom-call(s32[3]{0:T(128)S(1)} %pad_add_fusion.index_ref, f32[4,8,128]{2,1,0:T(8,128)S(1)} %bitcast.46, bf16[320,4096]{1,0:T(8,128)(2,1)S(1)} %get-tuple-element.20.refs_0_, bf16[320,4096]{1,0:T(8,128)(2,1)} %copy-done.3, bf16[2,320,4096]{2,1,0:T(8,128)(2,1)} %get-tuple-element.21.refs_2_, ...), custom_call_target="tpu_custom_call" | custom-call | flops 8053063680 | bytes 25165824 | tf_op jit(solution)/shard_map/pallas_call | solution.py:261
  169.9 1.5 copy-done.4
  171.4 16.1 %shard_map.91 = (bf16[128,1536]{1,0:T(8,128)(2,1)S(1)}, bf16[128,1536]{1,0:T(8,128)(2,1)S(1)}, bf16[128,1536]{1,0:T(8,128)(2,1)S(1)}, bf16[128,1536]{1,0:T(8,128)(2,1)S(1)}) custom-call(s32[3]{0:T(128)S(1)} %pad_add_fusion.index_ref, f32[4,8,128]{2,1,0:T(8,128)S(1)} %bitcast.47, bf16[320,1536]{1,0:T(8,128)(2,1)S(1)} %shard_map.90.refs_0_, ...), custom_call_target="tpu_custom_call" | custom-call | flops 8053063680 | bytes 25165824 | tf_op jit(solution)/shard_map/pallas_call | solution.py:261
  187.5 1.6 collective-permute-start.27
  190.0 2.9 %collective-permute-start.22 = (bf16[128,768]{1,0:T(8,128)(2,1)S(1)}, bf16[128,768]{1,0:T(8,128)(2,1)S(1)}, u32[]{:S(2)}, u32[]{:S(2)}) collective-permute-start(bf16[128,768]{1,0:T(8,128)(2,1)S(1)} %get-tuple-element.38), channel_id=1, source_target_pairs={{0,8},{4,12},{8,0},{12,4},{1,9},{5,13},{9,1},{13,5},{2,10},{6,14},... | collective-permute-start | bytes 589832 | tf_op jit(solution)/shard_map/ppermute | solution.py:29
  194.5 4.1 %collective-permute-done.27 = bf16[128,1536]{1,0:T(8,128)(2,1)S(1)} collective-permute-done((bf16[128,1536]{1,0:T(8,128)(2,1)S(1)}, bf16[128,1536]{1,0:T(8,128)(2,1)S(1)}, u32[]{:S(2)}, u32[]{:S(2)}) %collective-permute-start.27) | collective-permute-done | bytes 393248 | tf_op jit(solution)/shard_map/ppermute | solution.py:91
  198.6 8.9 %collective-permute-done.28 = bf16[128,1536]{1,0:T(8,128)(2,1)S(1)} collective-permute-done((bf16[128,1536]{1,0:T(8,128)(2,1)S(1)}, bf16[128,1536]{1,0:T(8,128)(2,1)S(1)}, u32[]{:S(2)}, u32[]{:S(2)}) %collective-permute-start.28) | collective-permute-done | bytes 393248 | tf_op jit(solution)/shard_map/ppermute | solution.py:25
  207.7 2.9 %collective-permute-start.30 = (bf16[128,768]{1,0:T(8,128)(2,1)S(1)}, bf16[128,768]{1,0:T(8,128)(2,1)S(1)}, u32[]{:S(2)}, u32[]{:S(2)}) collective-permute-start(bf16[128,768]{1,0:T(8,128)(2,1)S(1)} %get-tuple-element.36), channel_id=1, source_target_pairs={{0,8},{4,12},{8,0},{12,4},{1,9},{5,13},{9,1},{13,5},{2,10},{6,14},... | collective-permute-start | bytes 589832 | tf_op jit(solution)/shard_map/ppermute | solution.py:29
  213.0 11.7 %collective-permute-done.30 = bf16[128,768]{1,0:T(8,128)(2,1)S(1)} collective-permute-done((bf16[128,768]{1,0:T(8,128)(2,1)S(1)}, bf16[128,768]{1,0:T(8,128)(2,1)S(1)}, u32[]{:S(2)}, u32[]{:S(2)}) %collective-permute-start.30) | collective-permute-done | bytes 196640 | tf_op jit(solution)/shard_map/ppermute | solution.py:29
  (80 shorter events, 23.7 us)
Async XLA Ops:
  0.6 18.5 %collective-permute-start.8 = (bf16[128,768]{1,0:T(8,128)(2,1)}, bf16[128,768]{1,0:T(8,128)(2,1)S(1)}, u32[]{:S(2)}, u32[]{:S(2)}) collective-permute-start(bf16[128,768]{1,0:T(8,128)(2,1)} %param.7), channel_id=1, source_target_pairs={{0,8},{4,12},{8,0},{12,4},{1,9},{5,13},{9,1},{13,5},{2,10},{6,14},... | collective-permute-start | bytes 589832 | tf_op jit(solution)/shard_map/ppermute | solution.py:29
  4.7 16.3 %collective-permute-start.9 = (bf16[128,768]{1,0:T(8,128)(2,1)}, bf16[128,768]{1,0:T(8,128)(2,1)S(1)}, u32[]{:S(2)}, u32[]{:S(2)}) collective-permute-start(bf16[128,768]{1,0:T(8,128)(2,1)} %param.7), channel_id=1, source_target_pairs={{0,12},{4,8},{8,4},{12,0},{1,13},{5,9},{9,5},{13,1},{2,14},{6,10},... | collective-permute-start | bytes 589832 | tf_op jit(solution)/shard_map/ppermute | solution.py:29
  6.1 15.1 %collective-permute-start.12 = (bf16[128,768]{1,0:T(8,128)(2,1)}, bf16[128,768]{1,0:T(8,128)(2,1)S(1)}, u32[]{:S(2)}, u32[]{:S(2)}) collective-permute-start(bf16[128,768]{1,0:T(8,128)(2,1)} %param.7), channel_id=1, source_target_pairs={{0,4},{4,0},{8,12},{12,8},{1,5},{5,1},{9,13},{13,9},{2,6},{6,2},{1... | collective-permute-start | bytes 589832 | tf_op jit(solution)/shard_map/ppermute | solution.py:29
  6.3 18.2 %collective-permute-start.13 = (bf16[128,768]{1,0:T(8,128)(2,1)}, bf16[128,768]{1,0:T(8,128)(2,1)S(1)}, u32[]{:S(2)}, u32[]{:S(2)}) collective-permute-start(bf16[128,768]{1,0:T(8,128)(2,1)} %param.7), channel_id=1, source_target_pairs={{0,2},{2,0},{1,3},{3,1},{4,6},{6,4},{5,7},{7,5},{8,10},{10,8},{9,1... | collective-permute-start | bytes 589832 | tf_op jit(solution)/shard_map/ppermute | solution.py:25
  19.1 7.8 %collective-permute-start.10 = (bf16[128,768]{1,0:T(8,128)(2,1)S(1)}, bf16[128,768]{1,0:T(8,128)(2,1)S(1)}, u32[]{:S(2)}, u32[]{:S(2)}) collective-permute-start(bf16[128,768]{1,0:T(8,128)(2,1)S(1)} %collective-permute-done.8), channel_id=1, source_target_pairs={{0,2},{2,0},{1,3},{3,1},{4,6},{6,4},{5,7},{7,5},{8,10},{10,8},{9,1... | collective-permute-start | bytes 589832 | tf_op jit(solution)/shard_map/ppermute | solution.py:25
  21.0 9.7 %collective-permute-start.11 = (bf16[128,768]{1,0:T(8,128)(2,1)S(1)}, bf16[128,768]{1,0:T(8,128)(2,1)S(1)}, u32[]{:S(2)}, u32[]{:S(2)}) collective-permute-start(bf16[128,768]{1,0:T(8,128)(2,1)S(1)} %collective-permute-done.9), channel_id=1, source_target_pairs={{0,2},{2,0},{1,3},{3,1},{4,6},{6,4},{5,7},{7,5},{8,10},{10,8},{9,1... | collective-permute-start | bytes 589832 | tf_op jit(solution)/shard_map/ppermute | solution.py:25
  21.2 11.7 %collective-permute-start.14 = (bf16[128,768]{1,0:T(8,128)(2,1)S(1)}, bf16[128,768]{1,0:T(8,128)(2,1)S(1)}, u32[]{:S(2)}, u32[]{:S(2)}) collective-permute-start(bf16[128,768]{1,0:T(8,128)(2,1)S(1)} %collective-permute-done.12), channel_id=1, source_target_pairs={{0,2},{2,0},{1,3},{3,1},{4,6},{6,4},{5,7},{7,5},{8,10},{10,8},{9,1... | collective-permute-start | bytes 589832 | tf_op jit(solution)/shard_map/ppermute | solution.py:25
  34.0 7.3 %collective-permute-start.15 = (bf16[4,128,768]{2,1,0:T(8,128)(2,1)S(1)}, bf16[4,128,768]{2,1,0:T(8,128)(2,1)S(1)}, u32[]{:S(2)}, u32[]{:S(2)}) collective-permute-start(bf16[4,128,768]{2,1,0:T(8,128)(2,1)S(1)} %get-tuple-element.32), channel_id=1, source_target_pairs={{0,1},{1,0},{2,3},{3,2},{4,5},{5,4},{6,7},{7,6},{8,9},{9,8},{10,11... | collective-permute-start | bytes 2359304 | tf_op jit(solution)/shard_map/ppermute | solution.py:25
  56.4 54.8 %collective-permute-start.16 = (bf16[2,320,4096]{2,1,0:T(8,128)(2,1)}, bf16[2,320,4096]{2,1,0:T(8,128)(2,1)S(1)}, u32[]{:S(2)}, u32[]{:S(2)}) collective-permute-start(bf16[2,320,4096]{2,1,0:T(8,128)(2,1)} %shard_map.86.refs_2_), channel_id=1, source_target_pairs={{0,1},{1,0},{2,3},{3,2},{4,5},{5,4},{6,7},{7,6},{8,9},{9,8},{10,11... | collective-permute-start | bytes 15728648 | tf_op jit(solution)/shard_map/ppermute | solution.py:25
  72.0 58.3 %collective-permute-start.17 = (bf16[2,320,4096]{2,1,0:T(8,128)(2,1)}, bf16[2,320,4096]{2,1,0:T(8,128)(2,1)S(1)}, u32[]{:S(2)}, u32[]{:S(2)}) collective-permute-start(bf16[2,320,4096]{2,1,0:T(8,128)(2,1)} %shard_map.88.refs_3_), channel_id=1, source_target_pairs={{0,1},{1,0},{2,3},{3,2},{4,5},{5,4},{6,7},{7,6},{8,9},{9,8},{10,11... | collective-permute-start | bytes 15728648 | tf_op jit(solution)/shard_map/ppermute | solution.py:25
  72.2 17.5 %collective-permute-start = (bf16[128,768]{1,0:T(8,128)(2,1)S(1)}, bf16[128,768]{1,0:T(8,128)(2,1)S(1)}, u32[]{:S(2)}, u32[]{:S(2)}) collective-permute-start(bf16[128,768]{1,0:T(8,128)(2,1)S(1)} %copy-done.5), channel_id=1, source_target_pairs={{0,8},{4,12},{8,0},{12,4},{1,9},{5,13},{9,1},{13,5},{2,10},{6,14},... | collective-permute-start | bytes 589832 | tf_op jit(solution)/shard_map/ppermute | solution.py:29
  75.6 15.6 %collective-permute-start.1 = (bf16[128,768]{1,0:T(8,128)(2,1)S(1)}, bf16[128,768]{1,0:T(8,128)(2,1)S(1)}, u32[]{:S(2)}, u32[]{:S(2)}) collective-permute-start(bf16[128,768]{1,0:T(8,128)(2,1)S(1)} %copy-done.5), channel_id=1, source_target_pairs={{0,12},{4,8},{8,4},{12,0},{1,13},{5,9},{9,5},{13,1},{2,14},{6,10},... | collective-permute-start | bytes 589832 | tf_op jit(solution)/shard_map/ppermute | solution.py:29
  76.5 15.3 %collective-permute-start.4 = (bf16[128,768]{1,0:T(8,128)(2,1)S(1)}, bf16[128,768]{1,0:T(8,128)(2,1)S(1)}, u32[]{:S(2)}, u32[]{:S(2)}) collective-permute-start(bf16[128,768]{1,0:T(8,128)(2,1)S(1)} %copy-done.5), channel_id=1, source_target_pairs={{0,4},{4,0},{8,12},{12,8},{1,5},{5,1},{9,13},{13,9},{2,6},{6,2},{1... | collective-permute-start | bytes 589832 | tf_op jit(solution)/shard_map/ppermute | solution.py:29
  89.7 7.8 %collective-permute-start.5 = (bf16[128,768]{1,0:T(8,128)(2,1)S(1)}, bf16[128,768]{1,0:T(8,128)(2,1)S(1)}, u32[]{:S(2)}, u32[]{:S(2)}) collective-permute-start(bf16[128,768]{1,0:T(8,128)(2,1)S(1)} %copy-done.5), channel_id=1, source_target_pairs={{0,2},{2,0},{1,3},{3,1},{4,6},{6,4},{5,7},{7,5},{8,10},{10,8},{9,1... | collective-permute-start | bytes 589832 | tf_op jit(solution)/shard_map/ppermute | solution.py:25
  91.2 10.6 %collective-permute-start.2 = (bf16[128,768]{1,0:T(8,128)(2,1)S(1)}, bf16[128,768]{1,0:T(8,128)(2,1)S(1)}, u32[]{:S(2)}, u32[]{:S(2)}) collective-permute-start(bf16[128,768]{1,0:T(8,128)(2,1)S(1)} %collective-permute-done), channel_id=1, source_target_pairs={{0,2},{2,0},{1,3},{3,1},{4,6},{6,4},{5,7},{7,5},{8,10},{10,8},{9,1... | collective-permute-start | bytes 589832 | tf_op jit(solution)/shard_map/ppermute | solution.py:25
  91.7 14.2 %collective-permute-start.3 = (bf16[128,768]{1,0:T(8,128)(2,1)S(1)}, bf16[128,768]{1,0:T(8,128)(2,1)S(1)}, u32[]{:S(2)}, u32[]{:S(2)}) collective-permute-start(bf16[128,768]{1,0:T(8,128)(2,1)S(1)} %collective-permute-done.1), channel_id=1, source_target_pairs={{0,2},{2,0},{1,3},{3,1},{4,6},{6,4},{5,7},{7,5},{8,10},{10,8},{9,1... | collective-permute-start | bytes 589832 | tf_op jit(solution)/shard_map/ppermute | solution.py:25
  97.5 11.1 %collective-permute-start.6 = (bf16[128,768]{1,0:T(8,128)(2,1)S(1)}, bf16[128,768]{1,0:T(8,128)(2,1)S(1)}, u32[]{:S(2)}, u32[]{:S(2)}) collective-permute-start(bf16[128,768]{1,0:T(8,128)(2,1)S(1)} %collective-permute-done.4), channel_id=1, source_target_pairs={{0,2},{2,0},{1,3},{3,1},{4,6},{6,4},{5,7},{7,5},{8,10},{10,8},{9,1... | collective-permute-start | bytes 589832 | tf_op jit(solution)/shard_map/ppermute | solution.py:25
  108.9 2.4 %collective-permute-start.7 = (bf16[4,128,768]{2,1,0:T(8,128)(2,1)S(1)}, bf16[4,128,768]{2,1,0:T(8,128)(2,1)S(1)}, u32[]{:S(2)}, u32[]{:S(2)}) collective-permute-start(bf16[4,128,768]{2,1,0:T(8,128)(2,1)S(1)} %get-tuple-element.34), channel_id=1, source_target_pairs={{0,1},{1,0},{2,3},{3,2},{4,5},{5,4},{6,7},{7,6},{8,9},{9,8},{10,11... | collective-permute-start | bytes 2359304 | tf_op jit(solution)/shard_map/ppermute | solution.py:25
  130.1 23.0 %collective-permute-start.24 = (bf16[320,4096]{1,0:T(8,128)(2,1)S(1)}, bf16[320,4096]{1,0:T(8,128)(2,1)S(1)}, u32[]{:S(2)}, u32[]{:S(2)}) collective-permute-start(bf16[320,4096]{1,0:T(8,128)(2,1)S(1)} %get-tuple-element.20.refs_0_), channel_id=1, source_target_pairs={{0,1},{1,0},{2,3},{3,2},{4,5},{5,4},{6,7},{7,6},{8,9},{9,8},{10,11... | collective-permute-start | bytes 7864328 | tf_op jit(solution)/shard_map/ppermute | solution.py:25
  150.6 19.3 %collective-permute-start.25 = (bf16[320,4096]{1,0:T(8,128)(2,1)}, bf16[320,4096]{1,0:T(8,128)(2,1)S(1)}, u32[]{:S(2)}, u32[]{:S(2)}) collective-permute-start(bf16[320,4096]{1,0:T(8,128)(2,1)} %get-tuple-element.22.refs_1_), channel_id=1, source_target_pairs={{0,1},{1,0},{2,3},{3,2},{4,5},{5,4},{6,7},{7,6},{8,9},{9,8},{10,11... | collective-permute-start | bytes 7864328 | tf_op jit(solution)/shard_map/ppermute | solution.py:25
  150.9 38.2 %collective-permute-start.18 = (bf16[128,1536]{1,0:T(8,128)(2,1)S(1)}, bf16[128,1536]{1,0:T(8,128)(2,1)S(1)}, u32[]{:S(2)}, u32[]{:S(2)}) collective-permute-start(bf16[128,1536]{1,0:T(8,128)(2,1)S(1)} %get-tuple-element.16), channel_id=1, source_target_pairs={{0,1},{1,0},{2,3},{3,2},{4,5},{5,4},{6,7},{7,6},{8,9},{9,8},{10,11... | collective-permute-start | bytes 1179656 | tf_op jit(solution)/shard_map/ppermute | solution.py:25
  151.1 38.6 %collective-permute-start.19 = (bf16[128,1536]{1,0:T(8,128)(2,1)S(1)}, bf16[128,1536]{1,0:T(8,128)(2,1)S(1)}, u32[]{:S(2)}, u32[]{:S(2)}) collective-permute-start(bf16[128,1536]{1,0:T(8,128)(2,1)S(1)} %get-tuple-element.17), channel_id=1, source_target_pairs={{0,3},{1,2},{2,1},{3,0},{4,7},{5,6},{6,5},{7,4},{8,11},{9,10},{10,... | collective-permute-start | bytes 1179656 | tf_op jit(solution)/shard_map/ppermute | solution.py:91
  152.6 37.1 %collective-permute-start.20 = (bf16[128,1536]{1,0:T(8,128)(2,1)S(1)}, bf16[128,1536]{1,0:T(8,128)(2,1)S(1)}, u32[]{:S(2)}, u32[]{:S(2)}) collective-permute-start(bf16[128,1536]{1,0:T(8,128)(2,1)S(1)} %get-tuple-element.19), channel_id=1, source_target_pairs={{0,2},{2,0},{1,3},{3,1},{4,6},{6,4},{5,7},{7,5},{8,10},{10,8},{9,1... | collective-permute-start | bytes 1179656 | tf_op jit(solution)/shard_map/ppermute | solution.py:25
  187.5 6.5 %collective-permute-start.26 = (bf16[128,1536]{1,0:T(8,128)(2,1)S(1)}, bf16[128,1536]{1,0:T(8,128)(2,1)S(1)}, u32[]{:S(2)}, u32[]{:S(2)}) collective-permute-start(bf16[128,1536]{1,0:T(8,128)(2,1)S(1)} %get-tuple-element.24), channel_id=1, source_target_pairs={{0,1},{1,0},{2,3},{3,2},{4,5},{5,4},{6,7},{7,6},{8,9},{9,8},{10,11... | collective-permute-start | bytes 1179656 | tf_op jit(solution)/shard_map/ppermute | solution.py:25
  187.5 11.0 %collective-permute-start.27 = (bf16[128,1536]{1,0:T(8,128)(2,1)S(1)}, bf16[128,1536]{1,0:T(8,128)(2,1)S(1)}, u32[]{:S(2)}, u32[]{:S(2)}) collective-permute-start(bf16[128,1536]{1,0:T(8,128)(2,1)S(1)} %get-tuple-element.25), channel_id=1, source_target_pairs={{0,3},{1,2},{2,1},{3,0},{4,7},{5,6},{6,5},{7,4},{8,11},{9,10},{10,... | collective-permute-start | bytes 1179656 | tf_op jit(solution)/shard_map/ppermute | solution.py:91
  189.1 18.3 %collective-permute-start.28 = (bf16[128,1536]{1,0:T(8,128)(2,1)S(1)}, bf16[128,1536]{1,0:T(8,128)(2,1)S(1)}, u32[]{:S(2)}, u32[]{:S(2)}) collective-permute-start(bf16[128,1536]{1,0:T(8,128)(2,1)S(1)} %get-tuple-element.27), channel_id=1, source_target_pairs={{0,2},{2,0},{1,3},{3,1},{4,6},{6,4},{5,7},{7,5},{8,10},{10,8},{9,1... | collective-permute-start | bytes 1179656 | tf_op jit(solution)/shard_map/ppermute | solution.py:25
  190.0 21.7 %collective-permute-start.22 = (bf16[128,768]{1,0:T(8,128)(2,1)S(1)}, bf16[128,768]{1,0:T(8,128)(2,1)S(1)}, u32[]{:S(2)}, u32[]{:S(2)}) collective-permute-start(bf16[128,768]{1,0:T(8,128)(2,1)S(1)} %get-tuple-element.38), channel_id=1, source_target_pairs={{0,8},{4,12},{8,0},{12,4},{1,9},{5,13},{9,1},{13,5},{2,10},{6,14},... | collective-permute-start | bytes 589832 | tf_op jit(solution)/shard_map/ppermute | solution.py:29
  192.9 19.3 %collective-permute-start.23 = (bf16[128,768]{1,0:T(8,128)(2,1)S(1)}, bf16[128,768]{1,0:T(8,128)(2,1)S(1)}, u32[]{:S(2)}, u32[]{:S(2)}) collective-permute-start(bf16[128,768]{1,0:T(8,128)(2,1)S(1)} %get-tuple-element.39), channel_id=1, source_target_pairs={{0,12},{4,8},{8,4},{12,0},{1,13},{5,9},{9,5},{13,1},{2,14},{6,10},... | collective-permute-start | bytes 589832 | tf_op jit(solution)/shard_map/ppermute | solution.py:29
  193.9 18.3 %collective-permute-start.21 = (bf16[128,768]{1,0:T(8,128)(2,1)S(1)}, bf16[128,768]{1,0:T(8,128)(2,1)S(1)}, u32[]{:S(2)}, u32[]{:S(2)}) collective-permute-start(bf16[128,768]{1,0:T(8,128)(2,1)S(1)} %slice.42), channel_id=1, source_target_pairs={{0,4},{4,0},{8,12},{12,8},{1,5},{5,1},{9,13},{13,9},{2,6},{6,2},{1... | collective-permute-start | bytes 589832 | tf_op jit(solution)/shard_map/ppermute | solution.py:29
  207.7 17.0 %collective-permute-start.30 = (bf16[128,768]{1,0:T(8,128)(2,1)S(1)}, bf16[128,768]{1,0:T(8,128)(2,1)S(1)}, u32[]{:S(2)}, u32[]{:S(2)}) collective-permute-start(bf16[128,768]{1,0:T(8,128)(2,1)S(1)} %get-tuple-element.36), channel_id=1, source_target_pairs={{0,8},{4,12},{8,0},{12,4},{1,9},{5,13},{9,1},{13,5},{2,10},{6,14},... | collective-permute-start | bytes 589832 | tf_op jit(solution)/shard_map/ppermute | solution.py:29
  210.7 14.1 %collective-permute-start.31 = (bf16[128,768]{1,0:T(8,128)(2,1)S(1)}, bf16[128,768]{1,0:T(8,128)(2,1)S(1)}, u32[]{:S(2)}, u32[]{:S(2)}) collective-permute-start(bf16[128,768]{1,0:T(8,128)(2,1)S(1)} %get-tuple-element.37), channel_id=1, source_target_pairs={{0,12},{4,8},{8,4},{12,0},{1,13},{5,9},{9,5},{13,1},{2,14},{6,10},... | collective-permute-start | bytes 589832 | tf_op jit(solution)/shard_map/ppermute | solution.py:29
  211.7 13.6 %collective-permute-start.29 = (bf16[128,768]{1,0:T(8,128)(2,1)S(1)}, bf16[128,768]{1,0:T(8,128)(2,1)S(1)}, u32[]{:S(2)}, u32[]{:S(2)}) collective-permute-start(bf16[128,768]{1,0:T(8,128)(2,1)S(1)} %slice.46), channel_id=1, source_target_pairs={{0,4},{4,0},{8,12},{12,8},{1,5},{5,1},{9,13},{13,9},{2,6},{6,2},{1... | collective-permute-start | bytes 589832 | tf_op jit(solution)/shard_map/ppermute | solution.py:29
  (6 other events, 40.1 us)

commit v2 on v0

v2 whole, which is shorter than its diff:
```python
import functools

import jax
import jax.numpy as jnp
from jax import lax
from jax.experimental import pallas as pl
from jax.experimental.pallas import tpu as pltpu
from jax.sharding import PartitionSpec as P

EXPERTS = 4
CAP = 80
BF16 = jnp.bfloat16
F32 = jnp.float32
VMEM_BYTES = 36 * 1024 * 1024
TILE = 512
DEPTH = 3
COST = 50
FIRST_COST = 1


def swap(value, axis):
    return lax.ppermute(value, axis, [(0, 1), (1, 0)])


def across(value, distance):
    return lax.ppermute(value, "tensor", [(i, i ^ distance) for i in range(lax.axis_size("tensor"))])


def nt(a, b):
    return lax.dot_general(a, b, (((1,), (1,)), ((), ())), preferred_element_type=F32)


class Place:
    def __init__(self):
        self.sources = lax.axis_size("expert")
        self.tensors = lax.axis_size("tensor")
        self.small = self.sources == 2 and self.tensors == 4
        self.expert = lax.axis_index("expert")
        self.sub = lax.axis_index("sub")
        self.tensor = lax.axis_index("tensor")
        self.high = (self.tensor // 2 + self.sub) % 2 == 1
        self.blocks = 2 * self.sources


def other(index, far):
    return index + far - 2 * index * far


def axis_indices():
    return tuple(lax.axis_index(axis) for axis in ("expert", "sub", "tensor"))


def block_at(small, index, place_at):
    if not small:
        return place_at, place_at * CAP
    block = other(index[0], place_at // 2) * 2 + other(index[1], place_at % 2)
    return block, pl.multiple_of(block * CAP, 16)


def far_both(value):
    return lax.ppermute(value, ("expert", "sub"), [(i, 3 - i) for i in range(4)])


def gather_meta(place, meta):
    if place.small:
        return [part[None] for part in (meta, swap(meta, "sub"), swap(meta, "expert"), far_both(meta))]
    return [lax.all_gather(meta, ("expert", "sub"))]


def gather_now(place, rows, after):
    near = [rows] + [across(rows, k) for k in (1, 2, 3)]
    near[3], after = lax.optimization_barrier((near[3], after))
    far = [swap(block, "expert") for block in near]
    low_half = jnp.stack([near[0], near[1], far[0], far[1]])
    high_half = jnp.stack([near[2], near[3], far[2], far[3]])
    keep = jnp.where(place.high, high_half, low_half)
    send = jnp.where(place.high, low_half, high_half)
    return [keep, swap(send, "sub")], [[0, 0, 2, 2], [1, 1, 3, 3]], near[3], after


def gather_first(rows, after):
    rows, _ = lax.optimization_barrier((rows, after))
    return [rows] + [across(rows, k) for k in (1, 2, 3)]


def gather_last(place, near, after):
    *near, _ = lax.optimization_barrier((*near, after))
    low_half, high_half = jnp.stack(near[:2]), jnp.stack(near[2:])
    keep = jnp.where(place.high, high_half, low_half)
    send = jnp.where(place.high, low_half, high_half)
    groups = [keep, swap(send, "sub"), swap(keep, "expert"), far_both(send)]
    return groups, [[0, 0], [1, 1], [2, 2], [3, 3]], [keep, send]


def gather_rows(place, rows):
    count = rows.shape[0]
    whole = lax.all_gather(rows, ("tensor", "expert"))
    whole = whole.reshape(place.tensors, place.sources, count, rows.shape[1])
    whole = whole.transpose(1, 2, 0, 3).reshape(place.sources, count, 2, -1)
    halves = (whole[:, :, 0], whole[:, :, 1])
    first = place.sub == 0
    keep = jnp.where(first, halves[0], halves[1])
    got = swap(jnp.where(first, halves[1], halves[0]), "sub")
    both = jnp.where(first, jnp.stack([keep, got], 1), jnp.stack([got, keep], 1))
    both = both.reshape((2 * place.sources, count, -1))
    return [both], [list(range(2 * place.sources))]


def send_x(place, parts):
    kept, core_near, same_far, core_far = parts
    return kept, swap(core_near, "sub"), swap(same_far, "expert"), far_both(core_far)


def sum_x(place, terms):
    kept, from_core, from_far, from_both = (term.astype(F32) for term in terms)
    own_half, other_half = kept + from_far, from_core + from_both
    return [
        jnp.where(place.high, other_half, own_half).astype(BF16),
        jnp.where(place.high, own_half, other_half).astype(BF16),
    ]


def send_z(near, far, near_next, far_next):
    return near, across(far, 2), across(near_next, 1), across(far_next, 3)


def sum_z(terms):
    return functools.reduce(jnp.add, [term.astype(F32) for term in terms]).astype(BF16)


def scatter_rows(place, parts):
    stacked = jnp.stack(parts)
    count, half = stacked.shape[1:]
    stacked = stacked.reshape(place.sources, 2, count, half)
    first = place.sub == 0
    keep = jnp.where(first, stacked[:, 0], stacked[:, 1])
    got = swap(jnp.where(first, stacked[:, 1], stacked[:, 0]), "sub")
    both = jnp.where(first, jnp.concatenate([keep, got], 2), jnp.concatenate([got, keep], 2))
    both = both.reshape(place.sources, count, place.tensors, -1).transpose(0, 2, 1, 3)
    share = lax.psum_scatter(both, "expert", scatter_dimension=0)
    return lax.psum_scatter(share, "tensor", scatter_dimension=0)


def route_rows(small, locals_, index, metas, take_ref, gate_ref):
    places = [ref.at[i] for ref in metas for i in range(ref.shape[0])]
    rows = places[0].shape[0]
    row, column = (lax.broadcasted_iota(jnp.int32, (rows, rows), axis) for axis in (0, 1))
    before = jnp.where(row < column, 1.0, 0.0).astype(BF16)
    slot = lax.broadcasted_iota(jnp.int32, (CAP, rows), 0).astype(F32)
    for place_at, meta_ref in enumerate(places):
        start = block_at(small, index, place_at)[1]
        meta = jnp.concatenate([meta_ref[...], jnp.zeros((rows, 128 - meta_ref.shape[1]), F32)], axis=1).T
        for local in range(locals_):
            number = (index[0] * locals_ + local).astype(F32)
            one, two = meta[0:1] == number, meta[1:2] == number
            named = jnp.where(one | two, 1.0, 0.0)
            rank = jnp.dot(
                jnp.broadcast_to(named, (16, rows)).astype(BF16), before, preferred_element_type=F32
            )
            take = jnp.where(jnp.where(one | two, rank[0:1], -1.0) == slot, 1.0, 0.0)
            gate = jnp.where(one, meta[2:3], 0.0) + jnp.where(two, meta[3:4], 0.0)
            take_ref[local, place_at] = take.astype(BF16)
            gate_ref[local, pl.ds(start, CAP), :] = jnp.sum(take * gate, axis=1, keepdims=True)


def place_rows(small, index, take_ref, local, groups, places, rows_ref):
    width = groups[0].shape[2]
    seen = {}
    for group, held in zip(groups, places, strict=True):
        for i, place_at in enumerate(held):
            chunk = seen[place_at] = seen.get(place_at, -1) + 1
            start = block_at(small, index, place_at)[1]
            column = pl.multiple_of(other(lax.rem(index[2], 2), chunk) * width, 128) if small else 0
            rows_ref[pl.ds(start, CAP), pl.ds(column, width)] = jnp.dot(
                take_ref[local, place_at], group[i], preferred_element_type=F32
            ).astype(BF16)


def combine_rows(small, index, take_ref, slots_of, outs):
    half, width = slots_of[0].shape[1], outs[0].shape[1]
    chunks = 2 if small else 1
    places = len(outs) * width // half
    for place_at in range(places):
        start = block_at(small, index, place_at)[1]
        for chunk in range(chunks):
            span = half // chunks
            column = pl.multiple_of(other(lax.rem(index[2], 2), chunk) * span, 128) if small else 0
            total = None
            for local, slots in enumerate(slots_of):
                term = lax.dot_general(
                    take_ref[local, place_at], slots[pl.ds(start, CAP), pl.ds(column, span)],
                    (((0,), (0,)), ((), ())), preferred_element_type=F32,
                )
                total = term if total is None else total + term
            if width == half:
                outs[place_at][:, chunk * span : (chunk + 1) * span] = total.astype(BF16)
            else:
                outs[chunk * places + place_at][...] = total.astype(BF16)


class Stream:
    def __init__(self, weights, at, tile, rings, sems):
        self.weights, self.at, self.tile, self.rings, self.sems = weights, at, tile, rings, sems
        self.depth = rings[0].shape[0]

    def copies(self, step):
        slot = lax.rem(step, self.depth)
        cut = pl.ds(pl.multiple_of(step * self.tile, self.tile), self.tile)
        return [
            pltpu.make_async_copy(weight.at[self.at(cut)], ring.at[slot], self.sems.at[i, slot])
            for i, (weight, ring) in enumerate(zip(self.weights, self.rings, strict=True))
        ]

    def start(self, steps):
        for step in range(min(self.depth - 1, steps)):
            for copy in self.copies(step):
                copy.start()

    def take(self, step):
        @pl.when(step + self.depth - 1 < pl.num_programs(0))
        def _():
            for copy in self.copies(step + self.depth - 1):
                copy.start()

        for copy in self.copies(step):
            copy.wait()
        return [ring.at[lax.rem(step, self.depth)] for ring in self.rings]


def first_body(small, local, locals_, places, n_routes, n_after, tile, steps, *refs):
    routes, refs = refs[:n_routes], refs[n_routes + n_after :]
    groups, (gate_w, up_w, out, *routed, rows, gate_ring, up_ring, sems) = refs[: len(places)], refs[len(places) :]
    take_ref = routes[0] if local else routed[0]
    stream = Stream([gate_w, up_w], lambda cut: (local, slice(None), cut), tile, [gate_ring, up_ring], sems)
    step = pl.program_id(0)

    @pl.when(step == 0)
    def _():
        stream.start(steps)
        if not local:
            route_rows(small, locals_, axis_indices(), routes, *routed)
        place_rows(small, axis_indices(), take_ref, local, groups, places, rows)

    for i, weight in enumerate(stream.take(step)):
        out[i] = jnp.dot(rows[...], weight[...], preferred_element_type=F32).astype(BF16)


def middle_body(small, local, locals_, places, tile, steps, take_ref, gate_ref, *refs):
    groups, refs = refs[: len(places)], refs[len(places) :]
    last = local == locals_ - 1
    before, refs = (refs[:local], refs[local:]) if last else ((), refs)
    own, got, down, slopes, back, *outs, rows, total, slots, ring, sems = refs
    stream = Stream([down], lambda cut: (local, cut), tile, [ring], sems)
    step = pl.program_id(0)

    @pl.when(step == 0)
    def _():
        stream.start(steps)
        place_rows(small, axis_indices(), take_ref, local, groups, places, rows)
        total[...] = jnp.zeros_like(total)

    (weight,) = stream.take(step)
    back[...] = nt(rows[...], weight[...]).astype(BF16)
    gate_pre = own[0].astype(F32) + got[0].astype(F32)
    up_pre = own[1].astype(F32) + got[1].astype(F32)
    sigmoid = 0.5 * jnp.tanh(0.5 * gate_pre) + 0.5
    silu = gate_pre * sigmoid
    hidden = (silu * up_pre).astype(BF16)
    slopes[0] = silu.astype(BF16)
    slopes[1] = (up_pre * (sigmoid + silu * (1.0 - sigmoid))).astype(BF16)
    total[...] += jnp.dot(hidden, weight[...], preferred_element_type=F32)

    @pl.when(step == pl.num_programs(0) - 1)
    def _():
        finish(small, last, take_ref, gate_ref[local], before, total, slots, outs)


def last_body(small, local, locals_, n_after, tile, steps, take_ref, gate_ref, *refs):
    refs = refs[n_after:]
    last = local == locals_ - 1
    before, refs = (refs[:local], refs[local:]) if last else ((), refs)
    own, got, slopes, gate_w, up_w, *outs, total, slots, gate_ring, up_ring, sems = refs
    stream = Stream([gate_w, up_w], lambda cut: (local, slice(None), cut), tile, [gate_ring, up_ring], sems)
    step = pl.program_id(0)

    @pl.when(step == 0)
    def _():
        stream.start(steps)
        total[...] = jnp.zeros_like(total)

    gate_tile, up_tile = stream.take(step)
    back = own[...].astype(F32) + got[...].astype(F32)
    up_grad = (back * slopes[0].astype(F32)).astype(BF16)
    gate_grad = (back * slopes[1].astype(F32)).astype(BF16)
    total[...] += nt(gate_grad, gate_tile[...]) + nt(up_grad, up_tile[...])

    @pl.when(step == pl.num_programs(0) - 1)
    def _():
        finish(small, last, take_ref, gate_ref[local], before, total, slots, outs)


def finish(small, last, take_ref, gate, before, total, slots, outs):
    weighted = (total[...] * gate).astype(BF16)
    if last:
        slots[...] = weighted
        combine_rows(small, axis_indices(), take_ref, [*before, slots], outs)
    else:
        outs[0][...] = weighted


def whole(array):
    dims = len(array.shape)
    return pl.BlockSpec(array.shape, lambda f: (0,) * dims)


def call(body, steps, routes, after, near, near_specs, weights, outs, out_specs, scratch, flops):
    anywhere = pl.BlockSpec(memory_space=pl.ANY)
    return pl.pallas_call(
        body,
        grid=(steps,),
        in_specs=[*map(whole, routes), *[anywhere] * len(after), *near_specs,
                  *[anywhere] * len(weights)],
        out_specs=out_specs,
        out_shape=outs,
        scratch_shapes=scratch,
        compiler_params=pltpu.CompilerParams(vmem_limit_bytes=VMEM_BYTES),
        cost_estimate=pl.CostEstimate(flops=flops, bytes_accessed=0, transcendentals=0),
    )(*routes, *after, *near, *weights)


def per_device(tokens, cotangent, expert_ids, gate_values, w_gate, w_up, w_down):
    place = Place()
    small, blocks = place.small, place.blocks
    locals_, half, hidden = w_gate.shape
    count = tokens.shape[0]
    slots = blocks * CAP
    flops = 2 * slots * half * hidden

    ids = jnp.pad(expert_ids.astype(F32), ((0, 0), (0, gate_values.shape[1])))
    metas = gather_meta(place, ids + jnp.pad(gate_values, ((0, 0), (expert_ids.shape[1], 0))))
    routed = [jax.ShapeDtypeStruct((locals_, blocks, CAP, count), BF16),
              jax.ShapeDtypeStruct((locals_, slots, 1), F32)]

    if small:
        token_groups, token_places, token_last, metas = gather_now(place, tokens, metas)
        grad_near = gather_first(cotangent, token_last)
    else:
        token_groups, token_places = gather_rows(place, tokens)
        grad_groups, grad_places = gather_rows(place, cotangent)

    tile = min(TILE, hidden)
    steps = hidden // tile
    pair = pltpu.HBM((2, slots, hidden), BF16)
    one = pltpu.HBM((slots, hidden), BF16)
    pair_spec = pl.BlockSpec((2, slots, tile), lambda f: (0, 0, f))
    one_spec = pl.BlockSpec((slots, tile), lambda f: (0, f))
    two_sems, one_sem = pltpu.SemaphoreType.DMA((2, DEPTH)), pltpu.SemaphoreType.DMA((1, DEPTH))

    def ends(local, width):
        return [jax.ShapeDtypeStruct((count, width), BF16)] * (blocks * half // width) if local == locals_ - 1 else [
            jax.ShapeDtypeStruct((slots, width), BF16)]

    own_pre, got_pre, after = [], [], []
    for local in range(locals_):
        ring = pltpu.VMEM((DEPTH, half, tile), BF16)
        routes, new = ([take], []) if local else (metas, routed)
        own, *new = call(
            functools.partial(first_body, small, local, locals_, token_places, len(routes), len(after), tile, steps),
            steps, routes, after, token_groups, [*map(whole, token_groups)], [w_gate, w_up],
            [pair, *new], [pair_spec, *map(whole, new)], [pltpu.VMEM((slots, half), BF16), ring, ring, two_sems],
            (COST if local else FIRST_COST) * flops,
        )
        if not local:
            take, gate = new
        own_pre.append(own)
        got_pre.append(swap(own, "sub"))
        if small and local == 0:
            grad_groups, grad_places, after = gather_last(place, grad_near, own)

    done, own_back, got_back, slopes = [], [], [], []
    for local in range(locals_):
        before = done if local == locals_ - 1 else []
        outs = ends(local, half)
        slope, back, *mixed_parts = call(
            functools.partial(middle_body, small, local, locals_, grad_places, tile, steps),
            steps, [take, gate], [], [*grad_groups, *before, own_pre[local], got_pre[local]],
            [*map(whole, [*grad_groups, *before]), pair_spec, pair_spec], [w_down],
            [pair, one, *outs], [pair_spec, one_spec, *map(whole, outs)],
            [pltpu.VMEM((slots, half), BF16), pltpu.VMEM((slots, half), F32), pltpu.VMEM((slots, half), BF16),
             pltpu.VMEM((DEPTH, tile, half), BF16), one_sem],
            COST * flops,
        )
        slopes.append(slope)
        own_back.append(back)
        got_back.append(swap(back, "sub"))
        done.append(mixed_parts[0])

    ring = pltpu.VMEM((DEPTH, half, tile), BF16)
    done, after = [], []
    mixed_terms = send_x(place, mixed_parts) if small else []
    for local in range(locals_):
        last = local == locals_ - 1
        before = done if last else []
        outs = ends(local, half // 2 if small and last else half)
        grad_parts = call(
            functools.partial(last_body, small, local, locals_, len(after), tile, steps),
            steps, [take, gate], after, [*before, own_back[local], got_back[local], slopes[local]],
            [*map(whole, before), one_spec, one_spec, pair_spec], [w_gate, w_up],
            outs, [*map(whole, outs)],
            [pltpu.VMEM((slots, half), F32), pltpu.VMEM((slots, half), BF16), ring, ring, two_sems],
            COST * flops,
        )
        done.append(grad_parts[0])
        if small and local == 0:
            *terms, _ = lax.optimization_barrier((*mixed_terms, grad_parts[0]))
            terms = [[term[:, i * half // 2 : (i + 1) * half // 2] for term in terms] for i in range(2)]
            after = [*sum_x(place, terms[0]), *sum_x(place, terms[1])]
            mixed_terms = send_z(*after)
    if not small:
        return scatter_rows(place, mixed_parts), scatter_rows(place, grad_parts)
    *mixed_terms, grad_parts = lax.optimization_barrier((*mixed_terms, grad_parts))
    next_terms = send_x(place, grad_parts[blocks:])
    last_terms = send_x(place, grad_parts[:blocks])
    return sum_z(mixed_terms), sum_z(send_z(*sum_x(place, last_terms), *sum_x(place, next_terms)))


def solution(mesh):
    rows = P(("groups", "expert", "sub"), "tensor")
    ids = P(("groups", "expert", "sub"), None)
    return jax.shard_map(
        per_device,
        mesh=mesh,
        in_specs=(rows, rows, ids, ids, P("expert", "sub", "tensor"), P("expert", "sub", "tensor"),
                  P("expert", "tensor", "sub")),
        out_specs=(rows, rows),
        check_vma=False,
    )
```

time: 428 us -> 185 us (0.43)
  matrix products: 166 us -> 0 us
  waiting for transfers between devices: 177 us -> 41.4 us
  Pallas kernels: 0 us -> 89.3 us
  blocking collectives: 39 us -> 0 us
  starting transfers between devices: 16.2 us -> 41.6 us
  between operations: 14 us -> 0.89 us
  local copies, waits for them, and re-layouts: 10.7 us -> 3.41 us
    dot_general x8 -> x0, matrix products: 166 us -> none  [the longest x1 30.3 us: per_device(): jnp.einsum('secd,edf->secf', inputs, full_up, preferred_element_type=jnp....]
    all_gather x3 -> x0, waiting for transfers between devices: 110 us -> none  [the longest x1 47.9 us: per_device(): lax.all_gather(w_down, 'sub', axis=2, tiled=True)]
    pallas_call x0 -> x6, Pallas kernels: none -> 89.3 us  [call(): pl.pallas_call(body, grid=(steps,), in_specs=[*map(whole, routes), *[anyw...]
    reduce_scatter x2 -> x0, waiting for transfers between devices: 58.7 us -> none  [the longest x1 39.3 us: per_device(): lax.psum_scatter(out_terms.astype(jnp.bfloat16), 'tensor', scatter_dimens...]
    ppermute x0 -> x36, starting transfers between devices: none -> 41.6 us  [the longest x12 23.9 us: across(): lax.ppermute(value, 'tensor', [(i, i ^ distance) for i in range(lax.axis_...]
    ppermute x0 -> x36, waiting for transfers between devices: none -> 41.4 us  [the longest x19 24.6 us: swap(): return lax.ppermute(value, axis, [(0, 1), (1, 0)])]
    all_gather x2 -> x0, blocking collectives: 39 us -> none  [the longest x1 21.3 us: per_device(): lax.all_gather(tokens, 'tensor', axis=1, tiled=True)]
    all_to_all x4 -> x0, starting transfers between devices: 15.8 us -> none  [the longest x1 4.75 us: per_device(): lax.all_to_all(dispatch(whole_grads), 'expert', split_axis=0, concat_axis...]
  transfers between devices with their start and end apart: 9 -> 36, of which waited for: 6 -> 14; matrix products, arithmetic and copies ran while one was open for 23% -> 4% of each run, Pallas kernels for 0% -> 48%
where the time goes in v2:
time: 185 us
  Pallas kernels  89.3 us (48%)
  starting transfers between devices  41.6 us (22%)
  waiting for transfers between devices  41.4 us (22%)
  other arithmetic  8.21 us (4%)
  local copies, waits for them, and re-layouts  3.41 us (2%)
    pallas_call x6, Pallas kernels, call(): pl.pallas_call(body, grid=(steps,), in_specs=[*map(whole, routes), *[anyw...  89.3 us
    ppermute x19, waiting for transfers between devices, swap(): return lax.ppermute(value, axis, [(0, 1), (1, 0)])  24.6 us
    ppermute x12, starting transfers between devices, across(): lax.ppermute(value, 'tensor', [(i, i ^ distance) for i in range(lax.axis_...  23.9 us
    ppermute x12, waiting for transfers between devices, across(): lax.ppermute(value, 'tensor', [(i, i ^ distance) for i in range(lax.axis_...  13.8 us
    ppermute x19, starting transfers between devices, swap(): return lax.ppermute(value, axis, [(0, 1), (1, 0)])  12 us
    ppermute x5, starting transfers between devices, far_both(): lax.ppermute(value, ('expert', 'sub'), [(i, 3 - i) for i in range(4)])  5.75 us
  transfers between devices with their start and end apart: 36, of which 14 were waited for; matrix products, arithmetic and copies ran while one was open for 4% of the time, Pallas kernels for 48%

profile of v2, /device:TPU:0, one launch (start us, length us, event | category | flops | bytes accessed | tf_op | source)
XLA Modules:
  0.0 184.8 jit_solution(3215877517995026403)
XLA Ops:
  0.6 5.1 %collective-permute-start = (bf16[128,768]{1,0:T(8,128)(2,1)}, bf16[128,768]{1,0:T(8,128)(2,1)S(1)}, u32[]{:S(2)}, u32[]{:S(2)}) collective-permute-start(bf16[128,768]{1,0:T(8,128)(2,1)} %param.7), channel_id=1, source_target_pairs={{0,12},{4,8},{8,4},{12,0},{1,13},{5,9},{9,5},{13,1},{2,14},{6,10},... | collective-permute-start | bytes 589832 | tf_op jit(solution)/shard_map/ppermute | solution.py:26
  8.1 1.7 collective-permute-start.2
  10.9 1.8 collective-permute-done.2
  12.6 2.0 %collective-permute-start.8 = (bf16[128,768]{1,0:T(8,128)(2,1)}, bf16[128,768]{1,0:T(8,128)(2,1)S(1)}, u32[]{:S(2)}, u32[]{:S(2)}) collective-permute-start(bf16[128,768]{1,0:T(8,128)(2,1)} %param.7), channel_id=1, source_target_pairs={{0,2},{2,0},{1,3},{3,1},{4,6},{6,4},{5,7},{7,5},{8,10},{10,8},{9,1... | collective-permute-start | bytes 589832 | tf_op jit(solution)/shard_map/ppermute | solution.py:22
  17.6 5.1 %collective-permute-done.4 = bf16[128,768]{1,0:T(8,128)(2,1)S(1)} collective-permute-done((bf16[128,768]{1,0:T(8,128)(2,1)}, bf16[128,768]{1,0:T(8,128)(2,1)S(1)}, u32[]{:S(2)}, u32[]{:S(2)}) %collective-permute-start.4) | collective-permute-done | bytes 196640 | tf_op jit(solution)/shard_map/ppermute | solution.py:26
  22.6 1.5 collective-permute-start.5
  24.9 4.2 %collective-permute-done.9 = bf16[128,768]{1,0:T(8,128)(2,1)S(1)} collective-permute-done((bf16[128,768]{1,0:T(8,128)(2,1)S(1)}, bf16[128,768]{1,0:T(8,128)(2,1)S(1)}, u32[]{:S(2)}, u32[]{:S(2)}) %collective-permute-start.9) | collective-permute-done | bytes 196640 | tf_op jit(solution)/shard_map/ppermute | solution.py:22
  29.1 2.9 %collective-permute-done.5 = bf16[128,768]{1,0:T(8,128)(2,1)S(1)} collective-permute-done((bf16[128,768]{1,0:T(8,128)(2,1)S(1)}, bf16[128,768]{1,0:T(8,128)(2,1)S(1)}, u32[]{:S(2)}, u32[]{:S(2)}) %collective-permute-start.5) | collective-permute-done | bytes 196640 | tf_op jit(solution)/shard_map/ppermute | solution.py:22
  34.6 2.9 %collective-permute-start.12 = (bf16[128,768]{1,0:T(8,128)(2,1)}, bf16[128,768]{1,0:T(8,128)(2,1)S(1)}, u32[]{:S(2)}, u32[]{:S(2)}) collective-permute-start(bf16[128,768]{1,0:T(8,128)(2,1)} %param.8), channel_id=1, source_target_pairs={{0,8},{4,12},{8,0},{12,4},{1,9},{5,13},{9,1},{13,5},{2,10},{6,14},... | collective-permute-start | bytes 589832 | tf_op jit(solution)/shard_map/ppermute | solution.py:26
  37.6 12.9 %shard_map.86 = (bf16[2,320,4096]{2,1,0:T(8,128)(2,1)}, bf16[2,4,80,128]{3,2,1,0:T(8,128)(2,1)S(1)}, f32[2,320,1]{2,1,0:T(8,128)S(1)}) custom-call(f32[1,128,4]{2,1,0:T(8,128)S(1)} %fusion.refs_0_, f32[1,128,4]{2,1,0:T(8,128)S(1)} %bitcast.17, f32[1,128,4]{2,1,0:T(8,128)S(1)} %bitcast.18, f32[1,128,4]{2,1,0:T(8,128)S(1)} %bitcast.19, ...), custom_call_target="tpu_custom_call" | custom-call | flops 4026531840 | tf_op jit(solution)/shard_map/pallas_call | solution.py:318
  52.9 1.6 collective-permute-start.16
  55.1 12.8 %shard_map.88.refs_5_ = bf16[2,320,4096]{2,1,0:T(8,128)(2,1)} custom-call(bf16[2,4,80,128]{3,2,1,0:T(8,128)(2,1)S(1)} %get-tuple-element.53.take_ref.refs_0_, bf16[2,128,768]{2,1,0:T(8,128)(2,1)} %get-tuple-element.103.refs_0_.refs_1_, bf16[2,128,768]{2,1,0:T(8,128)(2,1)} %get-tuple-element.102.refs_2_, ...), custom_call_target="tpu_custom_call" | custom-call | flops 201326592000 | tf_op jit(solution)/shard_map/pallas_call | solution.py:318
  67.9 5.2 %collective-permute-done.15.refs_2_ = bf16[2,128,768]{2,1,0:T(8,128)(2,1)} collective-permute-done((bf16[2,128,768]{2,1,0:T(8,128)(2,1)}, bf16[2,128,768]{2,1,0:T(8,128)(2,1)}, u32[]{:S(2)}, u32[]{:S(2)}) %collective-permute-start.15) | collective-permute-done | bytes 393248 | tf_op jit(solution)/shard_map/ppermute | solution.py:22
  73.1 16.5 %shard_map.87 = (bf16[2,320,4096]{2,1,0:T(8,128)(2,1)}, bf16[320,4096]{1,0:T(8,128)(2,1)}, bf16[320,1536]{1,0:T(8,128)(2,1)S(1)}) custom-call(bf16[2,4,80,128]{3,2,1,0:T(8,128)(2,1)S(1)} %get-tuple-element.53.take_ref.refs_0_, f32[2,320,1]{2,1,0:T(8,128)S(1)} %get-tuple-element.54.gate_ref, bf16[2,128,768]{2,1,0:T(8,128)(2,1)} %get-tuple-element.103.refs_0_.refs_1_, ...), custom_call_target="tpu_custom_call" | custom-call | flops 201326592000 | tf_op jit(solution)/shard_map/pallas_call | solution.py:318
  89.8 17.8 %shard_map.89 = (bf16[2,320,4096]{2,1,0:T(8,128)(2,1)}, bf16[320,4096]{1,0:T(8,128)(2,1)}, bf16[128,1536]{1,0:T(8,128)(2,1)S(1)}, bf16[128,1536]{1,0:T(8,128)(2,...) custom-call(bf16[2,4,80,128]{3,2,1,0:T(8,128)(2,1)S(1)} %get-tuple-element.53.take_ref.refs_0_, ...), custom_call_target="tpu_custom_call" | custom-call | flops 201326592000 | tf_op jit(solution)/shard_map/pallas_call | solution.py:318
  108.1 1.5 collective-permute-start.20
  110.3 2.5 %copy-done.5 = bf16[2,320,4096]{2,1,0:T(8,128)(2,1)S(1)} copy-done((bf16[2,320,4096]{2,1,0:T(8,128)(2,1)S(1)}, bf16[2,320,4096]{2,1,0:T(8,128)(2,1)}, u32[]{:S(2)}) %copy-start.5) | copy-done | bytes 5242904
  112.8 14.5 %shard_map.90.refs_4_ = bf16[320,1536]{1,0:T(8,128)(2,1)S(1)} custom-call(bf16[2,4,80,128]{3,2,1,0:T(8,128)(2,1)S(1)} %get-tuple-element.53.take_ref.refs_0_, f32[2,320,1]{2,1,0:T(8,128)S(1)} %get-tuple-element.54.gate_ref, bf16[320,4096]{1,0:T(8,128)(2,1)S(1)} %copy-done.3, bf16[320,4096]{1,0:T(8,128)(2,1)} %collective-permute-done.22.refs_1_, ...), custom_call_target="tpu_custom_call" | custom-call | flops 201326592000 | tf_op jit(solution)/shard_map/pallas_call | solution.py:318
  127.3 2.3 %select_convert_fusion.4 = (bf16[128,768]{1,0:T(8,128)(2,1)}, bf16[128,768]{1,0:T(8,128)(2,1)}, bf16[128,768]{1,0:T(8,128)(2,1)}, bf16[128,768]{1,0:T(8,128)(2,1)S(1)}) fusion(pred[]{:T(512)S(6)} %eq.5, bf16[128,1536]{1,0:T(8,128)(2,1)} %collective-permute-done.20, bf16[128,1536]{1,0:T(8,128)(2,1)S(1)} %get-tuple-element.70, ...), kind=kLoop, calls=%fused_computation.16 | loop fusion | flops 1966080 | bytes 2359297 | tf_op jit(solution)/shard_map/convert_element_type | solution.py:119
  129.6 5.2 %collective-permute-start.23 = (bf16[128,768]{1,0:T(8,128)(2,1)}, bf16[128,768]{1,0:T(8,128)(2,1)}, u32[]{:S(2)}, u32[]{:S(2)}) collective-permute-start(bf16[128,768]{1,0:T(8,128)(2,1)} %get-tuple-element.95.refs_1_), channel_id=1, source_target_pairs={{0,8},{4,12},{8,0},{12,4},{1,9},{5,13},{9,1},{13,5},{2,10},{6,14},... | collective-permute-start | bytes 589832 | tf_op jit(solution)/shard_map/ppermute | solution.py:26
  134.8 1.5 collective-permute-start.25
  136.3 14.8 %shard_map.91 = (bf16[128,768]{1,0:T(8,128)(2,1)S(1)}, bf16[128,768]{1,0:T(8,128)(2,1)S(1)}, bf16[128,768]{1,0:T(8,128)(2,1)S(1)}, bf16[128,768]{1,0:T(8,128)(2,...) custom-call(bf16[2,4,80,128]{3,2,1,0:T(8,128)(2,1)S(1)} %get-tuple-e, ...), custom_call_target="tpu_custom_call" | custom-call | flops 201326592000 | tf_op jit(solution)/shard_map/pallas_call | solution.py:318
  151.2 1.6 collective-permute-start.28
  153.4 1.6 collective-permute-start.32
  155.5 2.6 %collective-permute-done.28 = bf16[128,768]{1,0:T(8,128)(2,1)S(1)} collective-permute-done((bf16[128,768]{1,0:T(8,128)(2,1)S(1)}, bf16[128,768]{1,0:T(8,128)(2,1)S(1)}, u32[]{:S(2)}, u32[]{:S(2)}) %collective-permute-start.28) | collective-permute-done | bytes 196640 | tf_op jit(solution)/shard_map/ppermute | solution.py:61
  158.1 5.2 %collective-permute-done.29 = bf16[128,768]{1,0:T(8,128)(2,1)S(1)} collective-permute-done((bf16[128,768]{1,0:T(8,128)(2,1)S(1)}, bf16[128,768]{1,0:T(8,128)(2,1)S(1)}, u32[]{:S(2)}, u32[]{:S(2)}) %collective-permute-start.29) | collective-permute-done | bytes 196640 | tf_op jit(solution)/shard_map/ppermute | solution.py:22
  163.4 2.8 %collective-permute-start.30 = (bf16[128,768]{1,0:T(8,128)(2,1)S(1)}, bf16[128,768]{1,0:T(8,128)(2,1)S(1)}, u32[]{:S(2)}, u32[]{:S(2)}) collective-permute-start(bf16[128,768]{1,0:T(8,128)(2,1)S(1)} %select_convert_fusion.2), channel_id=1, source_target_pairs={{0,8},{4,12},{8,0},{12,4},{1,9},{5,13},{9,1},{13,5},{2,10},{6,14},... | collective-permute-start | bytes 589832 | tf_op jit(solution)/shard_map/ppermute | solution.py:26
  166.5 4.6 %collective-permute-done.33 = bf16[128,768]{1,0:T(8,128)(2,1)S(1)} collective-permute-done((bf16[128,768]{1,0:T(8,128)(2,1)S(1)}, bf16[128,768]{1,0:T(8,128)(2,1)S(1)}, u32[]{:S(2)}, u32[]{:S(2)}) %collective-permute-start.33) | collective-permute-done | bytes 196640 | tf_op jit(solution)/shard_map/ppermute | solution.py:22
  171.2 2.7 %collective-permute-start.34 = (bf16[128,768]{1,0:T(8,128)(2,1)S(1)}, bf16[128,768]{1,0:T(8,128)(2,1)S(1)}, u32[]{:S(2)}, u32[]{:S(2)}) collective-permute-start(bf16[128,768]{1,0:T(8,128)(2,1)S(1)} %get-tuple-element.100), channel_id=1, source_target_pairs={{0,4},{4,0},{8,12},{12,8},{1,5},{5,1},{9,13},{13,9},{2,6},{6,2},{1... | collective-permute-start | bytes 589832 | tf_op jit(solution)/shard_map/ppermute | solution.py:26
  175.4 1.9 %add_convert_fusion.1 = bf16[128,768]{1,0:T(8,128)(2,1)} fusion(bf16[128,768]{1,0:T(8,128)(2,1)} %collective-permute-done.25, bf16[128,768]{1,0:T(8,128)(2,1)} %collective-permute-done.24, bf16[128,768]{1,0:T(8,128)(2,1)} %collective-permute-done.23, bf16[128,768]{1,0:T(8,128)(2,1)S(1)} %get-tuple-element.82.refs_0_), kind=kLoop, calls=%fused_computation.15 | loop fusion | flops 786432 | bytes 983040 | tf_op jit(solution)/shard_map/convert_element_type | solution.py:128
  177.3 2.0 %collective-permute-done.34 = bf16[128,768]{1,0:T(8,128)(2,1)S(1)} collective-permute-done((bf16[128,768]{1,0:T(8,128)(2,1)S(1)}, bf16[128,768]{1,0:T(8,128)(2,1)S(1)}, u32[]{:S(2)}, u32[]{:S(2)}) %collective-permute-start.34) | collective-permute-done | bytes 196640 | tf_op jit(solution)/shard_map/ppermute | solution.py:26
  179.3 4.6 %collective-permute-done.35 = bf16[128,768]{1,0:T(8,128)(2,1)S(1)} collective-permute-done((bf16[128,768]{1,0:T(8,128)(2,1)S(1)}, bf16[128,768]{1,0:T(8,128)(2,1)S(1)}, u32[]{:S(2)}, u32[]{:S(2)}) %collective-permute-start.35) | collective-permute-done | bytes 196640 | tf_op jit(solution)/shard_map/ppermute | solution.py:26
  (72 shorter events, 18.1 us)
Async XLA Ops:
  0.6 14.0 %collective-permute-start = (bf16[128,768]{1,0:T(8,128)(2,1)}, bf16[128,768]{1,0:T(8,128)(2,1)S(1)}, u32[]{:S(2)}, u32[]{:S(2)}) collective-permute-start(bf16[128,768]{1,0:T(8,128)(2,1)} %param.7), channel_id=1, source_target_pairs={{0,12},{4,8},{8,4},{12,0},{1,13},{5,9},{9,5},{13,1},{2,14},{6,10},... | collective-permute-start | bytes 589832 | tf_op jit(solution)/shard_map/ppermute | solution.py:26
  5.7 10.4 %collective-permute-start.7 = (bf16[128,768]{1,0:T(8,128)(2,1)}, bf16[128,768]{1,0:T(8,128)(2,1)S(1)}, u32[]{:S(2)}, u32[]{:S(2)}) collective-permute-start(bf16[128,768]{1,0:T(8,128)(2,1)} %param.7), channel_id=1, source_target_pairs={{0,4},{4,0},{8,12},{12,8},{1,5},{5,1},{9,13},{13,9},{2,6},{6,2},{1... | collective-permute-start | bytes 589832 | tf_op jit(solution)/shard_map/ppermute | solution.py:26
  5.7 16.9 %collective-permute-start.4 = (bf16[128,768]{1,0:T(8,128)(2,1)}, bf16[128,768]{1,0:T(8,128)(2,1)S(1)}, u32[]{:S(2)}, u32[]{:S(2)}) collective-permute-start(bf16[128,768]{1,0:T(8,128)(2,1)} %param.7), channel_id=1, source_target_pairs={{0,8},{4,12},{8,0},{12,4},{1,9},{5,13},{9,1},{13,5},{2,10},{6,14},... | collective-permute-start | bytes 589832 | tf_op jit(solution)/shard_map/ppermute | solution.py:26
  9.8 4.8 %collective-permute-start.3 = (f32[128,4]{1,0:T(8,128)S(1)}, f32[128,4]{1,0:T(8,128)S(1)}, u32[]{:S(2)}, u32[]{:S(2)}) collective-permute-start(f32[128,4]{1,0:T(8,128)S(1)} %pad_add_fusion), channel_id=1, source_target_pairs={{0,3},{1,2},{2,1},{3,0},{4,7},{5,6},{6,5},{7,4},{8,11},{9,10},{10,... | collective-permute-start | bytes 6152 | tf_op jit(solution)/shard_map/ppermute | solution.py:61
  12.6 11.5 %collective-permute-start.8 = (bf16[128,768]{1,0:T(8,128)(2,1)}, bf16[128,768]{1,0:T(8,128)(2,1)S(1)}, u32[]{:S(2)}, u32[]{:S(2)}) collective-permute-start(bf16[128,768]{1,0:T(8,128)(2,1)} %param.7), channel_id=1, source_target_pairs={{0,2},{2,0},{1,3},{3,1},{4,6},{6,4},{5,7},{7,5},{8,10},{10,8},{9,1... | collective-permute-start | bytes 589832 | tf_op jit(solution)/shard_map/ppermute | solution.py:22
  14.6 10.3 %collective-permute-start.6 = (bf16[128,768]{1,0:T(8,128)(2,1)S(1)}, bf16[128,768]{1,0:T(8,128)(2,1)S(1)}, u32[]{:S(2)}, u32[]{:S(2)}) collective-permute-start(bf16[128,768]{1,0:T(8,128)(2,1)S(1)} %collective-permute-done), channel_id=1, source_target_pairs={{0,2},{2,0},{1,3},{3,1},{4,6},{6,4},{5,7},{7,5},{8,10},{10,8},{9,1... | collective-permute-start | bytes 589832 | tf_op jit(solution)/shard_map/ppermute | solution.py:22
  16.2 12.9 %collective-permute-start.9 = (bf16[128,768]{1,0:T(8,128)(2,1)S(1)}, bf16[128,768]{1,0:T(8,128)(2,1)S(1)}, u32[]{:S(2)}, u32[]{:S(2)}) collective-permute-start(bf16[128,768]{1,0:T(8,128)(2,1)S(1)} %collective-permute-done.7), channel_id=1, source_target_pairs={{0,2},{2,0},{1,3},{3,1},{4,6},{6,4},{5,7},{7,5},{8,10},{10,8},{9,1... | collective-permute-start | bytes 589832 | tf_op jit(solution)/shard_map/ppermute | solution.py:22
  22.6 9.3 %collective-permute-start.5 = (bf16[128,768]{1,0:T(8,128)(2,1)S(1)}, bf16[128,768]{1,0:T(8,128)(2,1)S(1)}, u32[]{:S(2)}, u32[]{:S(2)}) collective-permute-start(bf16[128,768]{1,0:T(8,128)(2,1)S(1)} %collective-permute-done.4), channel_id=1, source_target_pairs={{0,2},{2,0},{1,3},{3,1},{4,6},{6,4},{5,7},{7,5},{8,10},{10,8},{9,1... | collective-permute-start | bytes 589832 | tf_op jit(solution)/shard_map/ppermute | solution.py:22
  33.2 17.5 %collective-permute-start.11 = (bf16[128,768]{1,0:T(8,128)(2,1)}, bf16[128,768]{1,0:T(8,128)(2,1)S(1)}, u32[]{:S(2)}, u32[]{:S(2)}) collective-permute-start(bf16[128,768]{1,0:T(8,128)(2,1)} %param.8), channel_id=1, source_target_pairs={{0,4},{4,0},{8,12},{12,8},{1,5},{5,1},{9,13},{13,9},{2,6},{6,2},{1... | collective-permute-start | bytes 589832 | tf_op jit(solution)/shard_map/ppermute | solution.py:26
  34.6 17.3 %collective-permute-start.12 = (bf16[128,768]{1,0:T(8,128)(2,1)}, bf16[128,768]{1,0:T(8,128)(2,1)S(1)}, u32[]{:S(2)}, u32[]{:S(2)}) collective-permute-start(bf16[128,768]{1,0:T(8,128)(2,1)} %param.8), channel_id=1, source_target_pairs={{0,8},{4,12},{8,0},{12,4},{1,9},{5,13},{9,1},{13,5},{2,10},{6,14},... | collective-permute-start | bytes 589832 | tf_op jit(solution)/shard_map/ppermute | solution.py:26
  37.6 14.4 %collective-permute-start.13 = (bf16[128,768]{1,0:T(8,128)(2,1)}, bf16[128,768]{1,0:T(8,128)(2,1)S(1)}, u32[]{:S(2)}, u32[]{:S(2)}) collective-permute-start(bf16[128,768]{1,0:T(8,128)(2,1)} %param.8), channel_id=1, source_target_pairs={{0,12},{4,8},{8,4},{12,0},{1,13},{5,9},{9,5},{13,1},{2,14},{6,10},... | collective-permute-start | bytes 589832 | tf_op jit(solution)/shard_map/ppermute | solution.py:26
  50.6 22.5 %collective-permute-start.17 = (bf16[2,320,4096]{2,1,0:T(8,128)(2,1)}, bf16[2,320,4096]{2,1,0:T(8,128)(2,1)}, u32[]{:S(2)}, u32[]{:S(2)}) collective-permute-start(bf16[2,320,4096]{2,1,0:T(8,128)(2,1)} %get-tuple-element.56.refs_4_), channel_id=1, source_target_pairs={{0,1},{1,0},{2,3},{3,2},{4,5},{5,4},{6,7},{7,6},{8,9},{9,8},{10,11... | collective-permute-start | bytes 15728648 | tf_op jit(solution)/shard_map/ppermute | solution.py:22
  52.9 15.0 %collective-permute-start.14 = (bf16[2,128,768]{2,1,0:T(8,128)(2,1)}, bf16[2,128,768]{2,1,0:T(8,128)(2,1)}, u32[]{:S(2)}, u32[]{:S(2)}) collective-permute-start(bf16[2,128,768]{2,1,0:T(8,128)(2,1)} %get-tuple-element.102.refs_2_), channel_id=1, source_target_pairs={{0,1},{1,0},{2,3},{3,2},{4,5},{5,4},{6,7},{7,6},{8,9},{9,8},{10,11... | collective-permute-start | bytes 1179656 | tf_op jit(solution)/shard_map/ppermute | solution.py:22
  52.9 20.2 %collective-permute-start.16 = (bf16[2,128,768]{2,1,0:T(8,128)(2,1)}, bf16[2,128,768]{2,1,0:T(8,128)(2,1)}, u32[]{:S(2)}, u32[]{:S(2)}) collective-permute-start(bf16[2,128,768]{2,1,0:T(8,128)(2,1)} %get-tuple-element.102.refs_2_), channel_id=1, source_target_pairs={{0,3},{1,2},{2,1},{3,0},{4,7},{5,6},{6,5},{7,4},{8,11},{9,10},{10,... | collective-permute-start | bytes 1179656 | tf_op jit(solution)/shard_map/ppermute | solution.py:61
  54.5 18.6 %collective-permute-start.15 = (bf16[2,128,768]{2,1,0:T(8,128)(2,1)}, bf16[2,128,768]{2,1,0:T(8,128)(2,1)}, u32[]{:S(2)}, u32[]{:S(2)}) collective-permute-start(bf16[2,128,768]{2,1,0:T(8,128)(2,1)} %get-tuple-element.103.refs_0_.refs_1_), channel_id=1, source_target_pairs={{0,2},{2,0},{1,3},{3,1},{4,6},{6,4},{5,7},{7,5},{8,10},{10,8},{9,1... | collective-permute-start | bytes 1179656 | tf_op jit(solution)/shard_map/ppermute | solution.py:22
  67.8 21.9 %collective-permute-start.18 = (bf16[2,320,4096]{2,1,0:T(8,128)(2,1)}, bf16[2,320,4096]{2,1,0:T(8,128)(2,1)}, u32[]{:S(2)}, u32[]{:S(2)}) collective-permute-start(bf16[2,320,4096]{2,1,0:T(8,128)(2,1)} %shard_map.88.refs_5_), channel_id=1, source_target_pairs={{0,1},{1,0},{2,3},{3,2},{4,5},{5,4},{6,7},{7,6},{8,9},{9,8},{10,11... | collective-permute-start | bytes 15728648 | tf_op jit(solution)/shard_map/ppermute | solution.py:22
  89.6 20.6 %collective-permute-start.22 = (bf16[320,4096]{1,0:T(8,128)(2,1)}, bf16[320,4096]{1,0:T(8,128)(2,1)}, u32[]{:S(2)}, u32[]{:S(2)}) collective-permute-start(bf16[320,4096]{1,0:T(8,128)(2,1)} %get-tuple-element.66.refs_0_), channel_id=1, source_target_pairs={{0,1},{1,0},{2,3},{3,2},{4,5},{5,4},{6,7},{7,6},{8,9},{9,8},{10,11... | collective-permute-start | bytes 7864328 | tf_op jit(solution)/shard_map/ppermute | solution.py:22
  107.6 19.7 %collective-permute-start.19 = (bf16[128,1536]{1,0:T(8,128)(2,1)}, bf16[128,1536]{1,0:T(8,128)(2,1)}, u32[]{:S(2)}, u32[]{:S(2)}) collective-permute-start(bf16[128,1536]{1,0:T(8,128)(2,1)} %get-tuple-element.63), channel_id=1, source_target_pairs={{0,1},{1,0},{2,3},{3,2},{4,5},{5,4},{6,7},{7,6},{8,9},{9,8},{10,11... | collective-permute-start | bytes 1179656 | tf_op jit(solution)/shard_map/ppermute | solution.py:22
  108.1 19.1 %collective-permute-start.20 = (bf16[128,1536]{1,0:T(8,128)(2,1)}, bf16[128,1536]{1,0:T(8,128)(2,1)}, u32[]{:S(2)}, u32[]{:S(2)}) collective-permute-start(bf16[128,1536]{1,0:T(8,128)(2,1)} %get-tuple-element.64), channel_id=1, source_target_pairs={{0,2},{2,0},{1,3},{3,1},{4,6},{6,4},{5,7},{7,5},{8,10},{10,8},{9,1... | collective-permute-start | bytes 1179656 | tf_op jit(solution)/shard_map/ppermute | solution.py:22
  109.6 17.7 %collective-permute-start.21 = (bf16[128,1536]{1,0:T(8,128)(2,1)}, bf16[128,1536]{1,0:T(8,128)(2,1)}, u32[]{:S(2)}, u32[]{:S(2)}) collective-permute-start(bf16[128,1536]{1,0:T(8,128)(2,1)} %get-tuple-element.65), channel_id=1, source_target_pairs={{0,3},{1,2},{2,1},{3,0},{4,7},{5,6},{6,5},{7,4},{8,11},{9,10},{10,... | collective-permute-start | bytes 1179656 | tf_op jit(solution)/shard_map/ppermute | solution.py:61
  109.6 26.7 %collective-permute-start.26 = (bf16[320,4096]{1,0:T(8,128)(2,1)}, bf16[320,4096]{1,0:T(8,128)(2,1)}, u32[]{:S(2)}, u32[]{:S(2)}) collective-permute-start(bf16[320,4096]{1,0:T(8,128)(2,1)} %get-tuple-element.72.refs_5_), channel_id=1, source_target_pairs={{0,1},{1,0},{2,3},{3,2},{4,5},{5,4},{6,7},{7,6},{8,9},{9,8},{10,11... | collective-permute-start | bytes 7864328 | tf_op jit(solution)/shard_map/ppermute | solution.py:22
  129.6 21.5 %collective-permute-start.23 = (bf16[128,768]{1,0:T(8,128)(2,1)}, bf16[128,768]{1,0:T(8,128)(2,1)}, u32[]{:S(2)}, u32[]{:S(2)}) collective-permute-start(bf16[128,768]{1,0:T(8,128)(2,1)} %get-tuple-element.95.refs_1_), channel_id=1, source_target_pairs={{0,8},{4,12},{8,0},{12,4},{1,9},{5,13},{9,1},{13,5},{2,10},{6,14},... | collective-permute-start | bytes 589832 | tf_op jit(solution)/shard_map/ppermute | solution.py:26
  134.8 16.3 %collective-permute-start.24 = (bf16[128,768]{1,0:T(8,128)(2,1)}, bf16[128,768]{1,0:T(8,128)(2,1)}, u32[]{:S(2)}, u32[]{:S(2)}) collective-permute-start(bf16[128,768]{1,0:T(8,128)(2,1)} %get-tuple-element.96.refs_2_), channel_id=1, source_target_pairs={{0,4},{4,0},{8,12},{12,8},{1,5},{5,1},{9,13},{13,9},{2,6},{6,2},{1... | collective-permute-start | bytes 589832 | tf_op jit(solution)/shard_map/ppermute | solution.py:26
  134.8 16.3 %collective-permute-start.25 = (bf16[128,768]{1,0:T(8,128)(2,1)}, bf16[128,768]{1,0:T(8,128)(2,1)}, u32[]{:S(2)}, u32[]{:S(2)}) collective-permute-start(bf16[128,768]{1,0:T(8,128)(2,1)} %get-tuple-element.94.refs_3_), channel_id=1, source_target_pairs={{0,12},{4,8},{8,4},{12,0},{1,13},{5,9},{9,5},{13,1},{2,14},{6,10},... | collective-permute-start | bytes 589832 | tf_op jit(solution)/shard_map/ppermute | solution.py:26
  151.2 6.8 %collective-permute-start.28 = (bf16[128,768]{1,0:T(8,128)(2,1)S(1)}, bf16[128,768]{1,0:T(8,128)(2,1)S(1)}, u32[]{:S(2)}, u32[]{:S(2)}) collective-permute-start(bf16[128,768]{1,0:T(8,128)(2,1)S(1)} %get-tuple-element.87), channel_id=1, source_target_pairs={{0,3},{1,2},{2,1},{3,0},{4,7},{5,6},{6,5},{7,4},{8,11},{9,10},{10,... | collective-permute-start | bytes 589832 | tf_op jit(solution)/shard_map/ppermute | solution.py:61
  152.8 10.4 %collective-permute-start.29 = (bf16[128,768]{1,0:T(8,128)(2,1)S(1)}, bf16[128,768]{1,0:T(8,128)(2,1)S(1)}, u32[]{:S(2)}, u32[]{:S(2)}) collective-permute-start(bf16[128,768]{1,0:T(8,128)(2,1)S(1)} %get-tuple-element.89), channel_id=1, source_target_pairs={{0,2},{2,0},{1,3},{3,1},{4,6},{6,4},{5,7},{7,5},{8,10},{10,8},{9,1... | collective-permute-start | bytes 589832 | tf_op jit(solution)/shard_map/ppermute | solution.py:22
  153.4 12.8 %collective-permute-start.31 = (bf16[128,768]{1,0:T(8,128)(2,1)S(1)}, bf16[128,768]{1,0:T(8,128)(2,1)S(1)}, u32[]{:S(2)}, u32[]{:S(2)}) collective-permute-start(bf16[128,768]{1,0:T(8,128)(2,1)S(1)} %get-tuple-element.90), channel_id=1, source_target_pairs={{0,1},{1,0},{2,3},{3,2},{4,5},{5,4},{6,7},{7,6},{8,9},{9,8},{10,11... | collective-permute-start | bytes 589832 | tf_op jit(solution)/shard_map/ppermute | solution.py:22
  153.4 13.1 %collective-permute-start.32 = (bf16[128,768]{1,0:T(8,128)(2,1)S(1)}, bf16[128,768]{1,0:T(8,128)(2,1)S(1)}, u32[]{:S(2)}, u32[]{:S(2)}) collective-permute-start(bf16[128,768]{1,0:T(8,128)(2,1)S(1)} %get-tuple-element.91), channel_id=1, source_target_pairs={{0,3},{1,2},{2,1},{3,0},{4,7},{5,6},{6,5},{7,4},{8,11},{9,10},{10,... | collective-permute-start | bytes 589832 | tf_op jit(solution)/shard_map/ppermute | solution.py:61
  155.0 16.2 %collective-permute-start.33 = (bf16[128,768]{1,0:T(8,128)(2,1)S(1)}, bf16[128,768]{1,0:T(8,128)(2,1)S(1)}, u32[]{:S(2)}, u32[]{:S(2)}) collective-permute-start(bf16[128,768]{1,0:T(8,128)(2,1)S(1)} %get-tuple-element.93), channel_id=1, source_target_pairs={{0,2},{2,0},{1,3},{3,1},{4,6},{6,4},{5,7},{7,5},{8,10},{10,8},{9,1... | collective-permute-start | bytes 589832 | tf_op jit(solution)/shard_map/ppermute | solution.py:22
  163.4 14.0 %collective-permute-start.30 = (bf16[128,768]{1,0:T(8,128)(2,1)S(1)}, bf16[128,768]{1,0:T(8,128)(2,1)S(1)}, u32[]{:S(2)}, u32[]{:S(2)}) collective-permute-start(bf16[128,768]{1,0:T(8,128)(2,1)S(1)} %select_convert_fusion.2), channel_id=1, source_target_pairs={{0,8},{4,12},{8,0},{12,4},{1,9},{5,13},{9,1},{13,5},{2,10},{6,14},... | collective-permute-start | bytes 589832 | tf_op jit(solution)/shard_map/ppermute | solution.py:26
  171.2 8.1 %collective-permute-start.34 = (bf16[128,768]{1,0:T(8,128)(2,1)S(1)}, bf16[128,768]{1,0:T(8,128)(2,1)S(1)}, u32[]{:S(2)}, u32[]{:S(2)}) collective-permute-start(bf16[128,768]{1,0:T(8,128)(2,1)S(1)} %get-tuple-element.100), channel_id=1, source_target_pairs={{0,4},{4,0},{8,12},{12,8},{1,5},{5,1},{9,13},{13,9},{2,6},{6,2},{1... | collective-permute-start | bytes 589832 | tf_op jit(solution)/shard_map/ppermute | solution.py:26
  173.9 10.0 %collective-permute-start.35 = (bf16[128,768]{1,0:T(8,128)(2,1)S(1)}, bf16[128,768]{1,0:T(8,128)(2,1)S(1)}, u32[]{:S(2)}, u32[]{:S(2)}) collective-permute-start(bf16[128,768]{1,0:T(8,128)(2,1)S(1)} %get-tuple-element.101), channel_id=1, source_target_pairs={{0,12},{4,8},{8,4},{12,0},{1,13},{5,9},{9,5},{13,1},{2,14},{6,10},... | collective-permute-start | bytes 589832 | tf_op jit(solution)/shard_map/ppermute | solution.py:26
  (11 other events, 133.8 us)

commit v3 on v2

--- a/solution.py
+++ b/solution.py
@@ -15,7 +15,7 @@
 TILE = 512
 DEPTH = 3
 COST = 50
-FIRST_COST = 1
+FIRST_COST = 0
 
 
 def swap(value, axis):
@@ -63,19 +63,20 @@
 
 def gather_meta(place, meta):
     if place.small:
-        return [part[None] for part in (meta, swap(meta, "sub"), swap(meta, "expert"), far_both(meta))]
-    return [lax.all_gather(meta, ("expert", "sub"))]
-
-
-def gather_now(place, rows, after):
+        pair = jnp.stack([meta, swap(meta, "sub")])
+        return jnp.concatenate([pair, swap(pair, "expert")])
+    return lax.all_gather(meta, ("expert", "sub"))
+
+
+def gather_now(place, rows, meta):
     near = [rows] + [across(rows, k) for k in (1, 2, 3)]
-    near[3], after = lax.optimization_barrier((near[3], after))
+    near[3], meta = lax.optimization_barrier((near[3], meta))
     far = [swap(block, "expert") for block in near]
     low_half = jnp.stack([near[0], near[1], far[0], far[1]])
     high_half = jnp.stack([near[2], near[3], far[2], far[3]])
     keep = jnp.where(place.high, high_half, low_half)
     send = jnp.where(place.high, low_half, high_half)
-    return [keep, swap(send, "sub")], [[0, 0, 2, 2], [1, 1, 3, 3]], near[3], after
+    return [keep, swap(send, "sub")], [[0, 0, 2, 2], [1, 1, 3, 3]], near[3], meta
 
 
 def gather_first(rows, after):
@@ -141,15 +142,14 @@
     return lax.psum_scatter(share, "tensor", scatter_dimension=0)
 
 
-def route_rows(small, locals_, index, metas, take_ref, gate_ref):
-    places = [ref.at[i] for ref in metas for i in range(ref.shape[0])]
-    rows = places[0].shape[0]
+def route_rows(small, locals_, index, meta_ref, take_ref, gate_ref):
+    rows = meta_ref.shape[2]
     row, column = (lax.broadcasted_iota(jnp.int32, (rows, rows), axis) for axis in (0, 1))
     before = jnp.where(row < column, 1.0, 0.0).astype(BF16)
     slot = lax.broadcasted_iota(jnp.int32, (CAP, rows), 0).astype(F32)
-    for place_at, meta_ref in enumerate(places):
+    for place_at in range(meta_ref.shape[0]):
         start = block_at(small, index, place_at)[1]
-        meta = jnp.concatenate([meta_ref[...], jnp.zeros((rows, 128 - meta_ref.shape[1]), F32)], axis=1).T
+        meta = meta_ref[place_at]
         for local in range(locals_):
             number = (index[0] * locals_ + local).astype(F32)
             one, two = meta[0:1] == number, meta[1:2] == number
@@ -199,16 +199,16 @@
 
 
 class Stream:
-    def __init__(self, weights, at, tile, rings, sems):
-        self.weights, self.at, self.tile, self.rings, self.sems = weights, at, tile, rings, sems
+    def __init__(self, arrays, places, tile, rings, sems):
+        self.arrays, self.places, self.tile, self.rings, self.sems = arrays, places, tile, rings, sems
         self.depth = rings[0].shape[0]
 
     def copies(self, step):
         slot = lax.rem(step, self.depth)
         cut = pl.ds(pl.multiple_of(step * self.tile, self.tile), self.tile)
         return [
-            pltpu.make_async_copy(weight.at[self.at(cut)], ring.at[slot], self.sems.at[i, slot])
-            for i, (weight, ring) in enumerate(zip(self.weights, self.rings, strict=True))
+            pltpu.make_async_copy(array.at[place(cut)], ring.at[slot], self.sems.at[i, slot])
+            for i, (array, place, ring) in enumerate(zip(self.arrays, self.places, self.rings, strict=True))
         ]
 
     def start(self, steps):
@@ -227,18 +227,30 @@
         return [ring.at[lax.rem(step, self.depth)] for ring in self.rings]
 
 
+def column_tile(local):
+    return lambda cut: (local, slice(None), cut)
+
+
+def pair_tile(cut):
+    return slice(None), slice(None), cut
+
+
+def one_tile(cut):
+    return slice(None), cut
+
+
 def first_body(small, local, locals_, places, n_routes, n_after, tile, steps, *refs):
     routes, refs = refs[:n_routes], refs[n_routes + n_after :]
     groups, (gate_w, up_w, out, *routed, rows, gate_ring, up_ring, sems) = refs[: len(places)], refs[len(places) :]
     take_ref = routes[0] if local else routed[0]
-    stream = Stream([gate_w, up_w], lambda cut: (local, slice(None), cut), tile, [gate_ring, up_ring], sems)
+    stream = Stream([gate_w, up_w], [column_tile(local)] * 2, tile, [gate_ring, up_ring], sems)
     step = pl.program_id(0)
 
     @pl.when(step == 0)
     def _():
         stream.start(steps)
         if not local:
-            route_rows(small, locals_, axis_indices(), routes, *routed)
+            route_rows(small, locals_, axis_indices(), *routes, *routed)
         place_rows(small, axis_indices(), take_ref, local, groups, places, rows)
 
     for i, weight in enumerate(stream.take(step)):
@@ -249,8 +261,10 @@
     groups, refs = refs[: len(places)], refs[len(places) :]
     last = local == locals_ - 1
     before, refs = (refs[:local], refs[local:]) if last else ((), refs)
-    own, got, down, slopes, back, *outs, rows, total, slots, ring, sems = refs
-    stream = Stream([down], lambda cut: (local, cut), tile, [ring], sems)
+    own_at, got_at, down, slopes, back, *outs, rows, total, slots, own_ring, got_ring, ring, sems = refs
+    stream = Stream(
+        [down, own_at, got_at], [lambda cut: (local, cut), pair_tile, pair_tile], tile, [ring, own_ring, got_ring], sems
+    )
     step = pl.program_id(0)
 
     @pl.when(step == 0)
@@ -259,7 +273,7 @@
         place_rows(small, axis_indices(), take_ref, local, groups, places, rows)
         total[...] = jnp.zeros_like(total)
 
-    (weight,) = stream.take(step)
+    weight, own, got = stream.take(step)
     back[...] = nt(rows[...], weight[...]).astype(BF16)
     gate_pre = own[0].astype(F32) + got[0].astype(F32)
     up_pre = own[1].astype(F32) + got[1].astype(F32)
@@ -279,8 +293,11 @@
     refs = refs[n_after:]
     last = local == locals_ - 1
     before, refs = (refs[:local], refs[local:]) if last else ((), refs)
-    own, got, slopes, gate_w, up_w, *outs, total, slots, gate_ring, up_ring, sems = refs
-    stream = Stream([gate_w, up_w], lambda cut: (local, slice(None), cut), tile, [gate_ring, up_ring], sems)
+    own_at, got_at, slopes_at, gate_w, up_w, *outs, total, slots, own_ring, got_ring, slope_ring, gate_ring, up_ring, sems = refs
+    stream = Stream(
+        [own_at, got_at, slopes_at, gate_w, up_w], [one_tile, one_tile, pair_tile, *[column_tile(local)] * 2], tile,
+        [own_ring, got_ring, slope_ring, gate_ring, up_ring], sems,
+    )
     step = pl.program_id(0)
 
     @pl.when(step == 0)
@@ -288,7 +305,7 @@
         stream.start(steps)
         total[...] = jnp.zeros_like(total)
 
-    gate_tile, up_tile = stream.take(step)
+    own, got, slopes, gate_tile, up_tile = stream.take(step)
     back = own[...].astype(F32) + got[...].astype(F32)
     up_grad = (back * slopes[0].astype(F32)).astype(BF16)
     gate_grad = (back * slopes[1].astype(F32)).astype(BF16)
@@ -328,6 +345,10 @@
     )(*routes, *after, *near, *weights)
 
 
+def in_hbm(*arrays):
+    return [pltpu.with_memory_space_constraint(array, pltpu.HBM) for array in arrays]
+
+
 def per_device(tokens, cotangent, expert_ids, gate_values, w_gate, w_up, w_down):
     place = Place()
     small, blocks = place.small, place.blocks
@@ -336,13 +357,13 @@
     slots = blocks * CAP
     flops = 2 * slots * half * hidden
 
-    ids = jnp.pad(expert_ids.astype(F32), ((0, 0), (0, gate_values.shape[1])))
-    metas = gather_meta(place, ids + jnp.pad(gate_values, ((0, 0), (expert_ids.shape[1], 0))))
+    meta = jnp.concatenate([expert_ids.astype(F32).T, gate_values.T, jnp.zeros((4, count), F32)])
+    meta = gather_meta(place, meta)
     routed = [jax.ShapeDtypeStruct((locals_, blocks, CAP, count), BF16),
               jax.ShapeDtypeStruct((locals_, slots, 1), F32)]
 
     if small:
-        token_groups, token_places, token_last, metas = gather_now(place, tokens, metas)
+        token_groups, token_places, token_last, meta = gather_now(place, tokens, meta)
         grad_near = gather_first(cotangent, token_last)
     else:
         token_groups, token_places = gather_rows(place, tokens)
@@ -354,7 +375,11 @@
     one = pltpu.HBM((slots, hidden), BF16)
     pair_spec = pl.BlockSpec((2, slots, tile), lambda f: (0, 0, f))
     one_spec = pl.BlockSpec((slots, tile), lambda f: (0, f))
-    two_sems, one_sem = pltpu.SemaphoreType.DMA((2, DEPTH)), pltpu.SemaphoreType.DMA((1, DEPTH))
+    pair_ring, one_ring = pltpu.VMEM((DEPTH, 2, slots, tile), BF16), pltpu.VMEM((DEPTH, slots, tile), BF16)
+
+    def sems(arrays):
+        return pltpu.SemaphoreType.DMA((arrays, DEPTH))
+
 
     def ends(local, width):
         return [jax.ShapeDtypeStruct((count, width), BF16)] * (blocks * half // width) if local == locals_ - 1 else [
@@ -363,11 +388,11 @@
     own_pre, got_pre, after = [], [], []
     for local in range(locals_):
         ring = pltpu.VMEM((DEPTH, half, tile), BF16)
-        routes, new = ([take], []) if local else (metas, routed)
+        routes, new = ([take], []) if local else ([meta], routed)
         own, *new = call(
             functools.partial(first_body, small, local, locals_, token_places, len(routes), len(after), tile, steps),
             steps, routes, after, token_groups, [*map(whole, token_groups)], [w_gate, w_up],
-            [pair, *new], [pair_spec, *map(whole, new)], [pltpu.VMEM((slots, half), BF16), ring, ring, two_sems],
+            [pair, *new], [pair_spec, *map(whole, new)], [pltpu.VMEM((slots, half), BF16), ring, ring, sems(2)],
             (COST if local else FIRST_COST) * flops,
         )
         if not local:
@@ -383,11 +408,11 @@
         outs = ends(local, half)
         slope, back, *mixed_parts = call(
             functools.partial(middle_body, small, local, locals_, grad_places, tile, steps),
-            steps, [take, gate], [], [*grad_groups, *before, own_pre[local], got_pre[local]],
-            [*map(whole, [*grad_groups, *before]), pair_spec, pair_spec], [w_down],
+            steps, [take, gate], [], [*grad_groups, *before], [*map(whole, [*grad_groups, *before])],
+            [*in_hbm(own_pre[local], got_pre[local]), w_down],
             [pair, one, *outs], [pair_spec, one_spec, *map(whole, outs)],
             [pltpu.VMEM((slots, half), BF16), pltpu.VMEM((slots, half), F32), pltpu.VMEM((slots, half), BF16),
-             pltpu.VMEM((DEPTH, tile, half), BF16), one_sem],
+             pair_ring, pair_ring, pltpu.VMEM((DEPTH, tile, half), BF16), sems(3)],
             COST * flops,
         )
         slopes.append(slope)
@@ -404,10 +429,11 @@
         outs = ends(local, half // 2 if small and last else half)
         grad_parts = call(
             functools.partial(last_body, small, local, locals_, len(after), tile, steps),
-            steps, [take, gate], after, [*before, own_back[local], got_back[local], slopes[local]],
-            [*map(whole, before), one_spec, one_spec, pair_spec], [w_gate, w_up],
+            steps, [take, gate], after, before, [*map(whole, before)],
+            [*in_hbm(own_back[local], got_back[local], slopes[local]), w_gate, w_up],
             outs, [*map(whole, outs)],
-            [pltpu.VMEM((slots, half), F32), pltpu.VMEM((slots, half), BF16), ring, ring, two_sems],
+            [pltpu.VMEM((slots, half), F32), pltpu.VMEM((slots, half), BF16), one_ring, one_ring, pair_ring, ring, ring,
+             sems(5)],
             COST * flops,
         )
         done.append(grad_parts[0])

time: 185 us -> 182 us (0.984)
  waiting for transfers between devices: 41.4 us -> 45.4 us
  local copies, waits for them, and re-layouts: 3.41 us -> 0.08 us
  Pallas kernels: 89.3 us -> 86.3 us
    ppermute x12, waiting for transfers between devices: 13.8 us -> 17.5 us  [across(): lax.ppermute(value, 'tensor', [(i, i ^ distance) for i in range(lax.axis_...]
    ppermute x5 -> x4, waiting for transfers between devices: 2.88 us -> 6.19 us  [far_both(): lax.ppermute(value, ('expert', 'sub'), [(i, 3 - i) for i in range(4)])]
    unnamed x15 -> x2, local copies, waits for them, and re-layouts: 3.29 us -> 0.01 us
    pallas_call x6, Pallas kernels: 89.3 us -> 86.3 us  [call(): pl.pallas_call(body, grid=(steps,), in_specs=[*map(whole, routes), *[anyw...]
    ppermute x19, waiting for transfers between devices: 24.6 us -> 21.7 us  [swap(): return lax.ppermute(value, axis, [(0, 1), (1, 0)])]
    ppermute x5 -> x4, starting transfers between devices: 5.75 us -> 4.59 us  [far_both(): lax.ppermute(value, ('expert', 'sub'), [(i, 3 - i) for i in range(4)])]
  transfers between devices with their start and end apart: 36 -> 35, of which waited for: 14 -> 13; matrix products, arithmetic and copies ran while one was open for 4% -> 3% of each run, Pallas kernels for 48% -> 47%
where the time goes in v3:
time: 182 us
  Pallas kernels  86.3 us (47%)
  waiting for transfers between devices  45.4 us (25%)
  starting transfers between devices  40.7 us (22%)
  other arithmetic  8.79 us (5%)
    pallas_call x6, Pallas kernels, call(): pl.pallas_call(body, grid=(steps,), in_specs=[*map(whole, routes), *[anyw...  86.3 us
    ppermute x12, starting transfers between devices, across(): lax.ppermute(value, 'tensor', [(i, i ^ distance) for i in range(lax.axis_...  24.2 us
    ppermute x19, waiting for transfers between devices, swap(): return lax.ppermute(value, axis, [(0, 1), (1, 0)])  21.7 us
    ppermute x12, waiting for transfers between devices, across(): lax.ppermute(value, 'tensor', [(i, i ^ distance) for i in range(lax.axis_...  17.5 us
    ppermute x19, starting transfers between devices, swap(): return lax.ppermute(value, axis, [(0, 1), (1, 0)])  11.9 us
    ppermute x4, waiting for transfers between devices, far_both(): lax.ppermute(value, ('expert', 'sub'), [(i, 3 - i) for i in range(4)])  6.19 us
    ppermute x4, starting transfers between devices, far_both(): lax.ppermute(value, ('expert', 'sub'), [(i, 3 - i) for i in range(4)])  4.59 us
  transfers between devices with their start and end apart: 35, of which 13 were waited for; matrix products, arithmetic and copies ran while one was open for 3% of the time, Pallas kernels for 47%

profile of v3, /device:TPU:0, one launch (start us, length us, event | category | flops | bytes accessed | tf_op | source)
XLA Modules:
  0.0 182.1 jit_solution(6181475094810613289)
XLA Ops:
  2.6 4.6 %collective-permute-start = (bf16[128,768]{1,0:T(8,128)(2,1)}, bf16[128,768]{1,0:T(8,128)(2,1)S(1)}, u32[]{:S(2)}, u32[]{:S(2)}) collective-permute-start(bf16[128,768]{1,0:T(8,128)(2,1)} %param.7), channel_id=1, source_target_pairs={{0,12},{4,8},{8,4},{12,0},{1,13},{5,9},{9,5},{13,1},{2,14},{6,10},... | collective-permute-start | bytes 589832 | tf_op jit(solution)/shard_map/ppermute | solution.py:26
  7.9 1.6 collective-permute-start.2
  9.9 1.6 collective-permute-done.2
  11.5 1.7 collective-permute-done
  13.2 1.6 collective-permute-start.5
  14.8 3.5 %collective-permute-done.6 = bf16[128,768]{1,0:T(8,128)(2,1)S(1)} collective-permute-done((bf16[128,768]{1,0:T(8,128)(2,1)}, bf16[128,768]{1,0:T(8,128)(2,1)S(1)}, u32[]{:S(2)}, u32[]{:S(2)}) %collective-permute-start.6) | collective-permute-done | bytes 196640 | tf_op jit(solution)/shard_map/ppermute | solution.py:26
  18.3 1.5 collective-permute-start.8
  19.8 5.0 %collective-permute-done.3 = bf16[128,768]{1,0:T(8,128)(2,1)S(1)} collective-permute-done((bf16[128,768]{1,0:T(8,128)(2,1)}, bf16[128,768]{1,0:T(8,128)(2,1)S(1)}, u32[]{:S(2)}, u32[]{:S(2)}) %collective-permute-start.3) | collective-permute-done | bytes 196640 | tf_op jit(solution)/shard_map/ppermute | solution.py:26
  24.8 1.5 collective-permute-start.4
  26.3 5.0 %collective-permute-done.4 = bf16[128,768]{1,0:T(8,128)(2,1)S(1)} collective-permute-done((bf16[128,768]{1,0:T(8,128)(2,1)S(1)}, bf16[128,768]{1,0:T(8,128)(2,1)S(1)}, u32[]{:S(2)}, u32[]{:S(2)}) %collective-permute-start.4) | collective-permute-done | bytes 196640 | tf_op jit(solution)/shard_map/ppermute | solution.py:22
  33.1 2.5 %collective-permute-start.11 = (bf16[128,768]{1,0:T(8,128)(2,1)}, bf16[128,768]{1,0:T(8,128)(2,1)S(1)}, u32[]{:S(2)}, u32[]{:S(2)}) collective-permute-start(bf16[128,768]{1,0:T(8,128)(2,1)} %param.8), channel_id=1, source_target_pairs={{0,8},{4,12},{8,0},{12,4},{1,9},{5,13},{9,1},{13,5},{2,10},{6,14},... | collective-permute-start | bytes 589832 | tf_op jit(solution)/shard_map/ppermute | solution.py:26
  37.0 13.0 %shard_map.86 = (bf16[2,320,4096]{2,1,0:T(8,128)(2,1)}, bf16[2,4,80,128]{3,2,1,0:T(8,128)(2,1)S(1)}, f32[2,320,1]{2,1,0:T(8,128)S(1)}) custom-call(f32[4,8,128]{2,1,0:T(8,128)S(1)} %pad_maximum_fusion.4.refs_0_, bf16[4,128,768]{2,1,0:T(8,128)(2,1)S(1)} %get-tuple-element.93.refs_1_.refs_3_, bf16[4,128,768]{2,1,0:T(8,128)(2,1)S(1)} %collective-permute-done.9.refs_2_.refs_4_, ...), custom_call_target="tpu_custom_call" | custom-call | tf_op jit(solution)/shard_map/pallas_call | solution.py:335
  51.5 1.5 collective-permute-start.15
  53.6 12.6 %shard_map.88.refs_5_ = bf16[2,320,4096]{2,1,0:T(8,128)(2,1)} custom-call(bf16[2,4,80,128]{3,2,1,0:T(8,128)(2,1)S(1)} %get-tuple-element.47.take_ref.refs_0_, bf16[2,128,768]{2,1,0:T(8,128)(2,1)} %get-tuple-element.97.refs_0_.refs_1_, bf16[2,128,768]{2,1,0:T(8,128)(2,1)} %get-tuple-element.96.refs_2_, ...), custom_call_target="tpu_custom_call" | custom-call | flops 201326592000 | tf_op jit(solution)/shard_map/pallas_call | solution.py:335
  66.3 5.4 %collective-permute-done.14.refs_2_ = bf16[2,128,768]{2,1,0:T(8,128)(2,1)} collective-permute-done((bf16[2,128,768]{2,1,0:T(8,128)(2,1)}, bf16[2,128,768]{2,1,0:T(8,128)(2,1)}, u32[]{:S(2)}, u32[]{:S(2)}) %collective-permute-start.14) | collective-permute-done | bytes 393248 | tf_op jit(solution)/shard_map/ppermute | solution.py:22
  71.7 15.9 %shard_map.87 = (bf16[2,320,4096]{2,1,0:T(8,128)(2,1)}, bf16[320,4096]{1,0:T(8,128)(2,1)}, bf16[320,1536]{1,0:T(8,128)(2,1)S(1)}) custom-call(bf16[2,4,80,128]{3,2,1,0:T(8,128)(2,1)S(1)} %get-tuple-element.47.take_ref.refs_0_, f32[2,320,1]{2,1,0:T(8,128)S(1)} %get-tuple-element.48.gate_ref, bf16[2,128,768]{2,1,0:T(8,128)(2,1)} %get-tuple-element.97.refs_0_.refs_1_, ...), custom_call_target="tpu_custom_call" | custom-call | flops 201326592000 | tf_op jit(solution)/shard_map/pallas_call | solution.py:335
  87.6 17.4 %shard_map.89 = (bf16[2,320,4096]{2,1,0:T(8,128)(2,1)}, bf16[320,4096]{1,0:T(8,128)(2,1)}, bf16[128,1536]{1,0:T(8,128)(2,1)S(1)}, bf16[128,1536]{1,0:T(8,128)(2,...) custom-call(bf16[2,4,80,128]{3,2,1,0:T(8,128)(2,1)S(1)} %get-tuple-element.47.take_ref.refs_0_, ...), custom_call_target="tpu_custom_call" | custom-call | flops 201326592000 | tf_op jit(solution)/shard_map/pallas_call | solution.py:335
  105.5 1.5 collective-permute-start.19
  107.7 13.2 %shard_map.90.refs_4_ = bf16[320,1536]{1,0:T(8,128)(2,1)S(1)} custom-call(bf16[2,4,80,128]{3,2,1,0:T(8,128)(2,1)S(1)} %get-tuple-element.47.take_ref.refs_0_, f32[2,320,1]{2,1,0:T(8,128)S(1)} %get-tuple-element.48.gate_ref, bf16[320,4096]{1,0:T(8,128)(2,1)} %get-tuple-element.60.refs_0_, bf16[320,4096]{1,0:T(8,128)(2,1)} %collective-permute-done.21.refs_1_, ...), custom_call_target="tpu_custom_call" | custom-call | flops 201326592000 | tf_op jit(solution)/shard_map/pallas_call | solution.py:335
  120.9 3.6 %collective-permute-done.20 = bf16[128,1536]{1,0:T(8,128)(2,1)} collective-permute-done((bf16[128,1536]{1,0:T(8,128)(2,1)}, bf16[128,1536]{1,0:T(8,128)(2,1)}, u32[]{:S(2)}, u32[]{:S(2)}) %collective-permute-start.20) | collective-permute-done | bytes 393248 | tf_op jit(solution)/shard_map/ppermute | solution.py:61
  124.5 2.3 %select_convert_fusion.4 = (bf16[128,768]{1,0:T(8,128)(2,1)}, bf16[128,768]{1,0:T(8,128)(2,1)}, bf16[128,768]{1,0:T(8,128)(2,1)}, bf16[128,768]{1,0:T(8,128)(2,1)S(1)}) fusion(pred[]{:T(512)S(6)} %eq.5, bf16[128,1536]{1,0:T(8,128)(2,1)} %collective-permute-done.19, bf16[128,1536]{1,0:T(8,128)(2,1)S(1)} %get-tuple-element.64, ...), kind=kLoop, calls=%fused_computation.16 | loop fusion | flops 1966080 | bytes 2359297 | tf_op jit(solution)/shard_map/convert_element_type | solution.py:120
  126.8 5.0 %collective-permute-start.22 = (bf16[128,768]{1,0:T(8,128)(2,1)}, bf16[128,768]{1,0:T(8,128)(2,1)}, u32[]{:S(2)}, u32[]{:S(2)}) collective-permute-start(bf16[128,768]{1,0:T(8,128)(2,1)} %get-tuple-element.89.refs_1_), channel_id=1, source_target_pairs={{0,8},{4,12},{8,0},{12,4},{1,9},{5,13},{9,1},{13,5},{2,10},{6,14},... | collective-permute-start | bytes 589832 | tf_op jit(solution)/shard_map/ppermute | solution.py:26
  133.2 14.3 %shard_map.91 = (bf16[128,768]{1,0:T(8,128)(2,1)S(1)}, bf16[128,768]{1,0:T(8,128)(2,1)S(1)}, bf16[128,768]{1,0:T(8,128)(2,1)S(1)}, bf16[128,768]{1,0:T(8,128)(2,...) custom-call(bf16[2,4,80,128]{3,2,1,0:T(8,128)(2,1)S(1)} %get-tuple-e, ...), custom_call_target="tpu_custom_call" | custom-call | flops 201326592000 | tf_op jit(solution)/shard_map/pallas_call | solution.py:335
  149.8 1.6 collective-permute-start.31
  151.9 2.6 %collective-permute-done.27 = bf16[128,768]{1,0:T(8,128)(2,1)S(1)} collective-permute-done((bf16[128,768]{1,0:T(8,128)(2,1)S(1)}, bf16[128,768]{1,0:T(8,128)(2,1)S(1)}, u32[]{:S(2)}, u32[]{:S(2)}) %collective-permute-start.27) | collective-permute-done | bytes 196640 | tf_op jit(solution)/shard_map/ppermute | solution.py:61
  154.6 5.1 %collective-permute-done.28 = bf16[128,768]{1,0:T(8,128)(2,1)S(1)} collective-permute-done((bf16[128,768]{1,0:T(8,128)(2,1)S(1)}, bf16[128,768]{1,0:T(8,128)(2,1)S(1)}, u32[]{:S(2)}, u32[]{:S(2)}) %collective-permute-start.28) | collective-permute-done | bytes 196640 | tf_op jit(solution)/shard_map/ppermute | solution.py:22
  159.8 3.3 %collective-permute-start.29 = (bf16[128,768]{1,0:T(8,128)(2,1)S(1)}, bf16[128,768]{1,0:T(8,128)(2,1)S(1)}, u32[]{:S(2)}, u32[]{:S(2)}) collective-permute-start(bf16[128,768]{1,0:T(8,128)(2,1)S(1)} %select_convert_fusion.2), channel_id=1, source_target_pairs={{0,8},{4,12},{8,0},{12,4},{1,9},{5,13},{9,1},{13,5},{2,10},{6,14},... | collective-permute-start | bytes 589832 | tf_op jit(solution)/shard_map/ppermute | solution.py:26
  163.1 4.5 %collective-permute-done.32 = bf16[128,768]{1,0:T(8,128)(2,1)S(1)} collective-permute-done((bf16[128,768]{1,0:T(8,128)(2,1)S(1)}, bf16[128,768]{1,0:T(8,128)(2,1)S(1)}, u32[]{:S(2)}, u32[]{:S(2)}) %collective-permute-start.32) | collective-permute-done | bytes 196640 | tf_op jit(solution)/shard_map/ppermute | solution.py:22
  167.8 3.5 %collective-permute-start.33 = (bf16[128,768]{1,0:T(8,128)(2,1)S(1)}, bf16[128,768]{1,0:T(8,128)(2,1)S(1)}, u32[]{:S(2)}, u32[]{:S(2)}) collective-permute-start(bf16[128,768]{1,0:T(8,128)(2,1)S(1)} %get-tuple-element.94), channel_id=1, source_target_pairs={{0,4},{4,0},{8,12},{12,8},{1,5},{5,1},{9,13},{13,9},{2,6},{6,2},{1... | collective-permute-start | bytes 589832 | tf_op jit(solution)/shard_map/ppermute | solution.py:26
  172.5 1.9 %add_convert_fusion.1 = bf16[128,768]{1,0:T(8,128)(2,1)} fusion(bf16[128,768]{1,0:T(8,128)(2,1)} %collective-permute-done.24, bf16[128,768]{1,0:T(8,128)(2,1)} %collective-permute-done.23, bf16[128,768]{1,0:T(8,128)(2,1)} %collective-permute-done.22, bf16[128,768]{1,0:T(8,128)(2,1)S(1)} %get-tuple-element.76.refs_0_), kind=kLoop, calls=%fused_computation.15 | loop fusion | flops 786432 | bytes 983040 | tf_op jit(solution)/shard_map/convert_element_type | solution.py:129
  174.4 2.1 %collective-permute-done.33 = bf16[128,768]{1,0:T(8,128)(2,1)S(1)} collective-permute-done((bf16[128,768]{1,0:T(8,128)(2,1)S(1)}, bf16[128,768]{1,0:T(8,128)(2,1)S(1)}, u32[]{:S(2)}, u32[]{:S(2)}) %collective-permute-start.33) | collective-permute-done | bytes 196640 | tf_op jit(solution)/shard_map/ppermute | solution.py:26
  176.6 4.7 %collective-permute-done.34 = bf16[128,768]{1,0:T(8,128)(2,1)S(1)} collective-permute-done((bf16[128,768]{1,0:T(8,128)(2,1)S(1)}, bf16[128,768]{1,0:T(8,128)(2,1)S(1)}, u32[]{:S(2)}, u32[]{:S(2)}) %collective-permute-start.34) | collective-permute-done | bytes 196640 | tf_op jit(solution)/shard_map/ppermute | solution.py:26
  (59 shorter events, 16.2 us)
Async XLA Ops:
  2.1 5.7 %collective-permute-start.1 = (f32[8,128]{1,0:T(8,128)S(1)}, f32[8,128]{1,0:T(8,128)S(1)}, u32[]{:S(2)}, u32[]{:S(2)}) collective-permute-start(f32[8,128]{1,0:T(8,128)S(1)} %get-tuple-element.99), channel_id=1, source_target_pairs={{0,1},{1,0},{2,3},{3,2},{4,5},{5,4},{6,7},{7,6},{8,9},{9,8},{10,11... | collective-permute-start | bytes 12296 | tf_op jit(solution)/shard_map/ppermute | solution.py:22
  2.6 10.6 %collective-permute-start = (bf16[128,768]{1,0:T(8,128)(2,1)}, bf16[128,768]{1,0:T(8,128)(2,1)S(1)}, u32[]{:S(2)}, u32[]{:S(2)}) collective-permute-start(bf16[128,768]{1,0:T(8,128)(2,1)} %param.7), channel_id=1, source_target_pairs={{0,12},{4,8},{8,4},{12,0},{1,13},{5,9},{9,5},{13,1},{2,14},{6,10},... | collective-permute-start | bytes 589832 | tf_op jit(solution)/shard_map/ppermute | solution.py:26
  7.2 11.1 %collective-permute-start.6 = (bf16[128,768]{1,0:T(8,128)(2,1)}, bf16[128,768]{1,0:T(8,128)(2,1)S(1)}, u32[]{:S(2)}, u32[]{:S(2)}) collective-permute-start(bf16[128,768]{1,0:T(8,128)(2,1)} %param.7), channel_id=1, source_target_pairs={{0,4},{4,0},{8,12},{12,8},{1,5},{5,1},{9,13},{13,9},{2,6},{6,2},{1... | collective-permute-start | bytes 589832 | tf_op jit(solution)/shard_map/ppermute | solution.py:26
  7.2 17.6 %collective-permute-start.3 = (bf16[128,768]{1,0:T(8,128)(2,1)}, bf16[128,768]{1,0:T(8,128)(2,1)S(1)}, u32[]{:S(2)}, u32[]{:S(2)}) collective-permute-start(bf16[128,768]{1,0:T(8,128)(2,1)} %param.7), channel_id=1, source_target_pairs={{0,8},{4,12},{8,0},{12,4},{1,9},{5,13},{9,1},{13,5},{2,10},{6,14},... | collective-permute-start | bytes 589832 | tf_op jit(solution)/shard_map/ppermute | solution.py:26
  9.5 16.8 %collective-permute-start.7 = (bf16[128,768]{1,0:T(8,128)(2,1)}, bf16[128,768]{1,0:T(8,128)(2,1)S(1)}, u32[]{:S(2)}, u32[]{:S(2)}) collective-permute-start(bf16[128,768]{1,0:T(8,128)(2,1)} %param.7), channel_id=1, source_target_pairs={{0,2},{2,0},{1,3},{3,1},{4,6},{6,4},{5,7},{7,5},{8,10},{10,8},{9,1... | collective-permute-start | bytes 589832 | tf_op jit(solution)/shard_map/ppermute | solution.py:22
  13.2 13.0 %collective-permute-start.5 = (bf16[128,768]{1,0:T(8,128)(2,1)S(1)}, bf16[128,768]{1,0:T(8,128)(2,1)S(1)}, u32[]{:S(2)}, u32[]{:S(2)}) collective-permute-start(bf16[128,768]{1,0:T(8,128)(2,1)S(1)} %collective-permute-done), channel_id=1, source_target_pairs={{0,2},{2,0},{1,3},{3,1},{4,6},{6,4},{5,7},{7,5},{8,10},{10,8},{9,1... | collective-permute-start | bytes 589832 | tf_op jit(solution)/shard_map/ppermute | solution.py:22
  18.3 8.0 %collective-permute-start.8 = (bf16[128,768]{1,0:T(8,128)(2,1)S(1)}, bf16[128,768]{1,0:T(8,128)(2,1)S(1)}, u32[]{:S(2)}, u32[]{:S(2)}) collective-permute-start(bf16[128,768]{1,0:T(8,128)(2,1)S(1)} %collective-permute-done.6), channel_id=1, source_target_pairs={{0,2},{2,0},{1,3},{3,1},{4,6},{6,4},{5,7},{7,5},{8,10},{10,8},{9,1... | collective-permute-start | bytes 589832 | tf_op jit(solution)/shard_map/ppermute | solution.py:22
  24.8 6.5 %collective-permute-start.4 = (bf16[128,768]{1,0:T(8,128)(2,1)S(1)}, bf16[128,768]{1,0:T(8,128)(2,1)S(1)}, u32[]{:S(2)}, u32[]{:S(2)}) collective-permute-start(bf16[128,768]{1,0:T(8,128)(2,1)S(1)} %collective-permute-done.3), channel_id=1, source_target_pairs={{0,2},{2,0},{1,3},{3,1},{4,6},{6,4},{5,7},{7,5},{8,10},{10,8},{9,1... | collective-permute-start | bytes 589832 | tf_op jit(solution)/shard_map/ppermute | solution.py:22
  32.5 17.5 %collective-permute-start.10 = (bf16[128,768]{1,0:T(8,128)(2,1)}, bf16[128,768]{1,0:T(8,128)(2,1)S(1)}, u32[]{:S(2)}, u32[]{:S(2)}) collective-permute-start(bf16[128,768]{1,0:T(8,128)(2,1)} %param.8), channel_id=1, source_target_pairs={{0,4},{4,0},{8,12},{12,8},{1,5},{5,1},{9,13},{13,9},{2,6},{6,2},{1... | collective-permute-start | bytes 589832 | tf_op jit(solution)/shard_map/ppermute | solution.py:26
  33.1 17.3 %collective-permute-start.11 = (bf16[128,768]{1,0:T(8,128)(2,1)}, bf16[128,768]{1,0:T(8,128)(2,1)S(1)}, u32[]{:S(2)}, u32[]{:S(2)}) collective-permute-start(bf16[128,768]{1,0:T(8,128)(2,1)} %param.8), channel_id=1, source_target_pairs={{0,8},{4,12},{8,0},{12,4},{1,9},{5,13},{9,1},{13,5},{2,10},{6,14},... | collective-permute-start | bytes 589832 | tf_op jit(solution)/shard_map/ppermute | solution.py:26
  35.7 14.8 %collective-permute-start.12 = (bf16[128,768]{1,0:T(8,128)(2,1)}, bf16[128,768]{1,0:T(8,128)(2,1)S(1)}, u32[]{:S(2)}, u32[]{:S(2)}) collective-permute-start(bf16[128,768]{1,0:T(8,128)(2,1)} %param.8), channel_id=1, source_target_pairs={{0,12},{4,8},{8,4},{12,0},{1,13},{5,9},{9,5},{13,1},{2,14},{6,10},... | collective-permute-start | bytes 589832 | tf_op jit(solution)/shard_map/ppermute | solution.py:26
  49.9 21.7 %collective-permute-start.16 = (bf16[2,320,4096]{2,1,0:T(8,128)(2,1)}, bf16[2,320,4096]{2,1,0:T(8,128)(2,1)}, u32[]{:S(2)}, u32[]{:S(2)}) collective-permute-start(bf16[2,320,4096]{2,1,0:T(8,128)(2,1)} %get-tuple-element.50.refs_4_), channel_id=1, source_target_pairs={{0,1},{1,0},{2,3},{3,2},{4,5},{5,4},{6,7},{7,6},{8,9},{9,8},{10,11... | collective-permute-start | bytes 15728648 | tf_op jit(solution)/shard_map/ppermute | solution.py:22
  51.4 14.8 %collective-permute-start.13 = (bf16[2,128,768]{2,1,0:T(8,128)(2,1)}, bf16[2,128,768]{2,1,0:T(8,128)(2,1)}, u32[]{:S(2)}, u32[]{:S(2)}) collective-permute-start(bf16[2,128,768]{2,1,0:T(8,128)(2,1)} %get-tuple-element.96.refs_2_), channel_id=1, source_target_pairs={{0,1},{1,0},{2,3},{3,2},{4,5},{5,4},{6,7},{7,6},{8,9},{9,8},{10,11... | collective-permute-start | bytes 1179656 | tf_op jit(solution)/shard_map/ppermute | solution.py:22
  51.5 20.2 %collective-permute-start.15 = (bf16[2,128,768]{2,1,0:T(8,128)(2,1)}, bf16[2,128,768]{2,1,0:T(8,128)(2,1)}, u32[]{:S(2)}, u32[]{:S(2)}) collective-permute-start(bf16[2,128,768]{2,1,0:T(8,128)(2,1)} %get-tuple-element.96.refs_2_), channel_id=1, source_target_pairs={{0,3},{1,2},{2,1},{3,0},{4,7},{5,6},{6,5},{7,4},{8,11},{9,10},{10,... | collective-permute-start | bytes 1179656 | tf_op jit(solution)/shard_map/ppermute | solution.py:61
  53.0 18.6 %collective-permute-start.14 = (bf16[2,128,768]{2,1,0:T(8,128)(2,1)}, bf16[2,128,768]{2,1,0:T(8,128)(2,1)}, u32[]{:S(2)}, u32[]{:S(2)}) collective-permute-start(bf16[2,128,768]{2,1,0:T(8,128)(2,1)} %get-tuple-element.97.refs_0_.refs_1_), channel_id=1, source_target_pairs={{0,2},{2,0},{1,3},{3,1},{4,6},{6,4},{5,7},{7,5},{8,10},{10,8},{9,1... | collective-permute-start | bytes 1179656 | tf_op jit(solution)/shard_map/ppermute | solution.py:22
  66.2 21.4 %collective-permute-start.17 = (bf16[2,320,4096]{2,1,0:T(8,128)(2,1)}, bf16[2,320,4096]{2,1,0:T(8,128)(2,1)}, u32[]{:S(2)}, u32[]{:S(2)}) collective-permute-start(bf16[2,320,4096]{2,1,0:T(8,128)(2,1)} %shard_map.88.refs_5_), channel_id=1, source_target_pairs={{0,1},{1,0},{2,3},{3,2},{4,5},{5,4},{6,7},{7,6},{8,9},{9,8},{10,11... | collective-permute-start | bytes 15728648 | tf_op jit(solution)/shard_map/ppermute | solution.py:22
  87.5 20.1 %collective-permute-start.21 = (bf16[320,4096]{1,0:T(8,128)(2,1)}, bf16[320,4096]{1,0:T(8,128)(2,1)}, u32[]{:S(2)}, u32[]{:S(2)}) collective-permute-start(bf16[320,4096]{1,0:T(8,128)(2,1)} %get-tuple-element.60.refs_0_), channel_id=1, source_target_pairs={{0,1},{1,0},{2,3},{3,2},{4,5},{5,4},{6,7},{7,6},{8,9},{9,8},{10,11... | collective-permute-start | bytes 7864328 | tf_op jit(solution)/shard_map/ppermute | solution.py:22
  105.0 15.9 %collective-permute-start.18 = (bf16[128,1536]{1,0:T(8,128)(2,1)}, bf16[128,1536]{1,0:T(8,128)(2,1)}, u32[]{:S(2)}, u32[]{:S(2)}) collective-permute-start(bf16[128,1536]{1,0:T(8,128)(2,1)} %get-tuple-element.57), channel_id=1, source_target_pairs={{0,1},{1,0},{2,3},{3,2},{4,5},{5,4},{6,7},{7,6},{8,9},{9,8},{10,11... | collective-permute-start | bytes 1179656 | tf_op jit(solution)/shard_map/ppermute | solution.py:22
  105.5 15.4 %collective-permute-start.19 = (bf16[128,1536]{1,0:T(8,128)(2,1)}, bf16[128,1536]{1,0:T(8,128)(2,1)}, u32[]{:S(2)}, u32[]{:S(2)}) collective-permute-start(bf16[128,1536]{1,0:T(8,128)(2,1)} %get-tuple-element.58), channel_id=1, source_target_pairs={{0,2},{2,0},{1,3},{3,1},{4,6},{6,4},{5,7},{7,5},{8,10},{10,8},{9,1... | collective-permute-start | bytes 1179656 | tf_op jit(solution)/shard_map/ppermute | solution.py:22
  107.0 17.5 %collective-permute-start.20 = (bf16[128,1536]{1,0:T(8,128)(2,1)}, bf16[128,1536]{1,0:T(8,128)(2,1)}, u32[]{:S(2)}, u32[]{:S(2)}) collective-permute-start(bf16[128,1536]{1,0:T(8,128)(2,1)} %get-tuple-element.59), channel_id=1, source_target_pairs={{0,3},{1,2},{2,1},{3,0},{4,7},{5,6},{6,5},{7,4},{8,11},{9,10},{10,... | collective-permute-start | bytes 1179656 | tf_op jit(solution)/shard_map/ppermute | solution.py:61
  107.0 26.2 %collective-permute-start.25 = (bf16[320,4096]{1,0:T(8,128)(2,1)}, bf16[320,4096]{1,0:T(8,128)(2,1)}, u32[]{:S(2)}, u32[]{:S(2)}) collective-permute-start(bf16[320,4096]{1,0:T(8,128)(2,1)} %get-tuple-element.66.refs_5_), channel_id=1, source_target_pairs={{0,1},{1,0},{2,3},{3,2},{4,5},{5,4},{6,7},{7,6},{8,9},{9,8},{10,11... | collective-permute-start | bytes 7864328 | tf_op jit(solution)/shard_map/ppermute | solution.py:22
  126.8 20.8 %collective-permute-start.22 = (bf16[128,768]{1,0:T(8,128)(2,1)}, bf16[128,768]{1,0:T(8,128)(2,1)}, u32[]{:S(2)}, u32[]{:S(2)}) collective-permute-start(bf16[128,768]{1,0:T(8,128)(2,1)} %get-tuple-element.89.refs_1_), channel_id=1, source_target_pairs={{0,8},{4,12},{8,0},{12,4},{1,9},{5,13},{9,1},{13,5},{2,10},{6,14},... | collective-permute-start | bytes 589832 | tf_op jit(solution)/shard_map/ppermute | solution.py:26
  131.8 15.8 %collective-permute-start.23 = (bf16[128,768]{1,0:T(8,128)(2,1)}, bf16[128,768]{1,0:T(8,128)(2,1)}, u32[]{:S(2)}, u32[]{:S(2)}) collective-permute-start(bf16[128,768]{1,0:T(8,128)(2,1)} %get-tuple-element.90.refs_2_), channel_id=1, source_target_pairs={{0,4},{4,0},{8,12},{12,8},{1,5},{5,1},{9,13},{13,9},{2,6},{6,2},{1... | collective-permute-start | bytes 589832 | tf_op jit(solution)/shard_map/ppermute | solution.py:26
  131.8 15.8 %collective-permute-start.24 = (bf16[128,768]{1,0:T(8,128)(2,1)}, bf16[128,768]{1,0:T(8,128)(2,1)}, u32[]{:S(2)}, u32[]{:S(2)}) collective-permute-start(bf16[128,768]{1,0:T(8,128)(2,1)} %get-tuple-element.88.refs_3_), channel_id=1, source_target_pairs={{0,12},{4,8},{8,4},{12,0},{1,13},{5,9},{9,5},{13,1},{2,14},{6,10},... | collective-permute-start | bytes 589832 | tf_op jit(solution)/shard_map/ppermute | solution.py:26
  147.8 6.8 %collective-permute-start.27 = (bf16[128,768]{1,0:T(8,128)(2,1)S(1)}, bf16[128,768]{1,0:T(8,128)(2,1)S(1)}, u32[]{:S(2)}, u32[]{:S(2)}) collective-permute-start(bf16[128,768]{1,0:T(8,128)(2,1)S(1)} %get-tuple-element.81), channel_id=1, source_target_pairs={{0,3},{1,2},{2,1},{3,0},{4,7},{5,6},{6,5},{7,4},{8,11},{9,10},{10,... | collective-permute-start | bytes 589832 | tf_op jit(solution)/shard_map/ppermute | solution.py:61
  149.2 10.4 %collective-permute-start.28 = (bf16[128,768]{1,0:T(8,128)(2,1)S(1)}, bf16[128,768]{1,0:T(8,128)(2,1)S(1)}, u32[]{:S(2)}, u32[]{:S(2)}) collective-permute-start(bf16[128,768]{1,0:T(8,128)(2,1)S(1)} %get-tuple-element.83), channel_id=1, source_target_pairs={{0,2},{2,0},{1,3},{3,1},{4,6},{6,4},{5,7},{7,5},{8,10},{10,8},{9,1... | collective-permute-start | bytes 589832 | tf_op jit(solution)/shard_map/ppermute | solution.py:22
  149.8 13.3 %collective-permute-start.30 = (bf16[128,768]{1,0:T(8,128)(2,1)S(1)}, bf16[128,768]{1,0:T(8,128)(2,1)S(1)}, u32[]{:S(2)}, u32[]{:S(2)}) collective-permute-start(bf16[128,768]{1,0:T(8,128)(2,1)S(1)} %get-tuple-element.84), channel_id=1, source_target_pairs={{0,1},{1,0},{2,3},{3,2},{4,5},{5,4},{6,7},{7,6},{8,9},{9,8},{10,11... | collective-permute-start | bytes 589832 | tf_op jit(solution)/shard_map/ppermute | solution.py:22
  149.8 13.3 %collective-permute-start.31 = (bf16[128,768]{1,0:T(8,128)(2,1)S(1)}, bf16[128,768]{1,0:T(8,128)(2,1)S(1)}, u32[]{:S(2)}, u32[]{:S(2)}) collective-permute-start(bf16[128,768]{1,0:T(8,128)(2,1)S(1)} %get-tuple-element.85), channel_id=1, source_target_pairs={{0,3},{1,2},{2,1},{3,0},{4,7},{5,6},{6,5},{7,4},{8,11},{9,10},{10,... | collective-permute-start | bytes 589832 | tf_op jit(solution)/shard_map/ppermute | solution.py:61
  151.4 16.3 %collective-permute-start.32 = (bf16[128,768]{1,0:T(8,128)(2,1)S(1)}, bf16[128,768]{1,0:T(8,128)(2,1)S(1)}, u32[]{:S(2)}, u32[]{:S(2)}) collective-permute-start(bf16[128,768]{1,0:T(8,128)(2,1)S(1)} %get-tuple-element.87), channel_id=1, source_target_pairs={{0,2},{2,0},{1,3},{3,1},{4,6},{6,4},{5,7},{7,5},{8,10},{10,8},{9,1... | collective-permute-start | bytes 589832 | tf_op jit(solution)/shard_map/ppermute | solution.py:22
  159.8 14.7 %collective-permute-start.29 = (bf16[128,768]{1,0:T(8,128)(2,1)S(1)}, bf16[128,768]{1,0:T(8,128)(2,1)S(1)}, u32[]{:S(2)}, u32[]{:S(2)}) collective-permute-start(bf16[128,768]{1,0:T(8,128)(2,1)S(1)} %select_convert_fusion.2), channel_id=1, source_target_pairs={{0,8},{4,12},{8,0},{12,4},{1,9},{5,13},{9,1},{13,5},{2,10},{6,14},... | collective-permute-start | bytes 589832 | tf_op jit(solution)/shard_map/ppermute | solution.py:26
  167.8 8.8 %collective-permute-start.33 = (bf16[128,768]{1,0:T(8,128)(2,1)S(1)}, bf16[128,768]{1,0:T(8,128)(2,1)S(1)}, u32[]{:S(2)}, u32[]{:S(2)}) collective-permute-start(bf16[128,768]{1,0:T(8,128)(2,1)S(1)} %get-tuple-element.94), channel_id=1, source_target_pairs={{0,4},{4,0},{8,12},{12,8},{1,5},{5,1},{9,13},{13,9},{2,6},{6,2},{1... | collective-permute-start | bytes 589832 | tf_op jit(solution)/shard_map/ppermute | solution.py:26
  171.2 10.0 %collective-permute-start.34 = (bf16[128,768]{1,0:T(8,128)(2,1)S(1)}, bf16[128,768]{1,0:T(8,128)(2,1)S(1)}, u32[]{:S(2)}, u32[]{:S(2)}) collective-permute-start(bf16[128,768]{1,0:T(8,128)(2,1)S(1)} %get-tuple-element.95), channel_id=1, source_target_pairs={{0,12},{4,8},{8,4},{12,0},{1,13},{5,9},{9,5},{13,1},{2,14},{6,10},... | collective-permute-start | bytes 589832 | tf_op jit(solution)/shard_map/ppermute | solution.py:26
  (4 other events, 25.5 us)

commit v4 on v3

--- a/solution.py
+++ b/solution.py
@@ -15,7 +15,7 @@
 TILE = 512
 DEPTH = 3
 COST = 50
-FIRST_COST = 0
+FIRST_COST = 1000
 
 
 def swap(value, axis):
@@ -341,7 +341,7 @@
         out_shape=outs,
         scratch_shapes=scratch,
         compiler_params=pltpu.CompilerParams(vmem_limit_bytes=VMEM_BYTES),
-        cost_estimate=pl.CostEstimate(flops=flops, bytes_accessed=0, transcendentals=0),
+        cost_estimate=pl.CostEstimate(flops=flops, bytes_accessed=1000, transcendentals=0),
     )(*routes, *after, *near, *weights)
 
 
@@ -393,7 +393,7 @@
             functools.partial(first_body, small, local, locals_, token_places, len(routes), len(after), tile, steps),
             steps, routes, after, token_groups, [*map(whole, token_groups)], [w_gate, w_up],
             [pair, *new], [pair_spec, *map(whole, new)], [pltpu.VMEM((slots, half), BF16), ring, ring, sems(2)],
-            (COST if local else FIRST_COST) * flops,
+            COST * flops if local else FIRST_COST,
         )
         if not local:
             take, gate = new
@@ -437,17 +437,19 @@
             COST * flops,
         )
         done.append(grad_parts[0])
-        if small and local == 0:
-            *terms, _ = lax.optimization_barrier((*mixed_terms, grad_parts[0]))
-            terms = [[term[:, i * half // 2 : (i + 1) * half // 2] for term in terms] for i in range(2)]
-            after = [*sum_x(place, terms[0]), *sum_x(place, terms[1])]
-            mixed_terms = send_z(*after)
     if not small:
         return scatter_rows(place, mixed_parts), scatter_rows(place, grad_parts)
-    *mixed_terms, grad_parts = lax.optimization_barrier((*mixed_terms, grad_parts))
     next_terms = send_x(place, grad_parts[blocks:])
     last_terms = send_x(place, grad_parts[:blocks])
-    return sum_z(mixed_terms), sum_z(send_z(*sum_x(place, last_terms), *sum_x(place, next_terms)))
+
+    *mixed_terms, _ = lax.optimization_barrier((*mixed_terms, grad_parts[0]))
+    mixed_terms = [[term[:, i * half // 2 : (i + 1) * half // 2] for term in mixed_terms] for i in range(2)]
+    (near, far), (near_next, far_next) = (sum_x(place, terms) for terms in mixed_terms)
+    got = across(jnp.stack([near_next, far]), 1)
+    rest = (far_next.astype(F32) + got[1].astype(F32)).astype(BF16)
+    *next_terms, rest = lax.optimization_barrier((*next_terms, rest))
+    mixed = sum_z((near, got[0], across(rest, 3)))
+    return mixed, sum_z(send_z(*sum_x(place, last_terms), *sum_x(place, next_terms)))
 
 
 def solution(mesh):

time: 182 us -> 176 us (0.967); the launches traced: 182 us -> 174 us
  waiting for transfers between devices: 45.4 us -> 36.4 us
    ppermute x19, waiting for transfers between devices: 21.7 us -> 14.1 us  [swap(): return lax.ppermute(value, axis, [(0, 1), (1, 0)])]
    ppermute x4, waiting for transfers between devices: 6.19 us -> 0.98 us  [far_both(): lax.ppermute(value, ('expert', 'sub'), [(i, 3 - i) for i in range(4)])]
    ppermute x12 -> x11, waiting for transfers between devices: 17.5 us -> 21.4 us  [across(): lax.ppermute(value, 'tensor', [(i, i ^ distance) for i in range(lax.axis_...]
    convert_element_type x2 -> x1, other arithmetic: 2.4 us -> 0.1 us  [sum_x(): jnp.where(place.high, own_half, other_half).astype(BF16)]
    ppermute x12 -> x11, starting transfers between devices: 24.2 us -> 24.9 us  [across(): lax.ppermute(value, 'tensor', [(i, i ^ distance) for i in range(lax.axis_...]
  transfers between devices with their start and end apart: 35 -> 34, of which waited for: 13 -> 13; matrix products, arithmetic and copies ran while one was open for 3% -> 3% of each run, Pallas kernels for 47% -> 50%
where the time goes in v4:
time: 176 us; the launch traced here: 174 us
  Pallas kernels  86.3 us (49%)
  starting transfers between devices  41 us (23%)
  waiting for transfers between devices  36.4 us (21%)
  other arithmetic  9.37 us (5%)
    pallas_call x6, Pallas kernels, call(): pl.pallas_call(body, grid=(steps,), in_specs=[*map(whole, routes), *[anyw...  86.3 us
    ppermute x11, starting transfers between devices, across(): lax.ppermute(value, 'tensor', [(i, i ^ distance) for i in range(lax.axis_...  24.9 us
    ppermute x11, waiting for transfers between devices, across(): lax.ppermute(value, 'tensor', [(i, i ^ distance) for i in range(lax.axis_...  21.4 us
    ppermute x19, waiting for transfers between devices, swap(): return lax.ppermute(value, axis, [(0, 1), (1, 0)])  14.1 us
    ppermute x19, starting transfers between devices, swap(): return lax.ppermute(value, axis, [(0, 1), (1, 0)])  12.3 us
    ppermute x4, starting transfers between devices, far_both(): lax.ppermute(value, ('expert', 'sub'), [(i, 3 - i) for i in range(4)])  3.78 us
  transfers between devices with their start and end apart: 34, of which 13 were waited for; matrix products, arithmetic and copies ran while one was open for 3% of the time, Pallas kernels for 50%

profile of v4, /device:TPU:0, one launch (start us, length us, event | category | flops | bytes accessed | tf_op | source)
XLA Modules:
  0.0 174.0 jit_solution(1184763878990363207)
XLA Ops:
  2.6 4.6 %collective-permute-start = (bf16[128,768]{1,0:T(8,128)(2,1)}, bf16[128,768]{1,0:T(8,128)(2,1)S(1)}, u32[]{:S(2)}, u32[]{:S(2)}) collective-permute-start(bf16[128,768]{1,0:T(8,128)(2,1)} %param.7), channel_id=1, source_target_pairs={{0,12},{4,8},{8,4},{12,0},{1,13},{5,9},{9,5},{13,1},{2,14},{6,10},... | collective-permute-start | bytes 589832 | tf_op jit(solution)/shard_map/ppermute | solution.py:26
  7.9 1.6 collective-permute-start.2
  9.9 1.6 collective-permute-done.2
  11.5 1.7 collective-permute-done
  13.2 1.6 collective-permute-start.5
  14.8 3.5 %collective-permute-done.6 = bf16[128,768]{1,0:T(8,128)(2,1)S(1)} collective-permute-done((bf16[128,768]{1,0:T(8,128)(2,1)}, bf16[128,768]{1,0:T(8,128)(2,1)S(1)}, u32[]{:S(2)}, u32[]{:S(2)}) %collective-permute-start.6) | collective-permute-done | bytes 196640 | tf_op jit(solution)/shard_map/ppermute | solution.py:26
  18.3 1.5 collective-permute-start.8
  19.8 5.0 %collective-permute-done.3 = bf16[128,768]{1,0:T(8,128)(2,1)S(1)} collective-permute-done((bf16[128,768]{1,0:T(8,128)(2,1)}, bf16[128,768]{1,0:T(8,128)(2,1)S(1)}, u32[]{:S(2)}, u32[]{:S(2)}) %collective-permute-start.3) | collective-permute-done | bytes 196640 | tf_op jit(solution)/shard_map/ppermute | solution.py:26
  24.8 1.5 collective-permute-start.4
  26.3 5.0 %collective-permute-done.4 = bf16[128,768]{1,0:T(8,128)(2,1)S(1)} collective-permute-done((bf16[128,768]{1,0:T(8,128)(2,1)S(1)}, bf16[128,768]{1,0:T(8,128)(2,1)S(1)}, u32[]{:S(2)}, u32[]{:S(2)}) %collective-permute-start.4) | collective-permute-done | bytes 196640 | tf_op jit(solution)/shard_map/ppermute | solution.py:22
  33.1 2.5 %collective-permute-start.11 = (bf16[128,768]{1,0:T(8,128)(2,1)}, bf16[128,768]{1,0:T(8,128)(2,1)S(1)}, u32[]{:S(2)}, u32[]{:S(2)}) collective-permute-start(bf16[128,768]{1,0:T(8,128)(2,1)} %param.8), channel_id=1, source_target_pairs={{0,8},{4,12},{8,0},{12,4},{1,9},{5,13},{9,1},{13,5},{2,10},{6,14},... | collective-permute-start | bytes 589832 | tf_op jit(solution)/shard_map/ppermute | solution.py:26
  37.0 13.0 %shard_map.86 = (bf16[2,320,4096]{2,1,0:T(8,128)(2,1)}, bf16[2,4,80,128]{3,2,1,0:T(8,128)(2,1)S(1)}, f32[2,320,1]{2,1,0:T(8,128)S(1)}) custom-call(f32[4,8,128]{2,1,0:T(8,128)S(1)} %pad_maximum_fusion.5.refs_0_, bf16[4,128,768]{2,1,0:T(8,128)(2,1)S(1)} %get-tuple-element.77.refs_1_.refs_3_, bf16[4,128,768]{2,1,0:T(8,128)(2,1)S(1)} %collective-permute-done.9.refs_2_.refs_4_, ...), custom_call_target="tpu_custom_call" | custom-call | flops 1000 | bytes 1000 | tf_op jit(solution)/shard_map/pallas_call | solution.py:335
  51.4 1.6 collective-permute-start.15
  53.6 12.5 %shard_map.88.refs_5_ = bf16[2,320,4096]{2,1,0:T(8,128)(2,1)} custom-call(bf16[2,4,80,128]{3,2,1,0:T(8,128)(2,1)S(1)} %get-tuple-element.40.take_ref.refs_0_, bf16[2,128,768]{2,1,0:T(8,128)(2,1)} %get-tuple-element.81.refs_0_.refs_1_, bf16[2,128,768]{2,1,0:T(8,128)(2,1)} %get-tuple-element.80.refs_2_, ...), custom_call_target="tpu_custom_call" | custom-call | flops 201326592000 | bytes 1000 | tf_op jit(solution)/shard_map/pallas_call | solution.py:335
  66.4 5.2 %collective-permute-done.14.refs_2_ = bf16[2,128,768]{2,1,0:T(8,128)(2,1)} collective-permute-done((bf16[2,128,768]{2,1,0:T(8,128)(2,1)}, bf16[2,128,768]{2,1,0:T(8,128)(2,1)}, u32[]{:S(2)}, u32[]{:S(2)}) %collective-permute-start.14) | collective-permute-done | bytes 393248 | tf_op jit(solution)/shard_map/ppermute | solution.py:22
  71.6 15.8 %shard_map.87 = (bf16[2,320,4096]{2,1,0:T(8,128)(2,1)}, bf16[320,4096]{1,0:T(8,128)(2,1)}, bf16[320,1536]{1,0:T(8,128)(2,1)S(1)}) custom-call(bf16[2,4,80,128]{3,2,1,0:T(8,128)(2,1)S(1)} %get-tuple-element.40.take_ref.refs_0_, f32[2,320,1]{2,1,0:T(8,128)S(1)} %get-tuple-element.41.gate_ref, bf16[2,128,768]{2,1,0:T(8,128)(2,1)} %get-tuple-element.81.refs_0_.refs_1_, ...), custom_call_target="tpu_custom_call" | custom-call | flops 201326592000 | bytes 1000 | tf_op jit(solution)/shard_map/pallas_call | solution.py:335
  87.5 17.4 %shard_map.89 = (bf16[2,320,4096]{2,1,0:T(8,128)(2,1)}, bf16[320,4096]{1,0:T(8,128)(2,1)}, bf16[128,1536]{1,0:T(8,128)(2,1)S(1)}, bf16[128,1536]{1,0:T(8,128)(2,...) custom-call(bf16[2,4,80,128]{3,2,1,0:T(8,128)(2,1)S(1)} %get-tuple-element.40.take_ref.refs_0_, ...), custom_call_target="tpu_custom_call" | custom-call | flops 201326592000 | bytes 1000 | tf_op jit(solution)/shard_map/pallas_call | solution.py:335
  105.5 1.5 collective-permute-start.19
  107.3 13.2 %shard_map.90.refs_0_ = bf16[320,1536]{1,0:T(8,128)(2,1)S(1)} custom-call(bf16[2,4,80,128]{3,2,1,0:T(8,128)(2,1)S(1)} %get-tuple-element.40.take_ref.refs_0_, f32[2,320,1]{2,1,0:T(8,128)S(1)} %get-tuple-element.41.gate_ref, bf16[320,4096]{1,0:T(8,128)(2,1)} %get-tuple-element.53.refs_0_, bf16[320,4096]{1,0:T(8,128)(2,1)} %collective-permute-done.21.refs_1_, ...), custom_call_target="tpu_custom_call" | custom-call | flops 201326592000 | bytes 1000 | tf_op jit(solution)/shard_map/pallas_call | solution.py:335
  120.5 14.3 %shard_map.91 = (bf16[128,768]{1,0:T(8,128)(2,1)S(1)}, bf16[128,768]{1,0:T(8,128)(2,1)S(1)}, bf16[128,768]{1,0:T(8,128)(2,1)S(1)}, bf16[128,768]{1,0:T(8,128)(2,...) custom-call(bf16[2,4,80,128]{3,2,1,0:T(8,128)(2,1)S(1)} %get-tuple-e, ...), custom_call_target="tpu_custom_call" | custom-call | flops 201326592000 | bytes 1000 | tf_op jit(solution)/shard_map/pallas_call | solution.py:335
  134.9 1.5 collective-permute-start.29
  137.1 1.5 fusion.3
  138.7 4.1 %collective-permute-start.23 = (bf16[2,128,768]{2,1,0:T(8,128)(2,1)S(1)}, bf16[2,128,768]{2,1,0:T(8,128)(2,1)S(1)}, u32[]{:S(2)}, u32[]{:S(2)}) collective-permute-start(bf16[2,128,768]{2,1,0:T(8,128)(2,1)S(1)} %pad_maximum_fusion.4), channel_id=1, source_target_pairs={{0,4},{4,0},{8,12},{12,8},{1,5},{5,1},{9,13},{13,9},{2,6},{6,2},{1... | collective-permute-start | bytes 1179656 | tf_op jit(solution)/shard_map/ppermute | solution.py:26
  142.8 1.5 collective-permute-start.25
  144.6 2.2 %collective-permute-done.30 = bf16[128,768]{1,0:T(8,128)(2,1)S(1)} collective-permute-done((bf16[128,768]{1,0:T(8,128)(2,1)S(1)}, bf16[128,768]{1,0:T(8,128)(2,1)S(1)}, u32[]{:S(2)}, u32[]{:S(2)}) %collective-permute-start.30) | collective-permute-done | bytes 196640 | tf_op jit(solution)/shard_map/ppermute | solution.py:22
  147.0 5.1 %collective-permute-start.31 = (bf16[128,768]{1,0:T(8,128)(2,1)S(1)}, bf16[128,768]{1,0:T(8,128)(2,1)S(1)}, u32[]{:S(2)}, u32[]{:S(2)}) collective-permute-start(bf16[128,768]{1,0:T(8,128)(2,1)S(1)} %select_convert_fusion.2), channel_id=1, source_target_pairs={{0,8},{4,12},{8,0},{12,4},{1,9},{5,13},{9,1},{13,5},{2,10},{6,14},... | collective-permute-start | bytes 589832 | tf_op jit(solution)/shard_map/ppermute | solution.py:26
  154.4 3.8 %collective-permute-start.27 = (bf16[128,768]{1,0:T(8,128)(2,1)S(1)}, bf16[128,768]{1,0:T(8,128)(2,1)S(1)}, u32[]{:S(2)}, u32[]{:S(2)}) collective-permute-start(bf16[128,768]{1,0:T(8,128)(2,1)S(1)} %fusion), channel_id=1, source_target_pairs={{0,12},{4,8},{8,4},{12,0},{1,13},{5,9},{9,5},{13,1},{2,14},{6,10},... | collective-permute-start | bytes 589832 | tf_op jit(solution)/shard_map/ppermute | solution.py:26
  158.4 2.2 %collective-permute-start.32 = (bf16[128,768]{1,0:T(8,128)(2,1)S(1)}, bf16[128,768]{1,0:T(8,128)(2,1)S(1)}, u32[]{:S(2)}, u32[]{:S(2)}) collective-permute-start(bf16[128,768]{1,0:T(8,128)(2,1)S(1)} %get-tuple-element.78), channel_id=1, source_target_pairs={{0,4},{4,0},{8,12},{12,8},{1,5},{5,1},{9,13},{13,9},{2,6},{6,2},{1... | collective-permute-start | bytes 589832 | tf_op jit(solution)/shard_map/ppermute | solution.py:26
  160.6 3.5 %collective-permute-done.27 = bf16[128,768]{1,0:T(8,128)(2,1)S(1)} collective-permute-done((bf16[128,768]{1,0:T(8,128)(2,1)S(1)}, bf16[128,768]{1,0:T(8,128)(2,1)S(1)}, u32[]{:S(2)}, u32[]{:S(2)}) %collective-permute-start.27) | collective-permute-done | bytes 196640 | tf_op jit(solution)/shard_map/ppermute | solution.py:26
  164.1 2.0 %fusion.2 = bf16[128,768]{1,0:T(8,128)(2,1)} fusion(bf16[128,768]{1,0:T(8,128)(2,1)S(1)} %collective-permute-done.27, bf16[2,128,768]{2,1,0:T(8,128)(2,1)S(1)} %collective-permute-done.23, pred[]{:T(512)S(6)} %eq.5, bf16[128,1536]{1,0:T(8,128)(2,1)} %collective-permute-done.19, bf16[128,1536]{1,0:T(8,128)(2,1)S(1)} %get-tuple-element.60, ...), kind=kLoop, calls=%fused_computation.11 | loop fusion | flops 1376256 | bytes 1376257 | tf_op jit(solution)/shard_map/convert_element_type | solution.py:129
  166.0 3.9 %collective-permute-done.31 = bf16[128,768]{1,0:T(8,128)(2,1)S(1)} collective-permute-done((bf16[128,768]{1,0:T(8,128)(2,1)S(1)}, bf16[128,768]{1,0:T(8,128)(2,1)S(1)}, u32[]{:S(2)}, u32[]{:S(2)}) %collective-permute-start.31) | collective-permute-done | bytes 196640 | tf_op jit(solution)/shard_map/ppermute | solution.py:26
  170.0 3.2 %collective-permute-done.32 = bf16[128,768]{1,0:T(8,128)(2,1)S(1)} collective-permute-done((bf16[128,768]{1,0:T(8,128)(2,1)S(1)}, bf16[128,768]{1,0:T(8,128)(2,1)S(1)}, u32[]{:S(2)}, u32[]{:S(2)}) %collective-permute-start.32) | collective-permute-done | bytes 196640 | tf_op jit(solution)/shard_map/ppermute | solution.py:26
  (59 shorter events, 14.1 us)
Async XLA Ops:
  2.1 5.7 %collective-permute-start.1 = (f32[8,128]{1,0:T(8,128)S(1)}, f32[8,128]{1,0:T(8,128)S(1)}, u32[]{:S(2)}, u32[]{:S(2)}) collective-permute-start(f32[8,128]{1,0:T(8,128)S(1)} %get-tuple-element.83), channel_id=1, source_target_pairs={{0,1},{1,0},{2,3},{3,2},{4,5},{5,4},{6,7},{7,6},{8,9},{9,8},{10,11... | collective-permute-start | bytes 12296 | tf_op jit(solution)/shard_map/ppermute | solution.py:22
  2.6 10.6 %collective-permute-start = (bf16[128,768]{1,0:T(8,128)(2,1)}, bf16[128,768]{1,0:T(8,128)(2,1)S(1)}, u32[]{:S(2)}, u32[]{:S(2)}) collective-permute-start(bf16[128,768]{1,0:T(8,128)(2,1)} %param.7), channel_id=1, source_target_pairs={{0,12},{4,8},{8,4},{12,0},{1,13},{5,9},{9,5},{13,1},{2,14},{6,10},... | collective-permute-start | bytes 589832 | tf_op jit(solution)/shard_map/ppermute | solution.py:26
  7.2 11.1 %collective-permute-start.6 = (bf16[128,768]{1,0:T(8,128)(2,1)}, bf16[128,768]{1,0:T(8,128)(2,1)S(1)}, u32[]{:S(2)}, u32[]{:S(2)}) collective-permute-start(bf16[128,768]{1,0:T(8,128)(2,1)} %param.7), channel_id=1, source_target_pairs={{0,4},{4,0},{8,12},{12,8},{1,5},{5,1},{9,13},{13,9},{2,6},{6,2},{1... | collective-permute-start | bytes 589832 | tf_op jit(solution)/shard_map/ppermute | solution.py:26
  7.2 17.6 %collective-permute-start.3 = (bf16[128,768]{1,0:T(8,128)(2,1)}, bf16[128,768]{1,0:T(8,128)(2,1)S(1)}, u32[]{:S(2)}, u32[]{:S(2)}) collective-permute-start(bf16[128,768]{1,0:T(8,128)(2,1)} %param.7), channel_id=1, source_target_pairs={{0,8},{4,12},{8,0},{12,4},{1,9},{5,13},{9,1},{13,5},{2,10},{6,14},... | collective-permute-start | bytes 589832 | tf_op jit(solution)/shard_map/ppermute | solution.py:26
  9.5 16.8 %collective-permute-start.7 = (bf16[128,768]{1,0:T(8,128)(2,1)}, bf16[128,768]{1,0:T(8,128)(2,1)S(1)}, u32[]{:S(2)}, u32[]{:S(2)}) collective-permute-start(bf16[128,768]{1,0:T(8,128)(2,1)} %param.7), channel_id=1, source_target_pairs={{0,2},{2,0},{1,3},{3,1},{4,6},{6,4},{5,7},{7,5},{8,10},{10,8},{9,1... | collective-permute-start | bytes 589832 | tf_op jit(solution)/shard_map/ppermute | solution.py:22
  13.2 13.0 %collective-permute-start.5 = (bf16[128,768]{1,0:T(8,128)(2,1)S(1)}, bf16[128,768]{1,0:T(8,128)(2,1)S(1)}, u32[]{:S(2)}, u32[]{:S(2)}) collective-permute-start(bf16[128,768]{1,0:T(8,128)(2,1)S(1)} %collective-permute-done), channel_id=1, source_target_pairs={{0,2},{2,0},{1,3},{3,1},{4,6},{6,4},{5,7},{7,5},{8,10},{10,8},{9,1... | collective-permute-start | bytes 589832 | tf_op jit(solution)/shard_map/ppermute | solution.py:22
  18.3 8.0 %collective-permute-start.8 = (bf16[128,768]{1,0:T(8,128)(2,1)S(1)}, bf16[128,768]{1,0:T(8,128)(2,1)S(1)}, u32[]{:S(2)}, u32[]{:S(2)}) collective-permute-start(bf16[128,768]{1,0:T(8,128)(2,1)S(1)} %collective-permute-done.6), channel_id=1, source_target_pairs={{0,2},{2,0},{1,3},{3,1},{4,6},{6,4},{5,7},{7,5},{8,10},{10,8},{9,1... | collective-permute-start | bytes 589832 | tf_op jit(solution)/shard_map/ppermute | solution.py:22
  24.8 6.5 %collective-permute-start.4 = (bf16[128,768]{1,0:T(8,128)(2,1)S(1)}, bf16[128,768]{1,0:T(8,128)(2,1)S(1)}, u32[]{:S(2)}, u32[]{:S(2)}) collective-permute-start(bf16[128,768]{1,0:T(8,128)(2,1)S(1)} %collective-permute-done.3), channel_id=1, source_target_pairs={{0,2},{2,0},{1,3},{3,1},{4,6},{6,4},{5,7},{7,5},{8,10},{10,8},{9,1... | collective-permute-start | bytes 589832 | tf_op jit(solution)/shard_map/ppermute | solution.py:22
  32.5 17.5 %collective-permute-start.10 = (bf16[128,768]{1,0:T(8,128)(2,1)}, bf16[128,768]{1,0:T(8,128)(2,1)S(1)}, u32[]{:S(2)}, u32[]{:S(2)}) collective-permute-start(bf16[128,768]{1,0:T(8,128)(2,1)} %param.8), channel_id=1, source_target_pairs={{0,4},{4,0},{8,12},{12,8},{1,5},{5,1},{9,13},{13,9},{2,6},{6,2},{1... | collective-permute-start | bytes 589832 | tf_op jit(solution)/shard_map/ppermute | solution.py:26
  33.1 17.3 %collective-permute-start.11 = (bf16[128,768]{1,0:T(8,128)(2,1)}, bf16[128,768]{1,0:T(8,128)(2,1)S(1)}, u32[]{:S(2)}, u32[]{:S(2)}) collective-permute-start(bf16[128,768]{1,0:T(8,128)(2,1)} %param.8), channel_id=1, source_target_pairs={{0,8},{4,12},{8,0},{12,4},{1,9},{5,13},{9,1},{13,5},{2,10},{6,14},... | collective-permute-start | bytes 589832 | tf_op jit(solution)/shard_map/ppermute | solution.py:26
  35.7 14.8 %collective-permute-start.12 = (bf16[128,768]{1,0:T(8,128)(2,1)}, bf16[128,768]{1,0:T(8,128)(2,1)S(1)}, u32[]{:S(2)}, u32[]{:S(2)}) collective-permute-start(bf16[128,768]{1,0:T(8,128)(2,1)} %param.8), channel_id=1, source_target_pairs={{0,12},{4,8},{8,4},{12,0},{1,13},{5,9},{9,5},{13,1},{2,14},{6,10},... | collective-permute-start | bytes 589832 | tf_op jit(solution)/shard_map/ppermute | solution.py:26
  51.4 15.0 %collective-permute-start.13 = (bf16[2,128,768]{2,1,0:T(8,128)(2,1)}, bf16[2,128,768]{2,1,0:T(8,128)(2,1)}, u32[]{:S(2)}, u32[]{:S(2)}) collective-permute-start(bf16[2,128,768]{2,1,0:T(8,128)(2,1)} %get-tuple-element.80.refs_2_), channel_id=1, source_target_pairs={{0,1},{1,0},{2,3},{3,2},{4,5},{5,4},{6,7},{7,6},{8,9},{9,8},{10,11... | collective-permute-start | bytes 1179656 | tf_op jit(solution)/shard_map/ppermute | solution.py:22
  51.4 20.2 %collective-permute-start.15 = (bf16[2,128,768]{2,1,0:T(8,128)(2,1)}, bf16[2,128,768]{2,1,0:T(8,128)(2,1)}, u32[]{:S(2)}, u32[]{:S(2)}) collective-permute-start(bf16[2,128,768]{2,1,0:T(8,128)(2,1)} %get-tuple-element.80.refs_2_), channel_id=1, source_target_pairs={{0,3},{1,2},{2,1},{3,0},{4,7},{5,6},{6,5},{7,4},{8,11},{9,10},{10,... | collective-permute-start | bytes 1179656 | tf_op jit(solution)/shard_map/ppermute | solution.py:61
  53.0 18.6 %collective-permute-start.16 = (bf16[2,320,4096]{2,1,0:T(8,128)(2,1)}, bf16[2,320,4096]{2,1,0:T(8,128)(2,1)}, u32[]{:S(2)}, u32[]{:S(2)}) collective-permute-start(bf16[2,320,4096]{2,1,0:T(8,128)(2,1)} %get-tuple-element.43.refs_4_), channel_id=1, source_target_pairs={{0,1},{1,0},{2,3},{3,2},{4,5},{5,4},{6,7},{7,6},{8,9},{9,8},{10,11... | collective-permute-start | bytes 15728648 | tf_op jit(solution)/shard_map/ppermute | solution.py:22
  53.0 18.6 %collective-permute-start.14 = (bf16[2,128,768]{2,1,0:T(8,128)(2,1)}, bf16[2,128,768]{2,1,0:T(8,128)(2,1)}, u32[]{:S(2)}, u32[]{:S(2)}) collective-permute-start(bf16[2,128,768]{2,1,0:T(8,128)(2,1)} %get-tuple-element.81.refs_0_.refs_1_), channel_id=1, source_target_pairs={{0,2},{2,0},{1,3},{3,1},{4,6},{6,4},{5,7},{7,5},{8,10},{10,8},{9,1... | collective-permute-start | bytes 1179656 | tf_op jit(solution)/shard_map/ppermute | solution.py:22
  66.1 21.4 %collective-permute-start.17 = (bf16[2,320,4096]{2,1,0:T(8,128)(2,1)}, bf16[2,320,4096]{2,1,0:T(8,128)(2,1)}, u32[]{:S(2)}, u32[]{:S(2)}) collective-permute-start(bf16[2,320,4096]{2,1,0:T(8,128)(2,1)} %shard_map.88.refs_5_), channel_id=1, source_target_pairs={{0,1},{1,0},{2,3},{3,2},{4,5},{5,4},{6,7},{7,6},{8,9},{9,8},{10,11... | collective-permute-start | bytes 15728648 | tf_op jit(solution)/shard_map/ppermute | solution.py:22
  87.4 19.9 %collective-permute-start.21 = (bf16[320,4096]{1,0:T(8,128)(2,1)}, bf16[320,4096]{1,0:T(8,128)(2,1)}, u32[]{:S(2)}, u32[]{:S(2)}) collective-permute-start(bf16[320,4096]{1,0:T(8,128)(2,1)} %get-tuple-element.53.refs_0_), channel_id=1, source_target_pairs={{0,1},{1,0},{2,3},{3,2},{4,5},{5,4},{6,7},{7,6},{8,9},{9,8},{10,11... | collective-permute-start | bytes 7864328 | tf_op jit(solution)/shard_map/ppermute | solution.py:22
  104.9 15.7 %collective-permute-start.22 = (bf16[320,4096]{1,0:T(8,128)(2,1)}, bf16[320,4096]{1,0:T(8,128)(2,1)}, u32[]{:S(2)}, u32[]{:S(2)}) collective-permute-start(bf16[320,4096]{1,0:T(8,128)(2,1)} %get-tuple-element.55.refs_1_), channel_id=1, source_target_pairs={{0,1},{1,0},{2,3},{3,2},{4,5},{5,4},{6,7},{7,6},{8,9},{9,8},{10,11... | collective-permute-start | bytes 7864328 | tf_op jit(solution)/shard_map/ppermute | solution.py:22
  105.4 29.5 %collective-permute-start.18 = (bf16[128,1536]{1,0:T(8,128)(2,1)}, bf16[128,1536]{1,0:T(8,128)(2,1)}, u32[]{:S(2)}, u32[]{:S(2)}) collective-permute-start(bf16[128,1536]{1,0:T(8,128)(2,1)} %get-tuple-element.50), channel_id=1, source_target_pairs={{0,1},{1,0},{2,3},{3,2},{4,5},{5,4},{6,7},{7,6},{8,9},{9,8},{10,11... | collective-permute-start | bytes 1179656 | tf_op jit(solution)/shard_map/ppermute | solution.py:22
  105.5 29.4 %collective-permute-start.19 = (bf16[128,1536]{1,0:T(8,128)(2,1)}, bf16[128,1536]{1,0:T(8,128)(2,1)}, u32[]{:S(2)}, u32[]{:S(2)}) collective-permute-start(bf16[128,1536]{1,0:T(8,128)(2,1)} %get-tuple-element.51), channel_id=1, source_target_pairs={{0,2},{2,0},{1,3},{3,1},{4,6},{6,4},{5,7},{7,5},{8,10},{10,8},{9,1... | collective-permute-start | bytes 1179656 | tf_op jit(solution)/shard_map/ppermute | solution.py:22
  107.0 27.9 %collective-permute-start.20 = (bf16[128,1536]{1,0:T(8,128)(2,1)}, bf16[128,1536]{1,0:T(8,128)(2,1)}, u32[]{:S(2)}, u32[]{:S(2)}) collective-permute-start(bf16[128,1536]{1,0:T(8,128)(2,1)} %get-tuple-element.52), channel_id=1, source_target_pairs={{0,3},{1,2},{2,1},{3,0},{4,7},{5,6},{6,5},{7,4},{8,11},{9,10},{10,... | collective-permute-start | bytes 1179656 | tf_op jit(solution)/shard_map/ppermute | solution.py:61
  134.9 7.9 %collective-permute-start.29 = (bf16[128,768]{1,0:T(8,128)(2,1)S(1)}, bf16[128,768]{1,0:T(8,128)(2,1)S(1)}, u32[]{:S(2)}, u32[]{:S(2)}) collective-permute-start(bf16[128,768]{1,0:T(8,128)(2,1)S(1)} %get-tuple-element.68), channel_id=1, source_target_pairs={{0,3},{1,2},{2,1},{3,0},{4,7},{5,6},{6,5},{7,4},{8,11},{9,10},{10,... | collective-permute-start | bytes 589832 | tf_op jit(solution)/shard_map/ppermute | solution.py:61
  136.4 7.9 %collective-permute-start.28 = (bf16[128,768]{1,0:T(8,128)(2,1)S(1)}, bf16[128,768]{1,0:T(8,128)(2,1)S(1)}, u32[]{:S(2)}, u32[]{:S(2)}) collective-permute-start(bf16[128,768]{1,0:T(8,128)(2,1)S(1)} %get-tuple-element.67), channel_id=1, source_target_pairs={{0,1},{1,0},{2,3},{3,2},{4,5},{5,4},{6,7},{7,6},{8,9},{9,8},{10,11... | collective-permute-start | bytes 589832 | tf_op jit(solution)/shard_map/ppermute | solution.py:22
  136.6 10.3 %collective-permute-start.30 = (bf16[128,768]{1,0:T(8,128)(2,1)S(1)}, bf16[128,768]{1,0:T(8,128)(2,1)S(1)}, u32[]{:S(2)}, u32[]{:S(2)}) collective-permute-start(bf16[128,768]{1,0:T(8,128)(2,1)S(1)} %get-tuple-element.69), channel_id=1, source_target_pairs={{0,2},{2,0},{1,3},{3,1},{4,6},{6,4},{5,7},{7,5},{8,10},{10,8},{9,1... | collective-permute-start | bytes 589832 | tf_op jit(solution)/shard_map/ppermute | solution.py:22
  138.7 13.4 %collective-permute-start.23 = (bf16[2,128,768]{2,1,0:T(8,128)(2,1)S(1)}, bf16[2,128,768]{2,1,0:T(8,128)(2,1)S(1)}, u32[]{:S(2)}, u32[]{:S(2)}) collective-permute-start(bf16[2,128,768]{2,1,0:T(8,128)(2,1)S(1)} %pad_maximum_fusion.4), channel_id=1, source_target_pairs={{0,4},{4,0},{8,12},{12,8},{1,5},{5,1},{9,13},{13,9},{2,6},{6,2},{1... | collective-permute-start | bytes 1179656 | tf_op jit(solution)/shard_map/ppermute | solution.py:26
  142.8 10.6 %collective-permute-start.24 = (bf16[128,768]{1,0:T(8,128)(2,1)S(1)}, bf16[128,768]{1,0:T(8,128)(2,1)S(1)}, u32[]{:S(2)}, u32[]{:S(2)}) collective-permute-start(bf16[128,768]{1,0:T(8,128)(2,1)S(1)} %get-tuple-element.63), channel_id=1, source_target_pairs={{0,1},{1,0},{2,3},{3,2},{4,5},{5,4},{6,7},{7,6},{8,9},{9,8},{10,11... | collective-permute-start | bytes 589832 | tf_op jit(solution)/shard_map/ppermute | solution.py:22
  142.8 10.6 %collective-permute-start.25 = (bf16[128,768]{1,0:T(8,128)(2,1)S(1)}, bf16[128,768]{1,0:T(8,128)(2,1)S(1)}, u32[]{:S(2)}, u32[]{:S(2)}) collective-permute-start(bf16[128,768]{1,0:T(8,128)(2,1)S(1)} %get-tuple-element.64), channel_id=1, source_target_pairs={{0,2},{2,0},{1,3},{3,1},{4,6},{6,4},{5,7},{7,5},{8,10},{10,8},{9,1... | collective-permute-start | bytes 589832 | tf_op jit(solution)/shard_map/ppermute | solution.py:22
  144.3 10.1 %collective-permute-start.26 = (bf16[128,768]{1,0:T(8,128)(2,1)S(1)}, bf16[128,768]{1,0:T(8,128)(2,1)S(1)}, u32[]{:S(2)}, u32[]{:S(2)}) collective-permute-start(bf16[128,768]{1,0:T(8,128)(2,1)S(1)} %get-tuple-element.65), channel_id=1, source_target_pairs={{0,3},{1,2},{2,1},{3,0},{4,7},{5,6},{6,5},{7,4},{8,11},{9,10},{10,... | collective-permute-start | bytes 589832 | tf_op jit(solution)/shard_map/ppermute | solution.py:61
  147.0 23.0 %collective-permute-start.31 = (bf16[128,768]{1,0:T(8,128)(2,1)S(1)}, bf16[128,768]{1,0:T(8,128)(2,1)S(1)}, u32[]{:S(2)}, u32[]{:S(2)}) collective-permute-start(bf16[128,768]{1,0:T(8,128)(2,1)S(1)} %select_convert_fusion.2), channel_id=1, source_target_pairs={{0,8},{4,12},{8,0},{12,4},{1,9},{5,13},{9,1},{13,5},{2,10},{6,14},... | collective-permute-start | bytes 589832 | tf_op jit(solution)/shard_map/ppermute | solution.py:26
  154.4 9.7 %collective-permute-start.27 = (bf16[128,768]{1,0:T(8,128)(2,1)S(1)}, bf16[128,768]{1,0:T(8,128)(2,1)S(1)}, u32[]{:S(2)}, u32[]{:S(2)}) collective-permute-start(bf16[128,768]{1,0:T(8,128)(2,1)S(1)} %fusion), channel_id=1, source_target_pairs={{0,12},{4,8},{8,4},{12,0},{1,13},{5,9},{9,5},{13,1},{2,14},{6,10},... | collective-permute-start | bytes 589832 | tf_op jit(solution)/shard_map/ppermute | solution.py:26
  158.3 11.6 %collective-permute-start.33 = (bf16[128,768]{1,0:T(8,128)(2,1)S(1)}, bf16[128,768]{1,0:T(8,128)(2,1)S(1)}, u32[]{:S(2)}, u32[]{:S(2)}) collective-permute-start(bf16[128,768]{1,0:T(8,128)(2,1)S(1)} %get-tuple-element.79), channel_id=1, source_target_pairs={{0,12},{4,8},{8,4},{12,0},{1,13},{5,9},{9,5},{13,1},{2,14},{6,10},... | collective-permute-start | bytes 589832 | tf_op jit(solution)/shard_map/ppermute | solution.py:26
  158.4 14.7 %collective-permute-start.32 = (bf16[128,768]{1,0:T(8,128)(2,1)S(1)}, bf16[128,768]{1,0:T(8,128)(2,1)S(1)}, u32[]{:S(2)}, u32[]{:S(2)}) collective-permute-start(bf16[128,768]{1,0:T(8,128)(2,1)S(1)} %get-tuple-element.78), channel_id=1, source_target_pairs={{0,4},{4,0},{8,12},{12,8},{1,5},{5,1},{9,13},{13,9},{2,6},{6,2},{1... | collective-permute-start | bytes 589832 | tf_op jit(solution)/shard_map/ppermute | solution.py:26
  (3 other events, 21.7 us)

commit v5 on v4

--- a/solution.py
+++ b/solution.py
@@ -160,7 +160,8 @@
             take = jnp.where(jnp.where(one | two, rank[0:1], -1.0) == slot, 1.0, 0.0)
             gate = jnp.where(one, meta[2:3], 0.0) + jnp.where(two, meta[3:4], 0.0)
             take_ref[local, place_at] = take.astype(BF16)
-            gate_ref[local, pl.ds(start, CAP), :] = jnp.sum(take * gate, axis=1, keepdims=True)
+            weight = jnp.sum(take * gate, axis=1, keepdims=True)
+            gate_ref[local, pl.ds(start, CAP), :] = jnp.broadcast_to(weight, (CAP, 128))
 
 
 def place_rows(small, index, take_ref, local, groups, places, rows_ref):
@@ -182,16 +183,14 @@
     places = len(outs) * width // half
     for place_at in range(places):
         start = block_at(small, index, place_at)[1]
+        takes = jnp.concatenate([take_ref[local, place_at] for local in range(len(slots_of))])
         for chunk in range(chunks):
             span = half // chunks
             column = pl.multiple_of(other(lax.rem(index[2], 2), chunk) * span, 128) if small else 0
-            total = None
-            for local, slots in enumerate(slots_of):
-                term = lax.dot_general(
-                    take_ref[local, place_at], slots[pl.ds(start, CAP), pl.ds(column, span)],
-                    (((0,), (0,)), ((), ())), preferred_element_type=F32,
-                )
-                total = term if total is None else total + term
+            total = lax.dot_general(
+                takes, jnp.concatenate([slots[pl.ds(start, CAP), pl.ds(column, span)] for slots in slots_of]),
+                (((0,), (0,)), ((), ())), preferred_element_type=F32,
+            )
             if width == half:
                 outs[place_at][:, chunk * span : (chunk + 1) * span] = total.astype(BF16)
             else:
@@ -239,26 +238,27 @@
     return slice(None), cut
 
 
-def first_body(small, local, locals_, places, n_routes, n_after, tile, steps, *refs):
-    routes, refs = refs[:n_routes], refs[n_routes + n_after :]
+def first_body(small, local, locals_, places, tile, steps, start_late, wait_early, wait_late, route, *refs):
     groups, (gate_w, up_w, out, *routed, rows, gate_ring, up_ring, sems) = refs[: len(places)], refs[len(places) :]
-    take_ref = routes[0] if local else routed[0]
+    take_ref = route if local else routed[0]
     stream = Stream([gate_w, up_w], [column_tile(local)] * 2, tile, [gate_ring, up_ring], sems)
     step = pl.program_id(0)
 
     @pl.when(step == 0)
     def _():
         stream.start(steps)
+        start_late()
+        wait_early()
         if not local:
-            route_rows(small, locals_, axis_indices(), *routes, *routed)
+            route_rows(small, locals_, axis_indices(), route, *routed)
         place_rows(small, axis_indices(), take_ref, local, groups, places, rows)
 
     for i, weight in enumerate(stream.take(step)):
         out[i] = jnp.dot(rows[...], weight[...], preferred_element_type=F32).astype(BF16)
 
 
-def middle_body(small, local, locals_, places, tile, steps, take_ref, gate_ref, *refs):
-    groups, refs = refs[: len(places)], refs[len(places) :]
+def middle_body(small, local, locals_, places, tile, steps, start_late, wait_early, wait_late, take_ref, *refs):
+    groups, gate_ref, refs = refs[: len(places)], refs[len(places)], refs[len(places) + 1 :]
     last = local == locals_ - 1
     before, refs = (refs[:local], refs[local:]) if last else ((), refs)
     own_at, got_at, down, slopes, back, *outs, rows, total, slots, own_ring, got_ring, ring, sems = refs
@@ -269,7 +269,9 @@
 
     @pl.when(step == 0)
     def _():
+        start_late()
         stream.start(steps)
+        wait_early()
         place_rows(small, axis_indices(), take_ref, local, groups, places, rows)
         total[...] = jnp.zeros_like(total)
 
@@ -286,13 +288,13 @@
 
     @pl.when(step == pl.num_programs(0) - 1)
     def _():
-        finish(small, last, take_ref, gate_ref[local], before, total, slots, outs)
-
-
-def last_body(small, local, locals_, n_after, tile, steps, take_ref, gate_ref, *refs):
-    refs = refs[n_after:]
+        wait_late()
+        finish(small, last, take_ref, gate_ref[local][:, :1], before, total, slots, outs)
+
+
+def last_body(small, local, locals_, tile, steps, start_late, wait_early, wait_late, gate_ref, *refs):
     last = local == locals_ - 1
-    before, refs = (refs[:local], refs[local:]) if last else ((), refs)
+    (take_ref, *before), refs = (refs[: local + 1], refs[local + 1 :]) if last else ((None,), refs)
     own_at, got_at, slopes_at, gate_w, up_w, *outs, total, slots, own_ring, got_ring, slope_ring, gate_ring, up_ring, sems = refs
     stream = Stream(
         [own_at, got_at, slopes_at, gate_w, up_w], [one_tile, one_tile, pair_tile, *[column_tile(local)] * 2], tile,
@@ -303,6 +305,7 @@
     @pl.when(step == 0)
     def _():
         stream.start(steps)
+        start_late()
         total[...] = jnp.zeros_like(total)
 
     own, got, slopes, gate_tile, up_tile = stream.take(step)
@@ -313,7 +316,8 @@
 
     @pl.when(step == pl.num_programs(0) - 1)
     def _():
-        finish(small, last, take_ref, gate_ref[local], before, total, slots, outs)
+        wait_late()
+        finish(small, last, take_ref, gate_ref[local][:, :1], before, total, slots, outs)
 
 
 def finish(small, last, take_ref, gate, before, total, slots, outs):
@@ -330,19 +334,44 @@
     return pl.BlockSpec(array.shape, lambda f: (0,) * dims)
 
 
-def call(body, steps, routes, after, near, near_specs, weights, outs, out_specs, scratch, flops):
-    anywhere = pl.BlockSpec(memory_space=pl.ANY)
+def call(body, steps, early, after, late, weights, outs, out_specs, scratch, flops):
+    near = [*early, *late]
+
+    def run(*refs):
+        sources, refs, held, near_sems = refs[: len(near)], refs[len(near) + len(after) : -len(near) - 1], refs[
+            -len(near) - 1 : -1], refs[-1]
+        copies = [pltpu.make_async_copy(sources[i], held[i], near_sems.at[i]) for i in range(len(near))]
+
+        @pl.when(pl.program_id(0) == 0)
+        def _():
+            for copy in copies[: len(early)]:
+                copy.start()
+
+        def start_late():
+            for copy in copies[len(early) :]:
+                copy.start()
+
+        def wait_early():
+            for copy in copies[: len(early)]:
+                copy.wait()
+
+        def wait_late():
+            for copy in copies[len(early) :]:
+                copy.wait()
+
+        body(start_late, wait_early, wait_late, *held, *refs)
+
     return pl.pallas_call(
-        body,
+        run,
         grid=(steps,),
-        in_specs=[*map(whole, routes), *[anywhere] * len(after), *near_specs,
-                  *[anywhere] * len(weights)],
+        in_specs=[pl.BlockSpec(memory_space=pl.ANY)] * (len(near) + len(after) + len(weights)),
         out_specs=out_specs,
         out_shape=outs,
-        scratch_shapes=scratch,
+        scratch_shapes=[*scratch, *[pltpu.VMEM(array.shape, array.dtype) for array in near],
+                        pltpu.SemaphoreType.DMA((len(near),))],
         compiler_params=pltpu.CompilerParams(vmem_limit_bytes=VMEM_BYTES),
         cost_estimate=pl.CostEstimate(flops=flops, bytes_accessed=1000, transcendentals=0),
-    )(*routes, *after, *near, *weights)
+    )(*near, *after, *weights)
 
 
 def in_hbm(*arrays):
@@ -360,7 +389,7 @@
     meta = jnp.concatenate([expert_ids.astype(F32).T, gate_values.T, jnp.zeros((4, count), F32)])
     meta = gather_meta(place, meta)
     routed = [jax.ShapeDtypeStruct((locals_, blocks, CAP, count), BF16),
-              jax.ShapeDtypeStruct((locals_, slots, 1), F32)]
+              jax.ShapeDtypeStruct((locals_, slots, 128), F32)]
 
     if small:
         token_groups, token_places, token_last, meta = gather_now(place, tokens, meta)
@@ -388,10 +417,10 @@
     own_pre, got_pre, after = [], [], []
     for local in range(locals_):
         ring = pltpu.VMEM((DEPTH, half, tile), BF16)
-        routes, new = ([take], []) if local else ([meta], routed)
+        route, new = (take, []) if local else (meta, routed)
         own, *new = call(
-            functools.partial(first_body, small, local, locals_, token_places, len(routes), len(after), tile, steps),
-            steps, routes, after, token_groups, [*map(whole, token_groups)], [w_gate, w_up],
+            functools.partial(first_body, small, local, locals_, token_places, tile, steps),
+            steps, [route, *token_groups], after, [], [w_gate, w_up],
             [pair, *new], [pair_spec, *map(whole, new)], [pltpu.VMEM((slots, half), BF16), ring, ring, sems(2)],
             COST * flops if local else FIRST_COST,
         )
@@ -408,7 +437,7 @@
         outs = ends(local, half)
         slope, back, *mixed_parts = call(
             functools.partial(middle_body, small, local, locals_, grad_places, tile, steps),
-            steps, [take, gate], [], [*grad_groups, *before], [*map(whole, [*grad_groups, *before])],
+            steps, [take, *grad_groups], [], [gate, *before],
             [*in_hbm(own_pre[local], got_pre[local]), w_down],
             [pair, one, *outs], [pair_spec, one_spec, *map(whole, outs)],
             [pltpu.VMEM((slots, half), BF16), pltpu.VMEM((slots, half), F32), pltpu.VMEM((slots, half), BF16),
@@ -421,15 +450,15 @@
         done.append(mixed_parts[0])
 
     ring = pltpu.VMEM((DEPTH, half, tile), BF16)
-    done, after = [], []
+    done = []
     mixed_terms = send_x(place, mixed_parts) if small else []
     for local in range(locals_):
         last = local == locals_ - 1
         before = done if last else []
         outs = ends(local, half // 2 if small and last else half)
         grad_parts = call(
-            functools.partial(last_body, small, local, locals_, len(after), tile, steps),
-            steps, [take, gate], after, before, [*map(whole, before)],
+            functools.partial(last_body, small, local, locals_, tile, steps),
+            steps, [], [], [gate, take, *before] if last else [gate],
             [*in_hbm(own_back[local], got_back[local], slopes[local]), w_gate, w_up],
             outs, [*map(whole, outs)],
             [pltpu.VMEM((slots, half), F32), pltpu.VMEM((slots, half), BF16), one_ring, one_ring, pair_ring, ring, ring,

time: 176 us -> 174 us (0.989)
  Pallas kernels: 86.3 us -> 83.9 us
    pallas_call x6, Pallas kernels: 86.3 us -> 83.9 us  [call(): pl.pallas_call(run, grid=(steps,), in_specs=[pl.BlockSpec(memory_space=pl...]
  transfers between devices with their start and end apart: 34 -> 34, of which waited for: 13 -> 13; matrix products, arithmetic and copies ran while one was open for 3% -> 3% of each run, Pallas kernels for 50% -> 49%
where the time goes in v5:
time: 174 us; the launch traced here: 172 us
  Pallas kernels  83.9 us (48%)
  starting transfers between devices  41 us (24%)
  waiting for transfers between devices  36.5 us (21%)
  other arithmetic  9.37 us (5%)
    pallas_call x6, Pallas kernels, call(): pl.pallas_call(run, grid=(steps,), in_specs=[pl.BlockSpec(memory_space=pl...  83.9 us
    ppermute x11, starting transfers between devices, across(): lax.ppermute(value, 'tensor', [(i, i ^ distance) for i in range(lax.axis_...  24.9 us
    ppermute x11, waiting for transfers between devices, across(): lax.ppermute(value, 'tensor', [(i, i ^ distance) for i in range(lax.axis_...  21.7 us
    ppermute x19, waiting for transfers between devices, swap(): return lax.ppermute(value, axis, [(0, 1), (1, 0)])  13.8 us
    ppermute x19, starting transfers between devices, swap(): return lax.ppermute(value, axis, [(0, 1), (1, 0)])  12.3 us
    ppermute x4, starting transfers between devices, far_both(): lax.ppermute(value, ('expert', 'sub'), [(i, 3 - i) for i in range(4)])  3.79 us
  transfers between devices with their start and end apart: 34, of which 13 were waited for; matrix products, arithmetic and copies ran while one was open for 3% of the time, Pallas kernels for 49%

profile of v5, /device:TPU:0, one launch (start us, length us, event | category | flops | bytes accessed | tf_op | source)
XLA Modules:
  0.0 171.7 jit_solution(10257518793994587831)
XLA Ops:
  2.6 4.6 %collective-permute-start = (bf16[128,768]{1,0:T(8,128)(2,1)}, bf16[128,768]{1,0:T(8,128)(2,1)S(1)}, u32[]{:S(2)}, u32[]{:S(2)}) collective-permute-start(bf16[128,768]{1,0:T(8,128)(2,1)} %param.7), channel_id=1, source_target_pairs={{0,12},{4,8},{8,4},{12,0},{1,13},{5,9},{9,5},{13,1},{2,14},{6,10},... | collective-permute-start | bytes 589832 | tf_op jit(solution)/shard_map/ppermute | solution.py:26
  7.9 1.6 collective-permute-start.2
  9.9 1.6 collective-permute-done.2
  11.5 1.7 %collective-permute-done = bf16[128,768]{1,0:T(8,128)(2,1)S(1)} collective-permute-done((bf16[128,768]{1,0:T(8,128)(2,1)}, bf16[128,768]{1,0:T(8,128)(2,1)S(1)}, u32[]{:S(2)}, u32[]{:S(2)}) %collective-permute-start) | collective-permute-done | bytes 196640 | tf_op jit(solution)/shard_map/ppermute | solution.py:26
  13.2 1.6 collective-permute-start.5
  14.8 3.5 %collective-permute-done.6 = bf16[128,768]{1,0:T(8,128)(2,1)S(1)} collective-permute-done((bf16[128,768]{1,0:T(8,128)(2,1)}, bf16[128,768]{1,0:T(8,128)(2,1)S(1)}, u32[]{:S(2)}, u32[]{:S(2)}) %collective-permute-start.6) | collective-permute-done | bytes 196640 | tf_op jit(solution)/shard_map/ppermute | solution.py:26
  18.3 1.5 collective-permute-start.8
  19.8 5.0 %collective-permute-done.3 = bf16[128,768]{1,0:T(8,128)(2,1)S(1)} collective-permute-done((bf16[128,768]{1,0:T(8,128)(2,1)}, bf16[128,768]{1,0:T(8,128)(2,1)S(1)}, u32[]{:S(2)}, u32[]{:S(2)}) %collective-permute-start.3) | collective-permute-done | bytes 196640 | tf_op jit(solution)/shard_map/ppermute | solution.py:26
  24.8 1.5 collective-permute-start.4
  26.3 5.0 %collective-permute-done.4 = bf16[128,768]{1,0:T(8,128)(2,1)S(1)} collective-permute-done((bf16[128,768]{1,0:T(8,128)(2,1)S(1)}, bf16[128,768]{1,0:T(8,128)(2,1)S(1)}, u32[]{:S(2)}, u32[]{:S(2)}) %collective-permute-start.4) | collective-permute-done | bytes 196640 | tf_op jit(solution)/shard_map/ppermute | solution.py:22
  33.1 2.5 %collective-permute-start.11 = (bf16[128,768]{1,0:T(8,128)(2,1)}, bf16[128,768]{1,0:T(8,128)(2,1)S(1)}, u32[]{:S(2)}, u32[]{:S(2)}) collective-permute-start(bf16[128,768]{1,0:T(8,128)(2,1)} %param.8), channel_id=1, source_target_pairs={{0,8},{4,12},{8,0},{12,4},{1,9},{5,13},{9,1},{13,5},{2,10},{6,14},... | collective-permute-start | bytes 589832 | tf_op jit(solution)/shard_map/ppermute | solution.py:26
  37.0 12.7 %shard_map.86 = (bf16[2,320,4096]{2,1,0:T(8,128)(2,1)}, bf16[2,4,80,128]{3,2,1,0:T(8,128)(2,1)S(1)}, f32[2,320,128]{2,1,0:T(8,128)S(1)}) custom-call(f32[4,8,128]{2,1,0:T(8,128)S(1)} %pad_maximum_fusion.5.refs_0_, bf16[4,128,768]{2,1,0:T(8,128)(2,1)S(1)} %get-tuple-element.77.refs_1_, bf16[4,128,768]{2,1,0:T(8,128)(2,1)S(1)} %collective-permute-done.9.refs_2_, ...), custom_call_target="tpu_custom_call" | custom-call | flops 1000 | bytes 1000 | tf_op jit(solution)/shard_map/pallas_call | solution.py:364
  51.4 1.6 collective-permute-start.15
  53.6 12.8 %shard_map.88.refs_7_ = bf16[2,320,4096]{2,1,0:T(8,128)(2,1)} custom-call(bf16[2,4,80,128]{3,2,1,0:T(8,128)(2,1)S(1)} %get-tuple-element.40.refs_0_.refs_1_, bf16[4,128,768]{2,1,0:T(8,128)(2,1)S(1)} %get-tuple-element.77.refs_1_, bf16[4,128,768]{2,1,0:T(8,128)(2,1)S(1)} %collective-permute-done.9.refs_2_, ...), custom_call_target="tpu_custom_call" | custom-call | flops 201326592000 | bytes 1000 | tf_op jit(solution)/shard_map/pallas_call | solution.py:364
  66.7 4.9 %collective-permute-done.14.refs_3_ = bf16[2,128,768]{2,1,0:T(8,128)(2,1)} collective-permute-done((bf16[2,128,768]{2,1,0:T(8,128)(2,1)}, bf16[2,128,768]{2,1,0:T(8,128)(2,1)}, u32[]{:S(2)}, u32[]{:S(2)}) %collective-permute-start.14) | collective-permute-done | bytes 393248 | tf_op jit(solution)/shard_map/ppermute | solution.py:22
  71.6 15.0 %shard_map.87 = (bf16[2,320,4096]{2,1,0:T(8,128)(2,1)}, bf16[320,4096]{1,0:T(8,128)(2,1)}, bf16[320,1536]{1,0:T(8,128)(2,1)S(1)}) custom-call(bf16[2,4,80,128]{3,2,1,0:T(8,128)(2,1)S(1)} %get-tuple-element.40.refs_0_.refs_1_, bf16[2,128,768]{2,1,0:T(8,128)(2,1)} %get-tuple-element.81.refs_1_.refs_3_, bf16[2,128,768]{2,1,0:T(8,128)(2,1)} %collective-permute-done.13.refs_2_, ...), custom_call_target="tpu_custom_call" | custom-call | flops 201326592000 | bytes 1000 | tf_op jit(solution)/shard_map/pallas_call | solution.py:364
  86.7 16.3 %shard_map.89 = (bf16[2,320,4096]{2,1,0:T(8,128)(2,1)}, bf16[320,4096]{1,0:T(8,128)(2,1)}, bf16[128,1536]{1,0:T(8,128)(2,1)S(1)}, bf16[128,1536]{1,0:T(8,128)(2,...) custom-call(bf16[2,4,80,128]{3,2,1,0:T(8,128)(2,1)S(1)} %get-tuple-element.40.refs_0_.refs_1_, ...), custom_call_target="tpu_custom_call" | custom-call | flops 201326592000 | bytes 1000 | tf_op jit(solution)/shard_map/pallas_call | solution.py:364
  103.6 1.5 collective-permute-start.19
  105.4 13.2 %shard_map.90.refs_2_ = bf16[320,1536]{1,0:T(8,128)(2,1)S(1)} custom-call(f32[2,320,128]{2,1,0:T(8,128)S(1)} %get-tuple-element.47.refs_5_.refs_0_, bf16[320,4096]{1,0:T(8,128)(2,1)} %get-tuple-element.53.refs_1_, bf16[320,4096]{1,0:T(8,128)(2,1)} %collective-permute-done.21.refs_2_, bf16[2,320,4096]{2,1,0:T(8,128)(2,1)} %get-tuple-element.54.refs_3_, ...), custom_call_target="tpu_custom_call" | custom-call | flops 201326592000 | bytes 1000 | tf_op jit(solution)/shard_map/pallas_call | solution.py:364
  118.7 13.9 %shard_map.91 = (bf16[128,768]{1,0:T(8,128)(2,1)S(1)}, bf16[128,768]{1,0:T(8,128)(2,1)S(1)}, bf16[128,768]{1,0:T(8,128)(2,1)S(1)}, bf16[128,768]{1,0:T(8,128)(2,...) custom-call(f32[2,320,128]{2,1,0:T(8,128)S(1)} %get-tuple-element.47, ...), custom_call_target="tpu_custom_call" | custom-call | flops 201326592000 | bytes 1000 | tf_op jit(solution)/shard_map/pallas_call | solution.py:364
  132.7 1.5 collective-permute-start.29
  134.9 1.5 fusion.3
  136.4 4.1 %collective-permute-start.23 = (bf16[2,128,768]{2,1,0:T(8,128)(2,1)S(1)}, bf16[2,128,768]{2,1,0:T(8,128)(2,1)S(1)}, u32[]{:S(2)}, u32[]{:S(2)}) collective-permute-start(bf16[2,128,768]{2,1,0:T(8,128)(2,1)S(1)} %pad_maximum_fusion.4), channel_id=1, source_target_pairs={{0,4},{4,0},{8,12},{12,8},{1,5},{5,1},{9,13},{13,9},{2,6},{6,2},{1... | collective-permute-start | bytes 1179656 | tf_op jit(solution)/shard_map/ppermute | solution.py:26
  140.5 1.5 collective-permute-start.25
  142.4 2.2 %collective-permute-done.30 = bf16[128,768]{1,0:T(8,128)(2,1)S(1)} collective-permute-done((bf16[128,768]{1,0:T(8,128)(2,1)S(1)}, bf16[128,768]{1,0:T(8,128)(2,1)S(1)}, u32[]{:S(2)}, u32[]{:S(2)}) %collective-permute-start.30) | collective-permute-done | bytes 196640 | tf_op jit(solution)/shard_map/ppermute | solution.py:22
  144.7 5.1 %collective-permute-start.31 = (bf16[128,768]{1,0:T(8,128)(2,1)S(1)}, bf16[128,768]{1,0:T(8,128)(2,1)S(1)}, u32[]{:S(2)}, u32[]{:S(2)}) collective-permute-start(bf16[128,768]{1,0:T(8,128)(2,1)S(1)} %select_convert_fusion.2), channel_id=1, source_target_pairs={{0,8},{4,12},{8,0},{12,4},{1,9},{5,13},{9,1},{13,5},{2,10},{6,14},... | collective-permute-start | bytes 589832 | tf_op jit(solution)/shard_map/ppermute | solution.py:26
  152.1 3.9 %collective-permute-start.27 = (bf16[128,768]{1,0:T(8,128)(2,1)S(1)}, bf16[128,768]{1,0:T(8,128)(2,1)S(1)}, u32[]{:S(2)}, u32[]{:S(2)}) collective-permute-start(bf16[128,768]{1,0:T(8,128)(2,1)S(1)} %fusion), channel_id=1, source_target_pairs={{0,12},{4,8},{8,4},{12,0},{1,13},{5,9},{9,5},{13,1},{2,14},{6,10},... | collective-permute-start | bytes 589832 | tf_op jit(solution)/shard_map/ppermute | solution.py:26
  156.2 2.1 %collective-permute-start.32 = (bf16[128,768]{1,0:T(8,128)(2,1)S(1)}, bf16[128,768]{1,0:T(8,128)(2,1)S(1)}, u32[]{:S(2)}, u32[]{:S(2)}) collective-permute-start(bf16[128,768]{1,0:T(8,128)(2,1)S(1)} %get-tuple-element.78), channel_id=1, source_target_pairs={{0,4},{4,0},{8,12},{12,8},{1,5},{5,1},{9,13},{13,9},{2,6},{6,2},{1... | collective-permute-start | bytes 589832 | tf_op jit(solution)/shard_map/ppermute | solution.py:26
  158.3 3.5 %collective-permute-done.27 = bf16[128,768]{1,0:T(8,128)(2,1)S(1)} collective-permute-done((bf16[128,768]{1,0:T(8,128)(2,1)S(1)}, bf16[128,768]{1,0:T(8,128)(2,1)S(1)}, u32[]{:S(2)}, u32[]{:S(2)}) %collective-permute-start.27) | collective-permute-done | bytes 196640 | tf_op jit(solution)/shard_map/ppermute | solution.py:26
  161.8 2.0 %fusion.2 = bf16[128,768]{1,0:T(8,128)(2,1)} fusion(bf16[128,768]{1,0:T(8,128)(2,1)S(1)} %collective-permute-done.27, bf16[2,128,768]{2,1,0:T(8,128)(2,1)S(1)} %collective-permute-done.23, pred[]{:T(512)S(6)} %eq.5, bf16[128,1536]{1,0:T(8,128)(2,1)} %collective-permute-done.19, bf16[128,1536]{1,0:T(8,128)(2,1)S(1)} %get-tuple-element.60, ...), kind=kLoop, calls=%fused_computation.11 | loop fusion | flops 1376256 | bytes 1376257 | tf_op jit(solution)/shard_map/convert_element_type | solution.py:129
  163.8 4.0 %collective-permute-done.31 = bf16[128,768]{1,0:T(8,128)(2,1)S(1)} collective-permute-done((bf16[128,768]{1,0:T(8,128)(2,1)S(1)}, bf16[128,768]{1,0:T(8,128)(2,1)S(1)}, u32[]{:S(2)}, u32[]{:S(2)}) %collective-permute-start.31) | collective-permute-done | bytes 196640 | tf_op jit(solution)/shard_map/ppermute | solution.py:26
  167.7 3.2 %collective-permute-done.32 = bf16[128,768]{1,0:T(8,128)(2,1)S(1)} collective-permute-done((bf16[128,768]{1,0:T(8,128)(2,1)S(1)}, bf16[128,768]{1,0:T(8,128)(2,1)S(1)}, u32[]{:S(2)}, u32[]{:S(2)}) %collective-permute-start.32) | collective-permute-done | bytes 196640 | tf_op jit(solution)/shard_map/ppermute | solution.py:26
  (59 shorter events, 14.3 us)
Async XLA Ops:
  2.1 5.7 %collective-permute-start.1 = (f32[8,128]{1,0:T(8,128)S(1)}, f32[8,128]{1,0:T(8,128)S(1)}, u32[]{:S(2)}, u32[]{:S(2)}) collective-permute-start(f32[8,128]{1,0:T(8,128)S(1)} %get-tuple-element.83), channel_id=1, source_target_pairs={{0,1},{1,0},{2,3},{3,2},{4,5},{5,4},{6,7},{7,6},{8,9},{9,8},{10,11... | collective-permute-start | bytes 12296 | tf_op jit(solution)/shard_map/ppermute | solution.py:22
  2.6 10.6 %collective-permute-start = (bf16[128,768]{1,0:T(8,128)(2,1)}, bf16[128,768]{1,0:T(8,128)(2,1)S(1)}, u32[]{:S(2)}, u32[]{:S(2)}) collective-permute-start(bf16[128,768]{1,0:T(8,128)(2,1)} %param.7), channel_id=1, source_target_pairs={{0,12},{4,8},{8,4},{12,0},{1,13},{5,9},{9,5},{13,1},{2,14},{6,10},... | collective-permute-start | bytes 589832 | tf_op jit(solution)/shard_map/ppermute | solution.py:26
  7.2 11.1 %collective-permute-start.6 = (bf16[128,768]{1,0:T(8,128)(2,1)}, bf16[128,768]{1,0:T(8,128)(2,1)S(1)}, u32[]{:S(2)}, u32[]{:S(2)}) collective-permute-start(bf16[128,768]{1,0:T(8,128)(2,1)} %param.7), channel_id=1, source_target_pairs={{0,4},{4,0},{8,12},{12,8},{1,5},{5,1},{9,13},{13,9},{2,6},{6,2},{1... | collective-permute-start | bytes 589832 | tf_op jit(solution)/shard_map/ppermute | solution.py:26
  7.2 17.6 %collective-permute-start.3 = (bf16[128,768]{1,0:T(8,128)(2,1)}, bf16[128,768]{1,0:T(8,128)(2,1)S(1)}, u32[]{:S(2)}, u32[]{:S(2)}) collective-permute-start(bf16[128,768]{1,0:T(8,128)(2,1)} %param.7), channel_id=1, source_target_pairs={{0,8},{4,12},{8,0},{12,4},{1,9},{5,13},{9,1},{13,5},{2,10},{6,14},... | collective-permute-start | bytes 589832 | tf_op jit(solution)/shard_map/ppermute | solution.py:26
  9.5 16.8 %collective-permute-start.7 = (bf16[128,768]{1,0:T(8,128)(2,1)}, bf16[128,768]{1,0:T(8,128)(2,1)S(1)}, u32[]{:S(2)}, u32[]{:S(2)}) collective-permute-start(bf16[128,768]{1,0:T(8,128)(2,1)} %param.7), channel_id=1, source_target_pairs={{0,2},{2,0},{1,3},{3,1},{4,6},{6,4},{5,7},{7,5},{8,10},{10,8},{9,1... | collective-permute-start | bytes 589832 | tf_op jit(solution)/shard_map/ppermute | solution.py:22
  13.2 13.0 %collective-permute-start.5 = (bf16[128,768]{1,0:T(8,128)(2,1)S(1)}, bf16[128,768]{1,0:T(8,128)(2,1)S(1)}, u32[]{:S(2)}, u32[]{:S(2)}) collective-permute-start(bf16[128,768]{1,0:T(8,128)(2,1)S(1)} %collective-permute-done), channel_id=1, source_target_pairs={{0,2},{2,0},{1,3},{3,1},{4,6},{6,4},{5,7},{7,5},{8,10},{10,8},{9,1... | collective-permute-start | bytes 589832 | tf_op jit(solution)/shard_map/ppermute | solution.py:22
  18.3 8.0 %collective-permute-start.8 = (bf16[128,768]{1,0:T(8,128)(2,1)S(1)}, bf16[128,768]{1,0:T(8,128)(2,1)S(1)}, u32[]{:S(2)}, u32[]{:S(2)}) collective-permute-start(bf16[128,768]{1,0:T(8,128)(2,1)S(1)} %collective-permute-done.6), channel_id=1, source_target_pairs={{0,2},{2,0},{1,3},{3,1},{4,6},{6,4},{5,7},{7,5},{8,10},{10,8},{9,1... | collective-permute-start | bytes 589832 | tf_op jit(solution)/shard_map/ppermute | solution.py:22
  24.8 6.5 %collective-permute-start.4 = (bf16[128,768]{1,0:T(8,128)(2,1)S(1)}, bf16[128,768]{1,0:T(8,128)(2,1)S(1)}, u32[]{:S(2)}, u32[]{:S(2)}) collective-permute-start(bf16[128,768]{1,0:T(8,128)(2,1)S(1)} %collective-permute-done.3), channel_id=1, source_target_pairs={{0,2},{2,0},{1,3},{3,1},{4,6},{6,4},{5,7},{7,5},{8,10},{10,8},{9,1... | collective-permute-start | bytes 589832 | tf_op jit(solution)/shard_map/ppermute | solution.py:22
  32.5 17.2 %collective-permute-start.10 = (bf16[128,768]{1,0:T(8,128)(2,1)}, bf16[128,768]{1,0:T(8,128)(2,1)S(1)}, u32[]{:S(2)}, u32[]{:S(2)}) collective-permute-start(bf16[128,768]{1,0:T(8,128)(2,1)} %param.8), channel_id=1, source_target_pairs={{0,4},{4,0},{8,12},{12,8},{1,5},{5,1},{9,13},{13,9},{2,6},{6,2},{1... | collective-permute-start | bytes 589832 | tf_op jit(solution)/shard_map/ppermute | solution.py:26
  33.1 17.3 %collective-permute-start.11 = (bf16[128,768]{1,0:T(8,128)(2,1)}, bf16[128,768]{1,0:T(8,128)(2,1)S(1)}, u32[]{:S(2)}, u32[]{:S(2)}) collective-permute-start(bf16[128,768]{1,0:T(8,128)(2,1)} %param.8), channel_id=1, source_target_pairs={{0,8},{4,12},{8,0},{12,4},{1,9},{5,13},{9,1},{13,5},{2,10},{6,14},... | collective-permute-start | bytes 589832 | tf_op jit(solution)/shard_map/ppermute | solution.py:26
  35.7 14.8 %collective-permute-start.12 = (bf16[128,768]{1,0:T(8,128)(2,1)}, bf16[128,768]{1,0:T(8,128)(2,1)S(1)}, u32[]{:S(2)}, u32[]{:S(2)}) collective-permute-start(bf16[128,768]{1,0:T(8,128)(2,1)} %param.8), channel_id=1, source_target_pairs={{0,12},{4,8},{8,4},{12,0},{1,13},{5,9},{9,5},{13,1},{2,14},{6,10},... | collective-permute-start | bytes 589832 | tf_op jit(solution)/shard_map/ppermute | solution.py:26
  51.4 15.2 %collective-permute-start.13 = (bf16[2,128,768]{2,1,0:T(8,128)(2,1)}, bf16[2,128,768]{2,1,0:T(8,128)(2,1)}, u32[]{:S(2)}, u32[]{:S(2)}) collective-permute-start(bf16[2,128,768]{2,1,0:T(8,128)(2,1)} %get-tuple-element.80.refs_4_), channel_id=1, source_target_pairs={{0,1},{1,0},{2,3},{3,2},{4,5},{5,4},{6,7},{7,6},{8,9},{9,8},{10,11... | collective-permute-start | bytes 1179656 | tf_op jit(solution)/shard_map/ppermute | solution.py:22
  51.4 20.2 %collective-permute-start.15 = (bf16[2,128,768]{2,1,0:T(8,128)(2,1)}, bf16[2,128,768]{2,1,0:T(8,128)(2,1)}, u32[]{:S(2)}, u32[]{:S(2)}) collective-permute-start(bf16[2,128,768]{2,1,0:T(8,128)(2,1)} %get-tuple-element.80.refs_4_), channel_id=1, source_target_pairs={{0,3},{1,2},{2,1},{3,0},{4,7},{5,6},{6,5},{7,4},{8,11},{9,10},{10,... | collective-permute-start | bytes 1179656 | tf_op jit(solution)/shard_map/ppermute | solution.py:61
  53.0 18.6 %collective-permute-start.16 = (bf16[2,320,4096]{2,1,0:T(8,128)(2,1)}, bf16[2,320,4096]{2,1,0:T(8,128)(2,1)}, u32[]{:S(2)}, u32[]{:S(2)}) collective-permute-start(bf16[2,320,4096]{2,1,0:T(8,128)(2,1)} %get-tuple-element.42.refs_6_), channel_id=1, source_target_pairs={{0,1},{1,0},{2,3},{3,2},{4,5},{5,4},{6,7},{7,6},{8,9},{9,8},{10,11... | collective-permute-start | bytes 15728648 | tf_op jit(solution)/shard_map/ppermute | solution.py:22
  53.0 18.6 %collective-permute-start.14 = (bf16[2,128,768]{2,1,0:T(8,128)(2,1)}, bf16[2,128,768]{2,1,0:T(8,128)(2,1)}, u32[]{:S(2)}, u32[]{:S(2)}) collective-permute-start(bf16[2,128,768]{2,1,0:T(8,128)(2,1)} %get-tuple-element.81.refs_1_.refs_3_), channel_id=1, source_target_pairs={{0,2},{2,0},{1,3},{3,1},{4,6},{6,4},{5,7},{7,5},{8,10},{10,8},{9,1... | collective-permute-start | bytes 1179656 | tf_op jit(solution)/shard_map/ppermute | solution.py:22
  66.4 20.4 %collective-permute-start.17 = (bf16[2,320,4096]{2,1,0:T(8,128)(2,1)}, bf16[2,320,4096]{2,1,0:T(8,128)(2,1)}, u32[]{:S(2)}, u32[]{:S(2)}) collective-permute-start(bf16[2,320,4096]{2,1,0:T(8,128)(2,1)} %shard_map.88.refs_7_), channel_id=1, source_target_pairs={{0,1},{1,0},{2,3},{3,2},{4,5},{5,4},{6,7},{7,6},{8,9},{9,8},{10,11... | collective-permute-start | bytes 15728648 | tf_op jit(solution)/shard_map/ppermute | solution.py:22
  86.6 18.8 %collective-permute-start.21 = (bf16[320,4096]{1,0:T(8,128)(2,1)}, bf16[320,4096]{1,0:T(8,128)(2,1)}, u32[]{:S(2)}, u32[]{:S(2)}) collective-permute-start(bf16[320,4096]{1,0:T(8,128)(2,1)} %get-tuple-element.53.refs_1_), channel_id=1, source_target_pairs={{0,1},{1,0},{2,3},{3,2},{4,5},{5,4},{6,7},{7,6},{8,9},{9,8},{10,11... | collective-permute-start | bytes 7864328 | tf_op jit(solution)/shard_map/ppermute | solution.py:22
  103.0 15.7 %collective-permute-start.22 = (bf16[320,4096]{1,0:T(8,128)(2,1)}, bf16[320,4096]{1,0:T(8,128)(2,1)}, u32[]{:S(2)}, u32[]{:S(2)}) collective-permute-start(bf16[320,4096]{1,0:T(8,128)(2,1)} %get-tuple-element.55.refs_3_), channel_id=1, source_target_pairs={{0,1},{1,0},{2,3},{3,2},{4,5},{5,4},{6,7},{7,6},{8,9},{9,8},{10,11... | collective-permute-start | bytes 7864328 | tf_op jit(solution)/shard_map/ppermute | solution.py:22
  103.5 29.1 %collective-permute-start.18 = (bf16[128,1536]{1,0:T(8,128)(2,1)}, bf16[128,1536]{1,0:T(8,128)(2,1)}, u32[]{:S(2)}, u32[]{:S(2)}) collective-permute-start(bf16[128,1536]{1,0:T(8,128)(2,1)} %get-tuple-element.50), channel_id=1, source_target_pairs={{0,1},{1,0},{2,3},{3,2},{4,5},{5,4},{6,7},{7,6},{8,9},{9,8},{10,11... | collective-permute-start | bytes 1179656 | tf_op jit(solution)/shard_map/ppermute | solution.py:22
  103.6 29.0 %collective-permute-start.19 = (bf16[128,1536]{1,0:T(8,128)(2,1)}, bf16[128,1536]{1,0:T(8,128)(2,1)}, u32[]{:S(2)}, u32[]{:S(2)}) collective-permute-start(bf16[128,1536]{1,0:T(8,128)(2,1)} %get-tuple-element.51), channel_id=1, source_target_pairs={{0,2},{2,0},{1,3},{3,1},{4,6},{6,4},{5,7},{7,5},{8,10},{10,8},{9,1... | collective-permute-start | bytes 1179656 | tf_op jit(solution)/shard_map/ppermute | solution.py:22
  105.1 27.5 %collective-permute-start.20 = (bf16[128,1536]{1,0:T(8,128)(2,1)}, bf16[128,1536]{1,0:T(8,128)(2,1)}, u32[]{:S(2)}, u32[]{:S(2)}) collective-permute-start(bf16[128,1536]{1,0:T(8,128)(2,1)} %get-tuple-element.52), channel_id=1, source_target_pairs={{0,3},{1,2},{2,1},{3,0},{4,7},{5,6},{6,5},{7,4},{8,11},{9,10},{10,... | collective-permute-start | bytes 1179656 | tf_op jit(solution)/shard_map/ppermute | solution.py:61
  132.7 7.9 %collective-permute-start.29 = (bf16[128,768]{1,0:T(8,128)(2,1)S(1)}, bf16[128,768]{1,0:T(8,128)(2,1)S(1)}, u32[]{:S(2)}, u32[]{:S(2)}) collective-permute-start(bf16[128,768]{1,0:T(8,128)(2,1)S(1)} %get-tuple-element.68), channel_id=1, source_target_pairs={{0,3},{1,2},{2,1},{3,0},{4,7},{5,6},{6,5},{7,4},{8,11},{9,10},{10,... | collective-permute-start | bytes 589832 | tf_op jit(solution)/shard_map/ppermute | solution.py:61
  134.2 7.8 %collective-permute-start.28 = (bf16[128,768]{1,0:T(8,128)(2,1)S(1)}, bf16[128,768]{1,0:T(8,128)(2,1)S(1)}, u32[]{:S(2)}, u32[]{:S(2)}) collective-permute-start(bf16[128,768]{1,0:T(8,128)(2,1)S(1)} %get-tuple-element.67), channel_id=1, source_target_pairs={{0,1},{1,0},{2,3},{3,2},{4,5},{5,4},{6,7},{7,6},{8,9},{9,8},{10,11... | collective-permute-start | bytes 589832 | tf_op jit(solution)/shard_map/ppermute | solution.py:22
  134.3 10.3 %collective-permute-start.30 = (bf16[128,768]{1,0:T(8,128)(2,1)S(1)}, bf16[128,768]{1,0:T(8,128)(2,1)S(1)}, u32[]{:S(2)}, u32[]{:S(2)}) collective-permute-start(bf16[128,768]{1,0:T(8,128)(2,1)S(1)} %get-tuple-element.69), channel_id=1, source_target_pairs={{0,2},{2,0},{1,3},{3,1},{4,6},{6,4},{5,7},{7,5},{8,10},{10,8},{9,1... | collective-permute-start | bytes 589832 | tf_op jit(solution)/shard_map/ppermute | solution.py:22
  136.4 13.4 %collective-permute-start.23 = (bf16[2,128,768]{2,1,0:T(8,128)(2,1)S(1)}, bf16[2,128,768]{2,1,0:T(8,128)(2,1)S(1)}, u32[]{:S(2)}, u32[]{:S(2)}) collective-permute-start(bf16[2,128,768]{2,1,0:T(8,128)(2,1)S(1)} %pad_maximum_fusion.4), channel_id=1, source_target_pairs={{0,4},{4,0},{8,12},{12,8},{1,5},{5,1},{9,13},{13,9},{2,6},{6,2},{1... | collective-permute-start | bytes 1179656 | tf_op jit(solution)/shard_map/ppermute | solution.py:26
  140.5 10.6 %collective-permute-start.24 = (bf16[128,768]{1,0:T(8,128)(2,1)S(1)}, bf16[128,768]{1,0:T(8,128)(2,1)S(1)}, u32[]{:S(2)}, u32[]{:S(2)}) collective-permute-start(bf16[128,768]{1,0:T(8,128)(2,1)S(1)} %get-tuple-element.63), channel_id=1, source_target_pairs={{0,1},{1,0},{2,3},{3,2},{4,5},{5,4},{6,7},{7,6},{8,9},{9,8},{10,11... | collective-permute-start | bytes 589832 | tf_op jit(solution)/shard_map/ppermute | solution.py:22
  140.5 10.6 %collective-permute-start.25 = (bf16[128,768]{1,0:T(8,128)(2,1)S(1)}, bf16[128,768]{1,0:T(8,128)(2,1)S(1)}, u32[]{:S(2)}, u32[]{:S(2)}) collective-permute-start(bf16[128,768]{1,0:T(8,128)(2,1)S(1)} %get-tuple-element.64), channel_id=1, source_target_pairs={{0,2},{2,0},{1,3},{3,1},{4,6},{6,4},{5,7},{7,5},{8,10},{10,8},{9,1... | collective-permute-start | bytes 589832 | tf_op jit(solution)/shard_map/ppermute | solution.py:22
  142.0 10.1 %collective-permute-start.26 = (bf16[128,768]{1,0:T(8,128)(2,1)S(1)}, bf16[128,768]{1,0:T(8,128)(2,1)S(1)}, u32[]{:S(2)}, u32[]{:S(2)}) collective-permute-start(bf16[128,768]{1,0:T(8,128)(2,1)S(1)} %get-tuple-element.65), channel_id=1, source_target_pairs={{0,3},{1,2},{2,1},{3,0},{4,7},{5,6},{6,5},{7,4},{8,11},{9,10},{10,... | collective-permute-start | bytes 589832 | tf_op jit(solution)/shard_map/ppermute | solution.py:61
  144.7 23.0 %collective-permute-start.31 = (bf16[128,768]{1,0:T(8,128)(2,1)S(1)}, bf16[128,768]{1,0:T(8,128)(2,1)S(1)}, u32[]{:S(2)}, u32[]{:S(2)}) collective-permute-start(bf16[128,768]{1,0:T(8,128)(2,1)S(1)} %select_convert_fusion.2), channel_id=1, source_target_pairs={{0,8},{4,12},{8,0},{12,4},{1,9},{5,13},{9,1},{13,5},{2,10},{6,14},... | collective-permute-start | bytes 589832 | tf_op jit(solution)/shard_map/ppermute | solution.py:26
  152.1 9.7 %collective-permute-start.27 = (bf16[128,768]{1,0:T(8,128)(2,1)S(1)}, bf16[128,768]{1,0:T(8,128)(2,1)S(1)}, u32[]{:S(2)}, u32[]{:S(2)}) collective-permute-start(bf16[128,768]{1,0:T(8,128)(2,1)S(1)} %fusion), channel_id=1, source_target_pairs={{0,12},{4,8},{8,4},{12,0},{1,13},{5,9},{9,5},{13,1},{2,14},{6,10},... | collective-permute-start | bytes 589832 | tf_op jit(solution)/shard_map/ppermute | solution.py:26
  156.1 11.6 %collective-permute-start.33 = (bf16[128,768]{1,0:T(8,128)(2,1)S(1)}, bf16[128,768]{1,0:T(8,128)(2,1)S(1)}, u32[]{:S(2)}, u32[]{:S(2)}) collective-permute-start(bf16[128,768]{1,0:T(8,128)(2,1)S(1)} %get-tuple-element.79), channel_id=1, source_target_pairs={{0,12},{4,8},{8,4},{12,0},{1,13},{5,9},{9,5},{13,1},{2,14},{6,10},... | collective-permute-start | bytes 589832 | tf_op jit(solution)/shard_map/ppermute | solution.py:26
  156.2 14.7 %collective-permute-start.32 = (bf16[128,768]{1,0:T(8,128)(2,1)S(1)}, bf16[128,768]{1,0:T(8,128)(2,1)S(1)}, u32[]{:S(2)}, u32[]{:S(2)}) collective-permute-start(bf16[128,768]{1,0:T(8,128)(2,1)S(1)} %get-tuple-element.78), channel_id=1, source_target_pairs={{0,4},{4,0},{8,12},{12,8},{1,5},{5,1},{9,13},{13,9},{2,6},{6,2},{1... | collective-permute-start | bytes 589832 | tf_op jit(solution)/shard_map/ppermute | solution.py:26
  (3 other events, 21.7 us)
